TPU v7x, 128 devices: a whole 4x4x4 slice. The times are simulated.
128 devices in a mesh: mem: 8 (over x, core), cell: 16 (over y, z).
Axes of the slice: x: 4, y: 4, z: 4, core: 2. Of those that a mesh axis runs over, the one named last changes fastest.
Arguments:
- prior_samples: float32 [512, 256, 512], P('mem', 'cell'), may hold values from -6 to 6
- neighbour_weights: float32 [4, 256, 512], P(None, 'cell'), may hold values from 0.02 to 0.22
- obs_cell: int32 [4, 128], replicated, may hold values from 0 to 131071
- obs_value: float32 [4, 128], replicated, may hold values from -8 to 8
- obs_var: float32 [4, 128], replicated, may hold values from 0.1 to 1
- block_order: int32 [4], replicated, may hold values from 0 to 3, each once
Outputs:
- analysis: float32 [512, 256, 512], P('mem', 'cell')
Inputs may be any that keep to these rules, and one draw needn't show every extreme that they name: `block_order`: each block number appears once.
All inputs are finite; a program needn't handle non-finite values.
Results may differ from a plain program's by a relative error of at most 0.00014.
Values sent between devices are 32-bit elements; how exact they have to be, the bound alone decides.
No kernel may reach another device: no remote copies, remote signals or barrier semaphores. Data moves between devices by JAX's collectives and lax.ppermute only.
A program may use at most 128 MiB of HBM per device.

v0:
```python
import jax
import jax.numpy as jnp
from jax import lax
from jax.sharding import PartitionSpec as P

SAMPLE_TOTAL = 512


def extended(block, sides, width):
    for axis, dim in sides:
        count = lax.axis_size(axis)
        forward = [(i, i + 1) for i in range(count - 1)]
        backward = [(target, source) for source, target in forward]
        low = lax.ppermute(
            lax.slice_in_dim(block, block.shape[dim] - width, None, axis=dim), axis, forward
        )
        high = lax.ppermute(lax.slice_in_dim(block, 0, width, axis=dim), axis, backward)
        block = jnp.concatenate([low, block, high], axis=dim)
    return block


def tri_solve(update_matrix, right, transposed):
    return lax.linalg.triangular_solve(
        update_matrix, right, left_side=True, lower=True, transpose_a=transposed
    )


def body(prior_samples, neighbour_weights, obs_cell, obs_value, obs_var, block_order):
    highest = lax.Precision.HIGHEST
    members_dev, tile_rows, width = prior_samples.shape
    cells = tile_rows * width
    haloed = extended(prior_samples, (("cell", 1),), 1)
    padded = jnp.pad(haloed, ((0, 0), (0, 0), (1, 1)))
    to_east = padded[:, 1:-1, 2:]
    to_west = padded[:, 1:-1, :-2]
    to_north = padded[:, :-2, 1:-1]
    to_south = padded[:, 2:, 1:-1]
    fore = (
        prior_samples
        + neighbour_weights[0] * (to_east - prior_samples)
        + neighbour_weights[1] * (to_west - prior_samples)
        + neighbour_weights[2] * (to_north - prior_samples)
        + neighbour_weights[3] * (to_south - prior_samples)
    )
    raveled_field = fore.reshape(members_dev, cells)
    ens_mean = lax.psum(jnp.sum(raveled_field, axis=0), "mem") / SAMPLE_TOTAL
    anomaly = raveled_field - ens_mean
    positions = lax.axis_index("cell") * cells + lax.iota(jnp.int32, cells)
    member_offset = lax.axis_index("mem") * members_dev
    first_member = (lax.axis_index("mem") == 0).astype(jnp.float32)
    placing = (
        lax.iota(jnp.int32, SAMPLE_TOTAL)[:, None]
        == member_offset + lax.iota(jnp.int32, members_dev)[None, :]
    ).astype(jnp.float32)

    def one_block(carry, block):
        ens_mean, anomaly = carry
        observed = obs_cell[block]
        noise_var = obs_var[block]
        selector = (positions[:, None] == observed[None, :]).astype(jnp.float32)
        local_cols = jnp.dot(anomaly, selector, precision=highest)
        mean_cols = jnp.dot(ens_mean, selector, precision=highest)
        placed = jnp.dot(placing, local_cols, precision=highest)
        all_cols, prior_mean = lax.psum((placed, mean_cols * first_member), ("mem", "cell"))
        prior_rows = lax.dynamic_slice_in_dim(all_cols, member_offset, members_dev, 0)
        spread = jnp.dot(all_cols.T, all_cols, precision=highest)
        spread = spread / (SAMPLE_TOTAL - 1) + jnp.diag(noise_var)
        innov = obs_value[block] - prior_mean
        factor_low = jnp.linalg.cholesky(spread)
        factor_sum = factor_low + jnp.diag(jnp.sqrt(noise_var))
        halfway = tri_solve(factor_low, innov[:, None], False)
        weights = tri_solve(factor_low, halfway, True)[:, 0]
        partial_cross = jnp.dot(prior_rows.T, anomaly, precision=highest)
        cross = lax.psum(partial_cross, "mem")
        scaled = tri_solve(factor_low, cross, False) / (SAMPLE_TOTAL - 1)
        mean_step = jnp.dot(weights, cross, precision=highest) / (SAMPLE_TOTAL - 1)
        ens_mean = ens_mean + mean_step
        mapped = tri_solve(factor_sum, prior_rows.T, False)
        anomaly = anomaly - jnp.dot(mapped.T, scaled, precision=highest)
        return ((ens_mean, anomaly), None)

    (ens_mean, anomaly), unused = lax.scan(one_block, (ens_mean, anomaly), block_order)
    return (ens_mean + anomaly).reshape(prior_samples.shape)


def solution(mesh):
    return jax.shard_map(
        body,
        mesh=mesh,
        in_specs=(P("mem", "cell", None), P(None, "cell", None), P(), P(), P(), P()),
        out_specs=P("mem", "cell", None),
        check_vma=False,
    )
```

profile of v0, /device:TPU:1, one launch (start us, length us, event | category | flops | bytes accessed | tf_op | source)
XLA Modules:
  0.0 1132.4 jit_solution(2534955312005271085)
XLA Ops:
  23.8 22.6 %psum.34 = f32[8192]{0:T(1024)S(1)} all-reduce(f32[8192]{0:T(1024)S(1)} %bitcast.138), channel_id=1, replica_groups=mesh['mem'=8,'cell'=16] {'mem'}, use_global_device_ids=true, to_apply=%region_1.2 | all-reduce | flops 8192 | bytes 65536 | tf_op jit(solution)/shard_map/psum | solution.py:46
  49.8 1073.1 %while.15 = (s32[]{:T(128)}, f32[8192]{0:T(1024)S(1)}, f32[64,8192]{1,0:T(8,128)S(1)}, s32[4]{0:T(128)S(1)}, s32[4,128]{1,0:T(4,128)}, /*index=5*/f32[4,128]{1,0...) while((s32[]{:T(128)}, f32[8192]{0:T(1024)S(1)}, ...), condition=%wide.region_8.9_spmd.clone, body=%wide.region_2.8_spmd.clone.sunk | while | flops 4221919744 | bytes 75902040 | solution.py:82
  58.2 147.1 %all-reduce.4.cloned.1.call-done = f32[512,128]{0,1:T(8,128)} async-done(((f32[512,128]{0,1:T(8,128)}), f32[512,128]{0,1:T(8,128)}) %all-reduce.4.cloned.1.call-update) | async-done | bytes 262160 | tf_op jit(solution)/shard_map/while/body/eval_jaxpr/psum | solution.py:64
  212.9 64.5 %psum.42 = f32[128]{0:T(128)S(1)} all-reduce(f32[128]{0:T(128)S(1)} %fusion.120), channel_id=1, replica_groups=mesh['mem'=8,'cell'=16] {'mem','cell'}, use_global_device_ids=true, to_apply=%region_6.6 | all-reduce | flops 128 | bytes 1024 | tf_op jit(solution)/shard_map/while/body/eval_jaxpr/psum | solution.py:64
  278.6 11.7 %cholesky.77 = f32[128,128]{1,0:T(8,128)S(1)} custom-call(f32[128,128]{1,0:T(8,128)S(1)} %fusion.119), custom_call_target="Cholesky" | custom-call | tf_op jit(solution)/shard_map/while/body/eval_jaxpr/jit(cholesky)/cholesky | solution.py:69
  291.7 9.8 custom-call.23
  301.6 9.8 custom-call.24
  333.1 138.3 %all-reduce.4.cloned.1.call-done = f32[512,128]{0,1:T(8,128)} async-done(((f32[512,128]{0,1:T(8,128)}), f32[512,128]{0,1:T(8,128)}) %all-reduce.4.cloned.1.call-update) | async-done | bytes 262160 | tf_op jit(solution)/shard_map/while/body/eval_jaxpr/psum | solution.py:64
  471.4 5.8 fusion.121
  479.0 64.4 %psum.42 = f32[128]{0:T(128)S(1)} all-reduce(f32[128]{0:T(128)S(1)} %fusion.120), channel_id=1, replica_groups=mesh['mem'=8,'cell'=16] {'mem','cell'}, use_global_device_ids=true, to_apply=%region_6.6 | all-reduce | flops 128 | bytes 1024 | tf_op jit(solution)/shard_map/while/body/eval_jaxpr/psum | solution.py:64
  544.7 11.7 %cholesky.77 = f32[128,128]{1,0:T(8,128)S(1)} custom-call(f32[128,128]{1,0:T(8,128)S(1)} %fusion.119), custom_call_target="Cholesky" | custom-call | tf_op jit(solution)/shard_map/while/body/eval_jaxpr/jit(cholesky)/cholesky | solution.py:69
  557.8 9.8 custom-call.23
  567.6 9.8 custom-call.24
  599.2 138.2 %all-reduce.4.cloned.1.call-done = f32[512,128]{0,1:T(8,128)} async-done(((f32[512,128]{0,1:T(8,128)}), f32[512,128]{0,1:T(8,128)}) %all-reduce.4.cloned.1.call-update) | async-done | bytes 262160 | tf_op jit(solution)/shard_map/while/body/eval_jaxpr/psum | solution.py:64
  737.4 5.8 fusion.121
  745.1 64.4 %psum.42 = f32[128]{0:T(128)S(1)} all-reduce(f32[128]{0:T(128)S(1)} %fusion.120), channel_id=1, replica_groups=mesh['mem'=8,'cell'=16] {'mem','cell'}, use_global_device_ids=true, to_apply=%region_6.6 | all-reduce | flops 128 | bytes 1024 | tf_op jit(solution)/shard_map/while/body/eval_jaxpr/psum | solution.py:64
  810.7 11.7 %cholesky.77 = f32[128,128]{1,0:T(8,128)S(1)} custom-call(f32[128,128]{1,0:T(8,128)S(1)} %fusion.119), custom_call_target="Cholesky" | custom-call | tf_op jit(solution)/shard_map/while/body/eval_jaxpr/jit(cholesky)/cholesky | solution.py:69
  823.9 9.8 custom-call.23
  833.7 9.8 custom-call.24
  865.2 138.3 %all-reduce.4.cloned.1.call-done = f32[512,128]{0,1:T(8,128)} async-done(((f32[512,128]{0,1:T(8,128)}), f32[512,128]{0,1:T(8,128)}) %all-reduce.4.cloned.1.call-update) | async-done | bytes 262160 | tf_op jit(solution)/shard_map/while/body/eval_jaxpr/psum | solution.py:64
  1011.2 64.4 %psum.42 = f32[128]{0:T(128)S(1)} all-reduce(f32[128]{0:T(128)S(1)} %fusion.120), channel_id=1, replica_groups=mesh['mem'=8,'cell'=16] {'mem','cell'}, use_global_device_ids=true, to_apply=%region_6.6 | all-reduce | flops 128 | bytes 1024 | tf_op jit(solution)/shard_map/while/body/eval_jaxpr/psum | solution.py:64
  1076.8 11.7 %cholesky.77 = f32[128,128]{1,0:T(8,128)S(1)} custom-call(f32[128,128]{1,0:T(8,128)S(1)} %fusion.119), custom_call_target="Cholesky" | custom-call | tf_op jit(solution)/shard_map/while/body/eval_jaxpr/jit(cholesky)/cholesky | solution.py:69
  1090.0 9.8 custom-call.23
  1099.8 9.8 custom-call.24
  (141 shorter events, 131.6 us)
Async XLA Ops:
  8.3 7.6 collective-permute-start.1
  9.7 7.1 collective-permute-start
  16.9 3.9 copy-start.2
  49.1 0.7 copy-start.3
  49.8 155.4 %all-reduce.4.cloned.1.call-start = ((), (), s32[]{:S(2)}) async-start(), calls=%async_computation | async-start | bytes 524288 | tf_op jit(solution)/shard_map/while/body/eval_jaxpr/psum | solution.py:64
  58.1 254.7 %all-reduce.6.cloned.1.call-start = ((), (), s32[]{:S(2)}) async-start(), calls=%async_computation.1 | async-start | bytes 8388608 | tf_op jit(solution)/shard_map/while/body/eval_jaxpr/psum | solution.py:74
  211.0 67.0 %copy-start.1 = (f32[512,128]{0,1:T(8,128)S(1)}, f32[512,128]{0,1:T(8,128)}, u32[]{:S(2)}) copy-start(f32[512,128]{0,1:T(8,128)} %all-reduce.4.cloned.1.call-done) | copy-start | bytes 786436 | tf_op jit(solution)/shard_map/while
  312.8 4.4 copy-start
  324.7 146.7 %all-reduce.4.cloned.1.call-start = ((), (), s32[]{:S(2)}) async-start(), calls=%async_computation | async-start | bytes 524288 | tf_op jit(solution)/shard_map/while/body/eval_jaxpr/psum | solution.py:64
  333.1 245.8 %all-reduce.6.cloned.1.call-start = ((), (), s32[]{:S(2)}) async-start(), calls=%async_computation.1 | async-start | bytes 8388608 | tf_op jit(solution)/shard_map/while/body/eval_jaxpr/psum | solution.py:74
  477.2 66.9 %copy-start.1 = (f32[512,128]{0,1:T(8,128)S(1)}, f32[512,128]{0,1:T(8,128)}, u32[]{:S(2)}) copy-start(f32[512,128]{0,1:T(8,128)} %all-reduce.4.cloned.1.call-done) | copy-start | bytes 786436 | tf_op jit(solution)/shard_map/while
  578.9 4.4 copy-start
  590.8 146.6 %all-reduce.4.cloned.1.call-start = ((), (), s32[]{:S(2)}) async-start(), calls=%async_computation | async-start | bytes 524288 | tf_op jit(solution)/shard_map/while/body/eval_jaxpr/psum | solution.py:64
  599.2 245.8 %all-reduce.6.cloned.1.call-start = ((), (), s32[]{:S(2)}) async-start(), calls=%async_computation.1 | async-start | bytes 8388608 | tf_op jit(solution)/shard_map/while/body/eval_jaxpr/psum | solution.py:74
  743.2 66.9 %copy-start.1 = (f32[512,128]{0,1:T(8,128)S(1)}, f32[512,128]{0,1:T(8,128)}, u32[]{:S(2)}) copy-start(f32[512,128]{0,1:T(8,128)} %all-reduce.4.cloned.1.call-done) | copy-start | bytes 786436 | tf_op jit(solution)/shard_map/while
  844.9 4.4 copy-start
  856.8 146.7 %all-reduce.4.cloned.1.call-start = ((), (), s32[]{:S(2)}) async-start(), calls=%async_computation | async-start | bytes 524288 | tf_op jit(solution)/shard_map/while/body/eval_jaxpr/psum | solution.py:64
  865.2 245.8 %all-reduce.6.cloned.1.call-start = ((), (), s32[]{:S(2)}) async-start(), calls=%async_computation.1 | async-start | bytes 8388608 | tf_op jit(solution)/shard_map/while/body/eval_jaxpr/psum | solution.py:74
  1009.3 66.9 %copy-start.1 = (f32[512,128]{0,1:T(8,128)S(1)}, f32[512,128]{0,1:T(8,128)}, u32[]{:S(2)}) copy-start(f32[512,128]{0,1:T(8,128)} %all-reduce.4.cloned.1.call-done) | copy-start | bytes 786436 | tf_op jit(solution)/shard_map/while
  1111.0 4.4 copy-start
Sparse Core Ops, SparseCore 0:
  58.2 146.9 all-reduce.3
  211.2 69.1 all-reduce.5
  333.2 138.1 all-reduce.3
  477.4 69.1 all-reduce.5
  599.3 138.0 all-reduce.3
  743.4 69.1 all-reduce.5
  865.3 138.1 all-reduce.3
  1009.5 69.0 all-reduce.5
where the time goes:
time: 1130 us
  waiting for transfers between devices  563 us (50%)
  blocking collectives  280 us (25%)
  other arithmetic  138 us (12%)
  matrix products  105 us (9%)
  local copies, waits for them, and re-layouts  17 us (2%)
  between operations  13.5 us (1%)
    psum x4, waiting for transfers between devices, one_block(): lax.psum((placed, mean_cols * first_member), ('mem', 'cell'))  562 us
    psum x4, blocking collectives, one_block(): lax.psum((placed, mean_cols * first_member), ('mem', 'cell'))  258 us
    another operation x12, other arithmetic, tri_solve(): lax.linalg.triangular_solve(update_matrix, right, left_side=True, lower=T...  81.4 us
    another operation x12, other arithmetic, one_block(): factor_low = jnp.linalg.cholesky(spread)  49.6 us
    dot_general x4, matrix products, one_block(): partial_cross = jnp.dot(prior_rows.T, anomaly, precision=highest)  23.3 us
  transfers between devices with their start and end apart: 10, of which 6 were waited for; matrix products, arithmetic and copies ran while one was open for 13% of the time, Pallas kernels for 0%

commit v1 on v0

v1 whole, which is shorter than its diff:
```python
import functools

import jax
import jax.numpy as jnp
from jax import lax
from jax.experimental import pallas as pl
from jax.experimental.pallas import tpu as pltpu
from jax.sharding import PartitionSpec as P

SAMPLE_TOTAL = 512
NOBS = 128
ALL_OBS = 512
HIGHEST = lax.Precision.HIGHEST
NT = (((1,), (1,)), ((), ()))
TN = (((0,), (0,)), ((), ()))
NN = (((1,), (0,)), ((), ()))
VMEM_LIMIT = 48 * 1024 * 1024


def halves(value):
    high = value.astype(jnp.bfloat16)
    low = (value - high.astype(jnp.float32)).astype(jnp.bfloat16)
    return high, low


def dot_split(left, right, dims):
    f32 = jnp.float32
    left_high, left_low = left
    right_high, right_low = right
    small = lax.dot_general(left_low, right_high, dims, preferred_element_type=f32)
    small = small + lax.dot_general(left_high, right_low, dims, preferred_element_type=f32)
    return small + lax.dot_general(left_high, right_high, dims, preferred_element_type=f32)


def dot3(left, right, dims):
    return dot_split(halves(left), halves(right), dims)


def dot6(left, right, dims):
    return lax.dot_general(
        left, right, dims, precision=HIGHEST, preferred_element_type=jnp.float32
    )


def forecast_kernel(x_ref, low_ref, high_ref, weight_ref, row_ref, col_ref, pieces_ref, seen_ref, flat_ref):
    members, rows, width = x_ref.shape
    row_at = lax.broadcasted_iota(jnp.int32, (rows, width), 0)
    col_at = lax.broadcasted_iota(jnp.int32, (rows, width), 1)
    east, west, north, south = [weight_ref[i] for i in range(4)]

    def member(m, carry):
        x = x_ref[m]
        to_east = jnp.where(col_at == width - 1, 0.0, pltpu.roll(x, width - 1, 1))
        to_west = jnp.where(col_at == 0, 0.0, pltpu.roll(x, 1, 1))
        to_north = jnp.where(row_at == 0, low_ref[m], pltpu.roll(x, 1, 0))
        to_south = jnp.where(row_at == rows - 1, high_ref[m], pltpu.roll(x, rows - 1, 0))
        f = (
            x
            + east * (to_east - x)
            + west * (to_west - x)
            + north * (to_north - x)
            + south * (to_south - x)
        )
        flat_ref[pl.ds(pl.multiple_of(m * rows, rows), rows), :] = f
        for h in range(2):
            for q in range(4):
                pieces_ref[4 * h + q, m] = f[8 * h : 8 * h + 8, 128 * q : 128 * q + 128]
        return carry

    lax.fori_loop(0, members, member, 0, unroll=4)
    pick = (lax.broadcasted_iota(jnp.int32, (width, ALL_OBS), 0) == col_ref[...]).astype(jnp.bfloat16)
    own_row = (lax.broadcasted_iota(jnp.int32, (rows, ALL_OBS), 0) == row_ref[...]).astype(jnp.float32)
    part = 8

    def select(g, carry):
        value = flat_ref[pl.ds(pl.multiple_of(g * part * rows, part * rows), part * rows), :]
        total = None
        for _ in range(3):
            cut = value.astype(jnp.bfloat16)
            value = value - cut.astype(jnp.float32)
            term = lax.dot_general(cut, pick, NN, preferred_element_type=jnp.float32)
            total = term if total is None else total + term
        total = total.reshape(part, rows, ALL_OBS) * own_row[None]
        seen_ref[pl.ds(pl.multiple_of(g * part, part), part), :] = jnp.sum(total, axis=1)
        return carry

    lax.fori_loop(0, members // part, select, 0, unroll=2)


def over_rows(value, row):
    return jnp.broadcast_to(value[row : row + 1, :], (8, NOBS))


def over_lanes(value, lane):
    return jnp.broadcast_to(value[:, lane : lane + 1], (8, NOBS))


def factor(block, root):
    count = NOBS // 8
    sub = lax.broadcasted_iota(jnp.int32, (8, NOBS), 0)
    lane = lax.broadcasted_iota(jnp.int32, (8, NOBS), 1)
    rows = [block[8 * i : 8 * i + 8, :] for i in range(count)]
    shifted = [(lane == sub + 8 * i).astype(jnp.float32) for i in range(count)]
    inverse = [None] * count
    for b in range(count):
        panel = rows[b]
        column = [over_lanes(panel, 8 * b + k) for k in range(8)]
        done = jnp.zeros((8, NOBS), jnp.float32)
        plus = shifted[b]
        inv_roots = []
        for k in range(8):
            at = 8 * b + k
            pivot = over_rows(column[k], k)
            inv = 1.0 / pivot
            inv_root = lax.rsqrt(pivot)
            inv_roots.append(inv_root)
            row = jnp.where(lane == at, 1.0, over_rows(panel, k))
            done = jnp.where(sub == k, row * inv_root, done)
            scaled = row * inv
            away = jnp.where(sub == k, -1.0, column[k])
            panel = jnp.where((sub == k) | (lane == at), 0.0, panel) - away * scaled
            plus_row = over_rows(plus, k) / (pivot * inv_root + over_rows(root[8 * b : 8 * b + 8, :], k))
            below = jnp.where(sub > k, column[k] * inv_root, 0.0)
            plus = jnp.where(sub == k, plus_row, plus - below * plus_row)
            for j in range(k + 1, 8):
                step = over_rows(column[j], k) * inv
                column[j] = jnp.where(sub == k, 0.0, column[j]) - away * step
        inverse[b] = jnp.where(lane <= sub + 8 * b, done, 0.0)
        shifted[b] = plus
        if b == count - 1:
            break
        for k in reversed(range(8)):
            above = jnp.where(sub < k, over_lanes(done, 8 * b + k), 0.0)
            row = over_rows(plus, k) * inv_roots[k]
            plus = jnp.where(sub == k, row, plus - above * row)
        panel_rows = [over_rows(panel, k) for k in range(8)]
        plus_rows = [over_rows(plus, k) for k in range(8)]
        inside = (lane >= 8 * b) & (lane < 8 * b + 8)
        for r in range(b + 1, count):
            left = [over_lanes(rows[r], 8 * b + k) for k in range(8)]
            new = jnp.where(inside, 0.0, rows[r])
            new_shifted = shifted[r]
            for k in range(8):
                new = new - left[k] * panel_rows[k]
                new_shifted = new_shifted - left[k] * plus_rows[k]
            rows[r] = new
            shifted[r] = new_shifted
    return jnp.concatenate(inverse, axis=0), jnp.concatenate(shifted, axis=0)


def transform_kernel(seen_ref, value_ref, var_ref, root_ref, high_ref, low_ref, cov_ref, state_ref, gain_ref, minus_ref):
    n = ALL_OBS
    blocks = n // NOBS
    seen = seen_ref[...]
    mean = jnp.sum(seen, axis=0, keepdims=True) / SAMPLE_TOTAL
    anomaly = seen - mean
    state_ref[0:SAMPLE_TOTAL, :] = anomaly
    state_ref[SAMPLE_TOTAL:, :] = jnp.broadcast_to(value_ref[...] - mean, (8, n))
    minus_ref[...] = anomaly
    cov = dot6(anomaly, anomaly, TN) / (SAMPLE_TOTAL - 1)
    eye = lax.broadcasted_iota(jnp.int32, (n, n), 0) == lax.broadcasted_iota(jnp.int32, (n, n), 1)
    cov_ref[...] = cov + jnp.where(eye, var_ref[...], 0.0)
    for j in range(blocks):
        low, high = NOBS * j, NOBS * (j + 1)
        inv_low, inv_sum = factor(cov_ref[low:high, low:high], root_ref[low:high, :])
        rest = high < n
        if rest:
            below = dot6(cov_ref[high:, low:high], inv_low, NT)
            cov_ref[high:, high:] = cov_ref[high:, high:] - dot6(below, below, NT)
            below = halves(below)
        inv_low, inv_sum = halves(inv_low), halves(inv_sum)
        gain = dot_split(halves(state_ref[:, low:high]), inv_low, NT)
        minus = dot_split(halves(minus_ref[:, low:high]), inv_sum, NT)
        gain_ref[:, low:high] = gain
        if rest:
            state_ref[:, high:] = state_ref[:, high:] - dot_split(halves(gain), below, NT)
            minus_ref[:, high:] = minus_ref[:, high:] - dot_split(halves(minus), below, NT)
        minus_ref[:, low:high] = minus
    mean_step = gain_ref[SAMPLE_TOTAL : SAMPLE_TOTAL + 1, :]
    left = (mean_step - minus_ref[...]) * (1.0 / (SAMPLE_TOTAL - 1))
    total = dot3(left, gain_ref[0:SAMPLE_TOTAL, :], NT)
    high_part, low_part = halves(total)
    high_ref[...] = high_part
    low_ref[...] = low_part


def update_kernel(high_ref, low_ref, cells_ref, out_ref):
    transform = (high_ref[...], low_ref[...])
    for r in range(0, 8, 2):
        field = jnp.concatenate(
            [cells_ref[pl.ds(r + i, SAMPLE_TOTAL, stride=8), :] for i in range(2)], axis=1
        )
        new = field + dot_split(transform, halves(field), NN)
        for i in range(2):
            out_ref[pl.ds(r + i, SAMPLE_TOTAL, stride=8), :] = new[:, 128 * i : 128 * i + 128]


def call(kernel, out_shape, scratch=(), flops=0, bytes_accessed=0):
    return pl.pallas_call(
        kernel,
        out_shape=out_shape,
        scratch_shapes=list(scratch),
        compiler_params=pltpu.CompilerParams(vmem_limit_bytes=VMEM_LIMIT),
        cost_estimate=pl.CostEstimate(flops=flops, bytes_accessed=bytes_accessed, transcendentals=0),
    )


def body(prior_samples, neighbour_weights, obs_cell, obs_value, obs_var, block_order):
    f32 = jnp.float32
    members_dev, tile_rows, width = prior_samples.shape
    mem_count, cell_count = lax.axis_size("mem"), lax.axis_size("cell")
    forward = [(i, i + 1) for i in range(cell_count - 1)]
    backward = [(i + 1, i) for i in range(cell_count - 1)]
    low = lax.ppermute(prior_samples[:, -1:, :], "cell", forward)
    high = lax.ppermute(prior_samples[:, :1, :], "cell", backward)
    cell = obs_cell[block_order].reshape(1, ALL_OBS)
    value = obs_value[block_order].reshape(1, ALL_OBS)
    var = obs_var[block_order].reshape(1, ALL_OBS)
    root = jnp.broadcast_to(jnp.sqrt(var).reshape(ALL_OBS, 1), (ALL_OBS, NOBS))
    row = cell // width - lax.axis_index("cell") * tile_rows
    col = cell % width

    pieces, seen = call(
        forecast_kernel,
        (
            jax.ShapeDtypeStruct((mem_count, members_dev, 8, 128), f32),
            jax.ShapeDtypeStruct((members_dev, ALL_OBS), f32),
        ),
        [pltpu.VMEM((members_dev * tile_rows, width), f32)],
    )(prior_samples, low, high, neighbour_weights, row, col)

    share = members_dev // cell_count
    seen = lax.all_to_all(seen.reshape(cell_count, share, ALL_OBS), "cell", 0, 0)
    seen = jnp.sum(seen, axis=0)
    seen = lax.all_to_all(jnp.broadcast_to(seen[None], (cell_count,) + seen.shape), "cell", 0, 0)
    seen = seen.reshape(members_dev, ALL_OBS)
    seen = lax.all_to_all(jnp.broadcast_to(seen[None], (mem_count,) + seen.shape), "mem", 0, 0)
    seen = seen.reshape(SAMPLE_TOTAL, ALL_OBS)
    cells = lax.all_to_all(pieces, "mem", 0, 0)

    square = (ALL_OBS, ALL_OBS)
    transform = call(
        transform_kernel,
        (jax.ShapeDtypeStruct(square, jnp.bfloat16),) * 2,
        [
            pltpu.VMEM(square, f32),
            pltpu.VMEM((SAMPLE_TOTAL + 8, ALL_OBS), f32),
            pltpu.VMEM((SAMPLE_TOTAL + 8, ALL_OBS), f32),
            pltpu.VMEM(square, f32),
        ],
        flops=20_000_000_000,
        bytes_accessed=2_000_000,
    )(seen, value, var, root)

    cells = cells.reshape(SAMPLE_TOTAL * 8, 128)
    new = call(update_kernel, jax.ShapeDtypeStruct(cells.shape, f32))(*transform, cells)
    new = lax.all_to_all(new.reshape(mem_count, members_dev, 8, 128), "mem", 0, 0)
    new = new.reshape(2, 4, members_dev, 8, 128).transpose(2, 0, 3, 1, 4)
    return new.reshape(prior_samples.shape)


def solution(mesh):
    return jax.shard_map(
        body,
        mesh=mesh,
        in_specs=(P("mem", "cell", None), P(None, "cell", None), P(), P(), P(), P()),
        out_specs=P("mem", "cell", None),
        check_vma=False,
    )
```

time: 1130 us -> 140 us (0.12)
  waiting for transfers between devices: 563 us -> 14.8 us
  blocking collectives: 280 us -> 57.9 us
  other arithmetic: 138 us -> 0.73 us
  matrix products: 105 us -> 0 us
  Pallas kernels: 0 us -> 32.6 us
  between operations: 13.5 us -> 0.13 us
  starting transfers between devices: 6.59 us -> 19.6 us
    psum x8 -> x0, waiting for transfers between devices: 562 us -> none  [the longest x4 562 us: one_block(): lax.psum((placed, mean_cols * first_member), ('mem', 'cell'))]
    psum x5 -> x0, blocking collectives: 280 us -> none  [the longest x4 258 us: one_block(): lax.psum((placed, mean_cols * first_member), ('mem', 'cell'))]
    another operation x24 -> x0, other arithmetic: 131 us -> none  [the longest x12 81.4 us: tri_solve(): lax.linalg.triangular_solve(update_matrix, right, left_side=True, lower=T...]
    dot_general x28 -> x0, matrix products: 82.7 us -> none  [the longest x4 23.3 us: one_block(): partial_cross = jnp.dot(prior_rows.T, anomaly, precision=highest)]
    all_to_all x0 -> x3, blocking collectives: none -> 57.9 us  [the longest x1 31.1 us: body(): lax.all_to_all(new.reshape(mem_count, members_dev, 8, 128), 'mem', 0, 0)]
    pallas_call x0 -> x3, Pallas kernels: none -> 32.6 us  [the longest x1 25.3 us: body(): call(transform_kernel, (jax.ShapeDtypeStruct(square, jnp.bfloat16),) * 2,...]
    another operation x16 -> x0, matrix products: 22.4 us -> none  [tri_solve(): lax.linalg.triangular_solve(update_matrix, right, left_side=True, lower=T...]
    all_to_all x0 -> x2, waiting for transfers between devices: none -> 14 us  [the longest x1 14 us: body(): lax.all_to_all(jnp.broadcast_to(seen[None], (mem_count,) + seen.shape), '...]
  transfers between devices with their start and end apart: 10 -> 4, of which waited for: 6 -> 2; matrix products, arithmetic and copies ran while one was open for 13% -> 2% of each run, Pallas kernels for 0% -> 18%
where the time goes in v1:
time: 140 us
  blocking collectives  57.9 us (41%)
  Pallas kernels  32.6 us (23%)
  starting transfers between devices  19.6 us (14%)
  waiting for transfers between devices  14.8 us (11%)
  local copies, waits for them, and re-layouts  13.9 us (10%)
    all_to_all x1, blocking collectives, body(): lax.all_to_all(new.reshape(mem_count, members_dev, 8, 128), 'mem', 0, 0)  31.1 us
    pallas_call x1, Pallas kernels, body(): call(transform_kernel, (jax.ShapeDtypeStruct(square, jnp.bfloat16),) * 2,...  25.3 us
    all_to_all x1, blocking collectives, body(): lax.all_to_all(seen.reshape(cell_count, share, ALL_OBS), 'cell', 0, 0)  16.7 us
    all_to_all x1, waiting for transfers between devices, body(): lax.all_to_all(jnp.broadcast_to(seen[None], (mem_count,) + seen.shape), '...  14 us
    all_to_all x1, blocking collectives, body(): lax.all_to_all(jnp.broadcast_to(seen[None], (cell_count,) + seen.shape),...  10.1 us
    all_to_all x1, starting transfers between devices, body(): lax.all_to_all(jnp.broadcast_to(seen[None], (mem_count,) + seen.shape), '...  8.97 us
    unnamed x20, local copies, waits for them, and re-layouts  7.49 us
    pallas_call x1, Pallas kernels, body(): call(forecast_kernel, (jax.ShapeDtypeStruct((mem_count, members_dev, 8, 1...  5.15 us
  transfers between devices with their start and end apart: 4, of which 2 were waited for; matrix products, arithmetic and copies ran while one was open for 2% of the time, Pallas kernels for 18%

profile of v1, /device:TPU:1, one launch (start us, length us, event | category | flops | bytes accessed | tf_op | source)
XLA Modules:
  0.0 139.7 jit_solution(3055683131270548412)
XLA Ops:
  0.0 1.8 %fusion.1 = (f32[64,1,512]{2,1,0:T(1,128)S(1)}, f32[64,1,512]{2,1,0:T(1,128)S(1)}) fusion(f32[64,16,512]{2,1,0:T(8,128)} %x_ref.1), kind=kLoop, calls=%fused_computation.13 | loop fusion | bytes 524288 | tf_op jit(solution)/shard_map/slice | solution.py:215
  1.8 1.3 collective-permute-start.1
  3.1 5.0 %collective-permute-start = (f32[64,1,512]{2,1,0:T(1,128)S(1)}, f32[64,1,512]{2,1,0:T(1,128)S(1)}, u32[]{:S(2)}, u32[]{:S(2)}) collective-permute-start(f32[64,1,512]{2,1,0:T(1,128)S(1)} %get-tuple-element.16), channel_id=1, source_target_pairs={{0,1},{1,2},{2,3},{3,4},{4,5},{5,6},{6,7},{7,8},{8,9},{9,10},{10,1... | collective-permute-start | bytes 393224 | tf_op jit(solution)/shard_map/ppermute | solution.py:214
  8.1 0.7 compare_select_fusion.3
  8.8 0.6 gather_fusion
  9.4 0.8 collective-permute-done.low_ref
  10.2 1.6 %copy-done.1 = f32[64,16,512]{2,1,0:T(8,128)S(1)} copy-done((f32[64,16,512]{2,1,0:T(8,128)S(1)}, f32[64,16,512]{2,1,0:T(8,128)}, u32[]{:S(2)}) %copy-start.1) | copy-done | bytes 2097176
  11.8 0.9 copy-done.7
  12.7 5.1 %shard_map.64 = (f32[8,64,8,128]{3,2,1,0:T(8,128)S(1)}, f32[64,512]{1,0:T(8,128)S(1)}) custom-call(f32[64,16,512]{2,1,0:T(8,128)S(1)} %copy-done.1, f32[64,1,512]{2,1,0:T(1,128)S(1)} %collective-permute-done.low_ref, f32[64,1,512]{2,1,0:T(1,128)S(1)} %collective-permute-done.1.high_ref, f32[4,16,512]{2,1,0:T(8,128)S(1)} %copy-done.7, ...), custom_call_target="tpu_custom_call" | custom-call | tf_op jit(solution)/shard_map/pallas_call | solution.py:223
  17.9 1.3 copy-done.2
  19.3 16.7 %all_to_all.25 = f32[16,4,512]{2,1,0:T(4,128)S(1)} all-to-all(f32[16,4,512]{2,1,0:T(4,128)S(1)} %reshape.184), channel_id=1, replica_groups=mesh['mem'=8,'cell'=16] {'cell'}, dimensions={0} | all-to-all | bytes 262144 | tf_op jit(solution)/shard_map/all_to_all | solution.py:233
  36.0 10.1 %all_to_all.26 = f32[16,4,512]{2,1,0:T(4,128)S(1)} all-to-all(f32[16,4,512]{2,1,0:T(4,128)S(1)} %broadcast_in_dim.11), channel_id=1, replica_groups=mesh['mem'=8,'cell'=16] {'cell'}, dimensions={0} | all-to-all | bytes 262144 | tf_op jit(solution)/shard_map/all_to_all | solution.py:235
  46.2 1.1 broadcast_in_dim.26
  47.3 9.0 %all-to-all-start.2 = ((f32[8,64,512]{2,1,0:T(8,128)}), f32[8,64,512]{2,1,0:T(8,128)S(1)}, u32[]{:S(2)}, u32[]{:S(2)}) async-start(f32[8,64,512]{2,1,0:T(8,128)} %broadcast_in_dim.26), calls=%async_computation.2 | async-start | bytes 2097152 | tf_op jit(solution)/shard_map/all_to_all | solution.py:237
  57.4 14.0 %all-to-all-done.2 = f32[8,64,512]{2,1,0:T(8,128)S(1)} async-done(((f32[8,64,512]{2,1,0:T(8,128)}), f32[8,64,512]{2,1,0:T(8,128)S(1)}, u32[]{:S(2)}, u32[]{:S(2)}) %all-to-all-start.2) | async-done | bytes 1048608 | tf_op jit(solution)/shard_map/all_to_all | solution.py:237
  71.3 4.4 %all-to-all-start.3 = ((f32[8,64,8,128]{3,2,1,0:T(8,128)}), f32[8,64,8,128]{3,2,1,0:T(8,128)S(1)}, u32[]{:S(2)}, u32[]{:S(2)}) async-start(f32[8,64,8,128]{3,2,1,0:T(8,128)} %copy-done.2), calls=%async_computation.3 | async-start | bytes 4194304 | tf_op jit(solution)/shard_map/all_to_all | solution.py:239
  75.8 25.3 %shard_map.65 = (bf16[512,512]{1,0:T(8,128)(2,1)S(1)}, bf16[512,512]{1,0:T(8,128)(2,1)S(1)}) custom-call(f32[512,512]{1,0:T(8,128)S(1)} %bitcast.16, f32[1,512]{1,0:T(1,128)S(1)} %bitcast.18, f32[1,512]{1,0:T(1,128)S(1)} %bitcast.17, f32[512,128]{1,0:T(8,128)S(1)} %broadcast_in_dim.27.root_ref), custom_call_target="tpu_custom_call" | custom-call | flops 20000000000 | bytes 2000000 | tf_op jit(solution)/shard_map/pallas_call | solution.py:242
  101.2 0.8 copy-done.3
  102.0 0.8 copy-done.5
  102.8 1.0 copy-done.4
  103.8 1.0 copy-done.6
  104.9 2.1 %shard_map.66 = f32[4096,128]{1,0:T(8,128)S(1)} custom-call(bf16[512,512]{1,0:T(8,128)(2,1)S(1)} %copy-done.4, bf16[512,512]{1,0:T(8,128)(2,1)S(1)} %copy-done.6, f32[4096,128]{1,0:T(8,128)S(1)} %bitcast.14), custom_call_target="tpu_custom_call" | custom-call | tf_op jit(solution)/shard_map/pallas_call | solution.py:256
  107.0 31.1 %all_to_all.27 = f32[8,64,8,128]{3,2,1,0:T(8,128)S(1)} all-to-all(f32[8,64,8,128]{3,2,1,0:T(8,128)S(1)} %bitcast.15), channel_id=1, replica_groups=mesh['mem'=8,'cell'=16] {'mem'}, dimensions={0} | all-to-all | bytes 4194304 | tf_op jit(solution)/shard_map/all_to_all | solution.py:257
  138.1 1.6 %copy.9 = f32[2,4,64,8,128]{4,3,1,0,2:T(8,128)} copy(f32[2,4,64,8,128]{4,3,2,1,0:T(8,128)S(1)} %bitcast.19) | data formatting | bytes 4194304 | tf_op jit(solution)/shard_map/reshape | solution.py:258
  (26 shorter events, 1.4 us)
Async XLA Ops:
  0.0 8.8 %copy-start = (s32[4,128]{1,0:T(4,128)S(1)}, s32[4,128]{1,0:T(4,128)}, u32[]{:S(2)}) copy-start(s32[4,128]{1,0:T(4,128)} %param.8) | copy-start | bytes 6148
  1.8 7.6 %collective-permute-start.1 = (f32[64,1,512]{2,1,0:T(1,128)S(1)}, f32[64,1,512]{2,1,0:T(1,128)S(1)}, u32[]{:S(2)}, u32[]{:S(2)}) collective-permute-start(f32[64,1,512]{2,1,0:T(1,128)S(1)} %get-tuple-element.15), channel_id=1, source_target_pairs={{1,0},{2,1},{3,2},{4,3},{5,4},{6,5},{7,6},{8,7},{9,8},{10,9},{11,1... | collective-permute-start | bytes 393224 | tf_op jit(solution)/shard_map/ppermute | solution.py:215
  3.1 7.1 %collective-permute-start = (f32[64,1,512]{2,1,0:T(1,128)S(1)}, f32[64,1,512]{2,1,0:T(1,128)S(1)}, u32[]{:S(2)}, u32[]{:S(2)}) collective-permute-start(f32[64,1,512]{2,1,0:T(1,128)S(1)} %get-tuple-element.16), channel_id=1, source_target_pairs={{0,1},{1,2},{2,3},{3,4},{4,5},{5,6},{6,7},{7,8},{8,9},{9,10},{10,1... | collective-permute-start | bytes 393224 | tf_op jit(solution)/shard_map/ppermute | solution.py:214
  10.2 1.6 %copy-start.1 = (f32[64,16,512]{2,1,0:T(8,128)S(1)}, f32[64,16,512]{2,1,0:T(8,128)}, u32[]{:S(2)}) copy-start(f32[64,16,512]{2,1,0:T(8,128)} %x_ref.1) | copy-start | bytes 6291460
  11.8 0.9 copy-start.7
  17.9 1.3 copy-start.2
  35.9 20.3 %copy-start.8 = (f32[4,128]{1,0:T(4,128)S(1)}, f32[4,128]{1,0:T(4,128)}, u32[]{:S(2)}) copy-start(f32[4,128]{1,0:T(4,128)} %param.10) | copy-start | bytes 6148
  35.9 20.9 %copy-start.9 = (f32[4,128]{1,0:T(4,128)S(1)}, f32[4,128]{1,0:T(4,128)}, u32[]{:S(2)}) copy-start(f32[4,128]{1,0:T(4,128)} %param.9) | copy-start | bytes 6148
  47.3 24.1 %all-to-all-start.2 = ((f32[8,64,512]{2,1,0:T(8,128)}), f32[8,64,512]{2,1,0:T(8,128)S(1)}, u32[]{:S(2)}, u32[]{:S(2)}) async-start(f32[8,64,512]{2,1,0:T(8,128)} %broadcast_in_dim.26), calls=%async_computation.2 | async-start | bytes 2097152 | tf_op jit(solution)/shard_map/all_to_all | solution.py:237
  71.3 31.5 %all-to-all-start.3 = ((f32[8,64,8,128]{3,2,1,0:T(8,128)}), f32[8,64,8,128]{3,2,1,0:T(8,128)S(1)}, u32[]{:S(2)}, u32[]{:S(2)}) async-start(f32[8,64,8,128]{3,2,1,0:T(8,128)} %copy-done.2), calls=%async_computation.3 | async-start | bytes 4194304 | tf_op jit(solution)/shard_map/all_to_all | solution.py:239
  101.2 0.8 copy-start.3
  102.0 0.8 copy-start.5
  102.8 1.0 copy-start.4
  103.8 1.0 copy-start.6

commit v2 on v1

--- a/solution.py
+++ b/solution.py
@@ -15,6 +15,8 @@
 TN = (((0,), (0,)), ((), ()))
 NN = (((1,), (0,)), ((), ()))
 VMEM_LIMIT = 48 * 1024 * 1024
+INNER = tuple(range(4, 12))
+OUTER = (0, 1, 2, 3, 12, 13, 14, 15)
 
 
 def halves(value):
@@ -42,18 +44,18 @@
     )
 
 
-def forecast_kernel(x_ref, low_ref, high_ref, weight_ref, row_ref, col_ref, pieces_ref, seen_ref, flat_ref):
+def forecast_kernel(x_ref, weight_ref, row_ref, col_ref, inner_ref, outer_ref, edge_ref, seen_ref, flat_ref, own_ref, raw_ref):
     members, rows, width = x_ref.shape
+    col_at = lax.broadcasted_iota(jnp.int32, (rows, width), 1)
     row_at = lax.broadcasted_iota(jnp.int32, (rows, width), 0)
-    col_at = lax.broadcasted_iota(jnp.int32, (rows, width), 1)
     east, west, north, south = [weight_ref[i] for i in range(4)]
 
     def member(m, carry):
         x = x_ref[m]
         to_east = jnp.where(col_at == width - 1, 0.0, pltpu.roll(x, width - 1, 1))
         to_west = jnp.where(col_at == 0, 0.0, pltpu.roll(x, 1, 1))
-        to_north = jnp.where(row_at == 0, low_ref[m], pltpu.roll(x, 1, 0))
-        to_south = jnp.where(row_at == rows - 1, high_ref[m], pltpu.roll(x, rows - 1, 0))
+        to_north = jnp.where(row_at == 0, 0.0, pltpu.roll(x, 1, 0))
+        to_south = jnp.where(row_at == rows - 1, 0.0, pltpu.roll(x, rows - 1, 0))
         f = (
             x
             + east * (to_east - x)
@@ -61,30 +63,70 @@
             + north * (to_north - x)
             + south * (to_south - x)
         )
-        flat_ref[pl.ds(pl.multiple_of(m * rows, rows), rows), :] = f
-        for h in range(2):
-            for q in range(4):
-                pieces_ref[4 * h + q, m] = f[8 * h : 8 * h + 8, 128 * q : 128 * q + 128]
+        for q in range(4):
+            at = pl.multiple_of(q * members * rows + m * rows, rows)
+            flat_ref[pl.ds(at, rows), :] = f[:, 128 * q : 128 * q + 128]
         return carry
 
     lax.fori_loop(0, members, member, 0, unroll=4)
     pick = (lax.broadcasted_iota(jnp.int32, (width, ALL_OBS), 0) == col_ref[...]).astype(jnp.bfloat16)
-    own_row = (lax.broadcasted_iota(jnp.int32, (rows, ALL_OBS), 0) == row_ref[...]).astype(jnp.float32)
+    at_row = row_ref[...]
+    own_row = (lax.broadcasted_iota(jnp.int32, (rows, ALL_OBS), 0) == at_row).astype(jnp.float32)
     part = 8
 
-    def select(g, carry):
-        value = flat_ref[pl.ds(pl.multiple_of(g * part * rows, part * rows), part * rows), :]
+    def picked(value):
         total = None
         for _ in range(3):
             cut = value.astype(jnp.bfloat16)
             value = value - cut.astype(jnp.float32)
             term = lax.dot_general(cut, pick, NN, preferred_element_type=jnp.float32)
             total = term if total is None else total + term
-        total = total.reshape(part, rows, ALL_OBS) * own_row[None]
-        seen_ref[pl.ds(pl.multiple_of(g * part, part), part), :] = jnp.sum(total, axis=1)
+        return total
+
+    def select(g, carry):
+        start = [q * members * rows + g * part * rows for q in range(4)]
+        value = [flat_ref[pl.ds(pl.multiple_of(at, part * rows), part * rows), :] for at in start]
+        value = jnp.concatenate(value, axis=1)
+        total = picked(value).reshape(part, rows, ALL_OBS) * own_row[None]
+        own_ref[pl.ds(pl.multiple_of(g * part, part), part), :] = jnp.sum(total, axis=1)
         return carry
 
     lax.fori_loop(0, members // part, select, 0, unroll=2)
+    top, bottom = x_ref[:, 0, :], x_ref[:, rows - 1, :]
+    edge_ref[0] = top
+    edge_ref[1] = bottom
+    raw_ref[...] = jnp.where(at_row == -1, picked(top), 0.0) + jnp.where(at_row == rows, picked(bottom), 0.0)
+    weight = jnp.concatenate([north[0:8], south[rows - 8 :]], axis=0)
+    weight = picked(weight)
+    weight = jnp.where(at_row == 0, weight[0:1], 0.0) + jnp.where(at_row == rows - 1, weight[15:16], 0.0)
+    groups, share = seen_ref.shape[0], members // seen_ref.shape[0]
+    for q in range(4):
+        lanes = slice(128 * q, 128 * q + 128)
+        for g in range(groups):
+            seen_ref[g, share * q : share * q + share, :] = own_ref[share * g : share * g + share, lanes]
+            seen_ref[g, 16 + share * q : 16 + share * q + share, :] = raw_ref[share * g : share * g + share, lanes]
+            seen_ref[g, 32 + q : 33 + q, :] = weight[:, lanes]
+    for g in range(groups):
+        seen_ref[g, 36:40, :] = jnp.zeros((4, 128), jnp.float32)
+    for r in range(rows):
+        for q in range(4):
+            value = flat_ref[pl.ds(q * members * rows + r, members, stride=rows), :]
+            lanes = slice(128 * q, 128 * q + 128)
+            if r in INNER:
+                at = width * (r - INNER[0])
+                inner_ref[:, at + 128 * q : at + 128 * q + 128] = value
+            else:
+                outer_ref[OUTER.index(r), :, lanes] = value
+
+
+def seen_kernel(parts_ref, out_ref):
+    total = parts_ref[0]
+    for i in range(1, parts_ref.shape[0]):
+        total = total + parts_ref[i]
+    for q in range(4):
+        own = total[4 * q : 4 * q + 4]
+        raw = total[16 + 4 * q : 20 + 4 * q]
+        out_ref[:, 128 * q : 128 * q + 128] = own + raw * total[32 + q : 33 + q]
 
 
 def over_rows(value, row):
@@ -148,14 +190,18 @@
     return jnp.concatenate(inverse, axis=0), jnp.concatenate(shifted, axis=0)
 
 
-def transform_kernel(seen_ref, value_ref, var_ref, root_ref, high_ref, low_ref, cov_ref, state_ref, gain_ref, minus_ref):
+def transform_kernel(order_ref, seen_ref, value_ref, var_ref, root_ref, high_ref, low_ref, cov_ref, state_ref, gain_ref, minus_ref):
     n = ALL_OBS
     blocks = n // NOBS
-    seen = seen_ref[...]
-    mean = jnp.sum(seen, axis=0, keepdims=True) / SAMPLE_TOTAL
-    anomaly = seen - mean
-    state_ref[0:SAMPLE_TOTAL, :] = anomaly
+    slots, share = seen_ref.shape[0], seen_ref.shape[1]
+    total = seen_ref[0]
+    for s in range(1, slots):
+        total = total + seen_ref[s]
+    mean = jnp.sum(total, axis=0, keepdims=True) / SAMPLE_TOTAL
+    for s in range(slots):
+        state_ref[pl.ds(pl.multiple_of(order_ref[s] * share, share), share), :] = seen_ref[s] - mean
     state_ref[SAMPLE_TOTAL:, :] = jnp.broadcast_to(value_ref[...] - mean, (8, n))
+    anomaly = state_ref[0:SAMPLE_TOTAL, :]
     minus_ref[...] = anomaly
     cov = dot6(anomaly, anomaly, TN) / (SAMPLE_TOTAL - 1)
     eye = lax.broadcasted_iota(jnp.int32, (n, n), 0) == lax.broadcasted_iota(jnp.int32, (n, n), 1)
@@ -184,24 +230,43 @@
     low_ref[...] = low_part
 
 
-def update_kernel(high_ref, low_ref, cells_ref, out_ref):
-    transform = (high_ref[...], low_ref[...])
-    for r in range(0, 8, 2):
-        field = jnp.concatenate(
-            [cells_ref[pl.ds(r + i, SAMPLE_TOTAL, stride=8), :] for i in range(2)], axis=1
-        )
-        new = field + dot_split(transform, halves(field), NN)
-        for i in range(2):
-            out_ref[pl.ds(r + i, SAMPLE_TOTAL, stride=8), :] = new[:, 128 * i : 128 * i + 128]
-
-
-def call(kernel, out_shape, scratch=(), flops=0, bytes_accessed=0):
+def outer_kernel(high_ref, low_ref, cells_ref, out_ref):
+    field = cells_ref[...]
+    out_ref[...] = field + dot_split((high_ref[...], low_ref[...]), halves(field), NN)
+
+
+def inner_kernel(place_ref, high_ref, low_ref, own_ref, cells_ref, out_ref):
+    out_ref[...] = own_ref[...] + dot_split(
+        (high_ref[...], low_ref[...]), halves(cells_ref[...]), NN
+    )
+
+
+def join_kernel(inner_ref, outer_ref, out_ref, flat_ref):
+    members = inner_ref.shape[0]
+    width = outer_ref.shape[2]
+    count = out_ref.shape[0]
+    rows = count // members
+    for r in range(rows):
+        if r in INNER:
+            value = inner_ref[:, width * (r - INNER[0]) : width * (r - INNER[0] + 1)]
+        else:
+            value = outer_ref[OUTER.index(r)]
+        for q in range(width // 128):
+            at = pl.ds(q * count + r, members, stride=rows)
+            flat_ref[at, :] = value[:, 128 * q : 128 * q + 128]
+    for q in range(width // 128):
+        out_ref[:, 128 * q : 128 * q + 128] = flat_ref[count * q : count * (q + 1), :]
+
+
+def call(kernel, out_shape, scratch=(), flops=0, bytes_accessed=0, in_specs=None):
+    extra = {} if in_specs is None else {"in_specs": in_specs}
     return pl.pallas_call(
         kernel,
         out_shape=out_shape,
         scratch_shapes=list(scratch),
         compiler_params=pltpu.CompilerParams(vmem_limit_bytes=VMEM_LIMIT),
         cost_estimate=pl.CostEstimate(flops=flops, bytes_accessed=bytes_accessed, transcendentals=0),
+        **extra,
     )
 
 
@@ -209,37 +274,59 @@
     f32 = jnp.float32
     members_dev, tile_rows, width = prior_samples.shape
     mem_count, cell_count = lax.axis_size("mem"), lax.axis_size("cell")
-    forward = [(i, i + 1) for i in range(cell_count - 1)]
-    backward = [(i + 1, i) for i in range(cell_count - 1)]
-    low = lax.ppermute(prior_samples[:, -1:, :], "cell", forward)
-    high = lax.ppermute(prior_samples[:, :1, :], "cell", backward)
+    me = lax.axis_index("mem")
     cell = obs_cell[block_order].reshape(1, ALL_OBS)
     value = obs_value[block_order].reshape(1, ALL_OBS)
     var = obs_var[block_order].reshape(1, ALL_OBS)
     root = jnp.broadcast_to(jnp.sqrt(var).reshape(ALL_OBS, 1), (ALL_OBS, NOBS))
     row = cell // width - lax.axis_index("cell") * tile_rows
     col = cell % width
-
-    pieces, seen = call(
+    share = members_dev // cell_count
+    inner_cells = len(INNER) * width
+
+    inner, outer, edge, seen = call(
         forecast_kernel,
         (
-            jax.ShapeDtypeStruct((mem_count, members_dev, 8, 128), f32),
-            jax.ShapeDtypeStruct((members_dev, ALL_OBS), f32),
+            jax.ShapeDtypeStruct((members_dev, inner_cells), f32),
+            jax.ShapeDtypeStruct((len(OUTER), members_dev, width), f32),
+            jax.ShapeDtypeStruct((2, members_dev, width), f32),
+            jax.ShapeDtypeStruct((cell_count, 40, 128), f32),
         ),
-        [pltpu.VMEM((members_dev * tile_rows, width), f32)],
-    )(prior_samples, low, high, neighbour_weights, row, col)
-
-    share = members_dev // cell_count
-    seen = lax.all_to_all(seen.reshape(cell_count, share, ALL_OBS), "cell", 0, 0)
-    seen = jnp.sum(seen, axis=0)
+        [
+            pltpu.VMEM((members_dev * tile_rows * 4, 128), f32),
+            pltpu.VMEM((members_dev, ALL_OBS), f32),
+            pltpu.VMEM((members_dev, ALL_OBS), f32),
+        ],
+    )(prior_samples, neighbour_weights, row, col)
+
+    seen = lax.all_to_all(seen, "cell", 0, 0)
+    all_inner = lax.all_gather(inner, "mem", tiled=True)
+    forward = [(i, i + 1) for i in range(cell_count - 1)]
+    backward = [(i + 1, i) for i in range(cell_count - 1)]
+    low = lax.ppermute(edge[1], "cell", forward)
+    high = lax.ppermute(edge[0], "cell", backward)
+    last = len(OUTER) - 1
+    outer = outer.at[0].add(neighbour_weights[2, 0] * low)
+    outer = outer.at[last].add(neighbour_weights[3, tile_rows - 1] * high)
+    cells = lax.all_to_all(outer, "mem", 0, 0)
+
+    seen = call(seen_kernel, jax.ShapeDtypeStruct((share, ALL_OBS), f32))(seen)
     seen = lax.all_to_all(jnp.broadcast_to(seen[None], (cell_count,) + seen.shape), "cell", 0, 0)
-    seen = seen.reshape(members_dev, ALL_OBS)
-    seen = lax.all_to_all(jnp.broadcast_to(seen[None], (mem_count,) + seen.shape), "mem", 0, 0)
-    seen = seen.reshape(SAMPLE_TOTAL, ALL_OBS)
-    cells = lax.all_to_all(pieces, "mem", 0, 0)
+    seen = seen.reshape(1, members_dev, ALL_OBS)
+    turns = [
+        lax.ppermute(seen, "mem", [(i, (i + 2 * d) % mem_count) for i in range(mem_count)])
+        for d in range(1, mem_count // 2)
+    ]
+    seen = jnp.concatenate([seen] + turns, axis=0)
+    other = lax.ppermute(seen, "mem", [(i, i ^ 1) for i in range(mem_count)])
+    seen = jnp.concatenate([seen, other], axis=0)
+    turn = jnp.arange(mem_count // 2, dtype=jnp.int32)
+    order = (me - 2 * turn) % mem_count
+    order = jnp.concatenate([order, order ^ 1])
 
     square = (ALL_OBS, ALL_OBS)
-    transform = call(
+    vmem = pl.BlockSpec(memory_space=pltpu.VMEM)
+    high_part, low_part = call(
         transform_kernel,
         (jax.ShapeDtypeStruct(square, jnp.bfloat16),) * 2,
         [
@@ -250,12 +337,38 @@
         ],
         flops=20_000_000_000,
         bytes_accessed=2_000_000,
-    )(seen, value, var, root)
-
-    cells = cells.reshape(SAMPLE_TOTAL * 8, 128)
-    new = call(update_kernel, jax.ShapeDtypeStruct(cells.shape, f32))(*transform, cells)
-    new = lax.all_to_all(new.reshape(mem_count, members_dev, 8, 128), "mem", 0, 0)
-    new = new.reshape(2, 4, members_dev, 8, 128).transpose(2, 0, 3, 1, 4)
+        in_specs=[pl.BlockSpec(memory_space=pltpu.SMEM)] + [vmem] * 4,
+    )(order, seen, value, var, root)
+
+    new = call(outer_kernel, jax.ShapeDtypeStruct((SAMPLE_TOTAL, width), f32))(
+        high_part, low_part, cells.reshape(SAMPLE_TOTAL, width)
+    )
+    new = lax.all_to_all(new.reshape(mem_count, members_dev, width), "mem", 0, 0)
+
+    block = 1024
+    mine = pl.BlockSpec((members_dev, ALL_OBS), lambda i, place: (place[0], 0))
+    inner = pl.pallas_call(
+        inner_kernel,
+        out_shape=jax.ShapeDtypeStruct((members_dev, inner_cells), f32),
+        grid_spec=pltpu.PrefetchScalarGridSpec(
+            num_scalar_prefetch=1,
+            grid=(inner_cells // block,),
+            in_specs=[
+                mine,
+                mine,
+                pl.BlockSpec((members_dev, block), lambda i, place: (0, i)),
+                pl.BlockSpec((SAMPLE_TOTAL, block), lambda i, place: (0, i)),
+            ],
+            out_specs=pl.BlockSpec((members_dev, block), lambda i, place: (0, i)),
+        ),
+        compiler_params=pltpu.CompilerParams(vmem_limit_bytes=VMEM_LIMIT),
+        cost_estimate=pl.CostEstimate(flops=3_000_000_000, bytes_accessed=10_000_000, transcendentals=0),
+    )(me.reshape(1), high_part, low_part, inner, all_inner)
+    new = call(
+        join_kernel,
+        jax.ShapeDtypeStruct((members_dev * tile_rows, width), f32),
+        [pltpu.VMEM((members_dev * tile_rows * 4, 128), f32)],
+    )(inner, new)
     return new.reshape(prior_samples.shape)
 
 

time: 140 us -> 132 us (0.943)
  blocking collectives: 57.9 us -> 0 us
  starting transfers between devices: 19.6 us -> 36.6 us
  between operations: 0.13 us -> 13.6 us
  Pallas kernels: 32.6 us -> 45.7 us
  waiting for transfers between devices: 14.8 us -> 25.8 us
  local copies, waits for them, and re-layouts: 13.9 us -> 5.87 us
  other arithmetic: 0.73 us -> 3.98 us
    all_to_all x3 -> x0, blocking collectives: 57.9 us -> none  [the longest x1 31.1 us: body(): lax.all_to_all(new.reshape(mem_count, members_dev, 8, 128), 'mem', 0, 0)]
    pallas_call x2 -> x5, Pallas kernels: 7.26 us -> 19.5 us  [the longest x1 8.83 us: body(): call(forecast_kernel, (jax.ShapeDtypeStruct((members_dev, inner_cells), f...]
    all_to_all x2 -> x4, starting transfers between devices: 13.3 us -> 23 us  [the longest x1 8.62 us: body(): seen = lax.all_to_all(seen, 'cell', 0, 0)]
    ppermute x2 -> x6, waiting for transfers between devices: 0.84 us -> 8.51 us  [the longest x3 8.51 us: body(): lax.ppermute(seen, 'mem', [(i, (i + 2 * d) % mem_count) for i in range(me...]
    ppermute x2 -> x6, starting transfers between devices: 6.3 us -> 13.5 us  [the longest x3 4.87 us: body(): lax.ppermute(seen, 'mem', [(i, (i + 2 * d) % mem_count) for i in range(me...]
    unnamed x20 -> x14, local copies, waits for them, and re-layouts: 7.49 us -> 2.55 us
    all_to_all x2 -> x4, waiting for transfers between devices: 14 us -> 17.3 us  [the longest x1 9.22 us: body(): lax.all_to_all(new.reshape(mem_count, members_dev, width), 'mem', 0, 0)]
    scatter-add x0 -> x2, other arithmetic: none -> 3.15 us  [the longest x1 1.58 us: body(): outer = outer.at[0].add(neighbour_weights[2, 0] * low)]
  transfers between devices with their start and end apart: 4 -> 11, of which waited for: 2 -> 5; matrix products, arithmetic and copies ran while one was open for 2% -> 5% of each run, Pallas kernels for 18% -> 26%
where the time goes in v2:
time: 132 us; the launch traced here: 131 us
  Pallas kernels  45.7 us (35%)
  starting transfers between devices  36.6 us (28%)
  waiting for transfers between devices  25.8 us (20%)
  between operations  13.6 us (10%)
  local copies, waits for them, and re-layouts  5.87 us (4%)
  other arithmetic  3.98 us (3%)
    pallas_call x1, Pallas kernels, body(): call(transform_kernel, (jax.ShapeDtypeStruct(square, jnp.bfloat16),) * 2,...  26.1 us
    all_to_all x1, waiting for transfers between devices, body(): lax.all_to_all(new.reshape(mem_count, members_dev, width), 'mem', 0, 0)  9.22 us
    pallas_call x1, Pallas kernels, body(): call(forecast_kernel, (jax.ShapeDtypeStruct((members_dev, inner_cells), f...  8.83 us
    all_to_all x1, starting transfers between devices, body(): seen = lax.all_to_all(seen, 'cell', 0, 0)  8.62 us
    ppermute x3, waiting for transfers between devices, body(): lax.ppermute(seen, 'mem', [(i, (i + 2 * d) % mem_count) for i in range(me...  8.51 us
    all_to_all x1, waiting for transfers between devices, body(): lax.all_to_all(jnp.broadcast_to(seen[None], (cell_count,) + seen.shape),...  6.08 us
    pallas_call x1, Pallas kernels, body(): pl.pallas_call(inner_kernel, out_shape=jax.ShapeDtypeStruct((members_dev,...  5.87 us
    all_to_all x1, starting transfers between devices, body(): lax.all_to_all(jnp.broadcast_to(seen[None], (cell_count,) + seen.shape),...  5.43 us
  transfers between devices with their start and end apart: 11, of which 5 were waited for; matrix products, arithmetic and copies ran while one was open for 5% of the time, Pallas kernels for 26%

profile of v2, /device:TPU:1, one launch (start us, length us, event | category | flops | bytes accessed | tf_op | source)
XLA Modules:
  0.0 131.5 jit_solution(17585165408039549099)
XLA Ops:
  7.8 1.6 %copy-done.1 = f32[64,16,512]{2,1,0:T(8,128)S(1)} copy-done((f32[64,16,512]{2,1,0:T(8,128)S(1)}, f32[64,16,512]{2,1,0:T(8,128)}, u32[]{:S(2)}) %copy-start.1) | copy-done | bytes 2097176
  9.4 0.9 copy-done.2
  10.3 8.8 %shard_map.64 = (f32[64,4096]{1,0:T(8,128)}, f32[8,64,512]{2,1,0:T(8,128)}, f32[2,64,512]{2,1,0:T(8,128)S(1)}, f32[16,40,128]{2,1,0:T(8,128)}) custom-call(f32[64,16,512]{2,1,0:T(8,128)S(1)} %copy-done.1, f32[4,16,512]{2,1,0:T(8,128)S(1)} %copy-done.2, s32[1,512]{1,0:T(1,128)S(1)} %fusion.2.row_ref, s32[1,512]{1,0:T(1,128)S(1)} %get-tuple-element.41.col_ref), custom_call_target="tpu_custom_call" | custom-call | tf_op jit(solution)/shard_map/pallas_call | solution.py:287
  19.2 8.6 %all-to-all-start = ((f32[16,40,128]{2,1,0:T(8,128)}), f32[16,40,128]{2,1,0:T(8,128)S(1)}, u32[]{:S(2)}, u32[]{:S(2)}) async-start(f32[16,40,128]{2,1,0:T(8,128)} %get-tuple-element.35), calls=%async_computation | async-start | bytes 655360 | tf_op jit(solution)/shard_map/all_to_all | solution.py:302
  27.8 3.3 %collective-permute-start.4 = (f32[64,512]{1,0:T(8,128)S(1)}, f32[64,512]{1,0:T(8,128)S(1)}, u32[]{:S(2)}, u32[]{:S(2)}) collective-permute-start(f32[64,512]{1,0:T(8,128)S(1)} %get-tuple-element.44), channel_id=1, source_target_pairs={{0,1},{1,2},{2,3},{3,4},{4,5},{5,6},{6,7},{7,8},{8,9},{9,10},{10,1... | collective-permute-start | bytes 393224 | tf_op jit(solution)/shard_map/ppermute | solution.py:306
  31.1 1.3 collective-permute-start.5
  33.7 1.9 %all-to-all-done.parts_ref = f32[16,40,128]{2,1,0:T(8,128)S(1)} async-done(((f32[16,40,128]{2,1,0:T(8,128)}), f32[16,40,128]{2,1,0:T(8,128)S(1)}, u32[]{:S(2)}, u32[]{:S(2)}) %all-to-all-start) | async-done | bytes 327712 | tf_op jit(solution)/shard_map/all_to_all | solution.py:302
  36.4 5.4 %all-to-all-start.1 = ((f32[16,4,512]{2,1,0:T(4,128)}), f32[16,4,512]{2,1,0:T(4,128)S(1)}, u32[]{:S(2)}, u32[]{:S(2)}) async-start(f32[16,4,512]{2,1,0:T(4,128)} %broadcast_in_dim.7), calls=%async_computation.1 | async-start | bytes 262144 | tf_op jit(solution)/shard_map/all_to_all | solution.py:314
  42.5 6.1 %all-to-all-done.1 = f32[16,4,512]{2,1,0:T(4,128)S(1)} async-done(((f32[16,4,512]{2,1,0:T(4,128)}), f32[16,4,512]{2,1,0:T(4,128)S(1)}, u32[]{:S(2)}, u32[]{:S(2)}) %all-to-all-start.1) | async-done | bytes 131104 | tf_op jit(solution)/shard_map/all_to_all | solution.py:314
  48.6 1.3 collective-permute-start
  49.9 2.4 %collective-permute-start.1 = (f32[1,64,512]{2,1,0:T(8,128)S(1)}, f32[1,64,512]{2,1,0:T(8,128)S(1)}, u32[]{:S(2)}, u32[]{:S(2)}) collective-permute-start(f32[1,64,512]{2,1,0:T(8,128)S(1)} %reshape.245), channel_id=1, source_target_pairs={{0,64},{16,80},{32,96},{48,112},{64,0},{80,16},{96,32},{112,48},{1... | collective-permute-start | bytes 393224 | tf_op jit(solution)/shard_map/ppermute | solution.py:317
  52.3 1.2 collective-permute-start.2
  53.5 1.6 %fusion.1 = f32[8,64,512]{2,1,0:T(8,128)} fusion(f32[8,64,512]{2,1,0:T(8,128)} %get-tuple-element.39, f32[64,512]{1,0:T(8,128)S(1)} %collective-permute-done.4, f32[512]{0:T(512)S(1)} %bitcast.27), kind=kLoop, calls=%fused_computation.7 | loop fusion | flops 65536 | bytes 395264 | tf_op jit(solution)/shard_map/scatter-add | solution.py:309
  55.1 2.0 %collective-permute-done = f32[1,64,512]{2,1,0:T(8,128)S(1)} collective-permute-done((f32[1,64,512]{2,1,0:T(8,128)S(1)}, f32[1,64,512]{2,1,0:T(8,128)S(1)}, u32[]{:S(2)}, u32[]{:S(2)}) %collective-permute-start) | collective-permute-done | bytes 131104 | tf_op jit(solution)/shard_map/ppermute | solution.py:317
  57.1 6.5 %collective-permute-done.1 = f32[1,64,512]{2,1,0:T(8,128)S(1)} collective-permute-done((f32[1,64,512]{2,1,0:T(8,128)S(1)}, f32[1,64,512]{2,1,0:T(8,128)S(1)}, u32[]{:S(2)}, u32[]{:S(2)}) %collective-permute-start.1) | collective-permute-done | bytes 131104 | tf_op jit(solution)/shard_map/ppermute | solution.py:317
  63.6 4.1 %collective-permute-start.3 = (f32[4,64,512]{2,1,0:T(8,128)S(1)}, f32[4,64,512]{2,1,0:T(8,128)S(1)}, u32[]{:S(2)}, u32[]{:S(2)}) collective-permute-start(f32[4,64,512]{2,1,0:T(8,128)S(1)} %pad_maximum_fusion), channel_id=1, source_target_pairs={{0,16},{16,0},{32,48},{48,32},{64,80},{80,64},{96,112},{112,96},{1... | collective-permute-start | bytes 1572872 | tf_op jit(solution)/shard_map/ppermute | solution.py:321
  67.7 1.6 %fusion = f32[8,64,512]{2,1,0:T(8,128)} fusion(f32[8,64,512]{2,1,0:T(8,128)} %fusion.1, f32[64,512]{1,0:T(8,128)S(1)} %collective-permute-done.5, f32[512]{0:T(512)S(1)} %bitcast.26), kind=kLoop, calls=%fused_computation.5 | loop fusion | flops 65536 | bytes 395264 | tf_op jit(solution)/shard_map/scatter-add | solution.py:310
  69.3 4.2 %all-to-all-start.2 = ((f32[8,64,512]{2,1,0:T(8,128)}), f32[8,64,512]{2,1,0:T(8,128)S(1)}, u32[]{:S(2)}, u32[]{:S(2)}) async-start(f32[8,64,512]{2,1,0:T(8,128)} %fusion), calls=%async_computation.2 | async-start | bytes 2097152 | tf_op jit(solution)/shard_map/all_to_all | solution.py:311
  73.7 26.1 %shard_map.66 = (bf16[512,512]{1,0:T(8,128)(2,1)S(1)}, bf16[512,512]{1,0:T(8,128)(2,1)S(1)}) custom-call(s32[8]{0:T(128)S(1)} %pad_add_fusion.order_ref, f32[8,64,512]{2,1,0:T(8,128)S(1)} %constant_dynamic-update-slice_fusion.seen_ref, f32[1,512]{1,0:T(1,128)S(1)} %bitcast.23, f32[1,512]{1,0:T(1,128)S(1)} %bitcast.22, f32[512,128]{1,0:T(8,128)S(1)} %broadcast_in_dim.8.root_ref), custom_call_target="tpu_custom_call" | custom-call | flops 20000000000 | bytes 2000000 | tf_op jit(solution)/shard_map/pallas_call | solution.py:329
  99.9 2.1 %shard_map.68 = f32[512,512]{1,0:T(8,128)} custom-call(bf16[512,512]{1,0:T(8,128)(2,1)S(1)} %get-tuple-element.36.high_ref, bf16[512,512]{1,0:T(8,128)(2,1)S(1)} %get-tuple-element.37.low_ref, f32[512,512]{1,0:T(8,128)S(1)} %bitcast.21), custom_call_target="tpu_custom_call" | custom-call | tf_op jit(solution)/shard_map/pallas_call | solution.py:343
  102.0 4.8 %all-to-all-start.3 = ((f32[8,64,512]{2,1,0:T(8,128)}), f32[8,64,512]{2,1,0:T(8,128)S(1)}, u32[]{:S(2)}, u32[]{:S(2)}) async-start(f32[8,64,512]{2,1,0:T(8,128)} %bitcast.12), calls=%async_computation.3 | async-start | bytes 2097152 | tf_op jit(solution)/shard_map/all_to_all | solution.py:346
  106.8 5.9 %shard_map.67.inner_ref = f32[64,4096]{1,0:T(8,128)S(1)} custom-call(s32[1]{0:T(128)} %bitcast.place_ref, bf16[512,512]{1,0:T(8,128)(2,1)S(1)} %get-tuple-element.36.high_ref, bf16[512,512]{1,0:T(8,128)(2,1)S(1)} %get-tuple-element.37.low_ref, f32[64,4096]{1,0:T(8,128)} %get-tuple-element.38.own_ref, f32[512,4096]{1,0:T(8,128)} %all-gather.2.cloned.1.call-done.cells_ref), custom_call_target="tpu_custom_call" | custom-call | flops 3000000000 | bytes 10000000 | tf_op jit(solution)/shard_map/pallas_call | solution.py:350
  112.7 9.2 %all-to-all-done.3.outer_ref = f32[8,64,512]{2,1,0:T(8,128)S(1)} async-done(((f32[8,64,512]{2,1,0:T(8,128)}), f32[8,64,512]{2,1,0:T(8,128)S(1)}, u32[]{:S(2)}, u32[]{:S(2)}) %all-to-all-start.3) | async-done | bytes 1048608 | tf_op jit(solution)/shard_map/all_to_all | solution.py:346
  121.9 2.7 %shard_map.69 = f32[1024,512]{1,0:T(8,128)} custom-call(f32[64,4096]{1,0:T(8,128)S(1)} %shard_map.67.inner_ref, f32[8,64,512]{2,1,0:T(8,128)S(1)} %all-to-all-done.3.outer_ref), custom_call_target="tpu_custom_call" | custom-call | tf_op jit(solution)/shard_map/pallas_call | solution.py:367
  (38 shorter events, 4.3 us)
Async XLA Ops:
  6.5 0.7 copy-start
  6.5 100.2 %all-gather.2.cloned.1.call-start = ((), (), s32[]{:S(2)}) async-start(), calls=%async_computation.4 | async-start | bytes 9437184 | tf_op jit(solution)/shard_map/all_gather | solution.py:303
  7.8 1.6 %copy-start.1 = (f32[64,16,512]{2,1,0:T(8,128)S(1)}, f32[64,16,512]{2,1,0:T(8,128)}, u32[]{:S(2)}) copy-start(f32[64,16,512]{2,1,0:T(8,128)} %x_ref.1) | copy-start | bytes 6291460
  9.4 0.9 copy-start.2
  10.3 22.1 %copy-start.3 = (f32[4,128]{1,0:T(4,128)S(1)}, f32[4,128]{1,0:T(4,128)}, u32[]{:S(2)}) copy-start(f32[4,128]{1,0:T(4,128)} %param.14) | copy-start | bytes 6148
  10.3 31.5 %copy-start.4 = (f32[4,128]{1,0:T(4,128)S(1)}, f32[4,128]{1,0:T(4,128)}, u32[]{:S(2)}) copy-start(f32[4,128]{1,0:T(4,128)} %param.13) | copy-start | bytes 6148
  19.2 16.5 %all-to-all-start = ((f32[16,40,128]{2,1,0:T(8,128)}), f32[16,40,128]{2,1,0:T(8,128)S(1)}, u32[]{:S(2)}, u32[]{:S(2)}) async-start(f32[16,40,128]{2,1,0:T(8,128)} %get-tuple-element.35), calls=%async_computation | async-start | bytes 655360 | tf_op jit(solution)/shard_map/all_to_all | solution.py:302
  27.8 25.7 %collective-permute-start.4 = (f32[64,512]{1,0:T(8,128)S(1)}, f32[64,512]{1,0:T(8,128)S(1)}, u32[]{:S(2)}, u32[]{:S(2)}) collective-permute-start(f32[64,512]{1,0:T(8,128)S(1)} %get-tuple-element.44), channel_id=1, source_target_pairs={{0,1},{1,2},{2,3},{3,4},{4,5},{5,6},{6,7},{7,8},{8,9},{9,10},{10,1... | collective-permute-start | bytes 393224 | tf_op jit(solution)/shard_map/ppermute | solution.py:306
  31.1 36.6 %collective-permute-start.5 = (f32[64,512]{1,0:T(8,128)S(1)}, f32[64,512]{1,0:T(8,128)S(1)}, u32[]{:S(2)}, u32[]{:S(2)}) collective-permute-start(f32[64,512]{1,0:T(8,128)S(1)} %get-tuple-element.43), channel_id=1, source_target_pairs={{1,0},{2,1},{3,2},{4,3},{5,4},{6,5},{7,6},{8,7},{9,8},{10,9},{11,1... | collective-permute-start | bytes 393224 | tf_op jit(solution)/shard_map/ppermute | solution.py:307
  36.4 12.2 %all-to-all-start.1 = ((f32[16,4,512]{2,1,0:T(4,128)}), f32[16,4,512]{2,1,0:T(4,128)S(1)}, u32[]{:S(2)}, u32[]{:S(2)}) async-start(f32[16,4,512]{2,1,0:T(4,128)} %broadcast_in_dim.7), calls=%async_computation.1 | async-start | bytes 262144 | tf_op jit(solution)/shard_map/all_to_all | solution.py:314
  48.6 8.5 %collective-permute-start = (f32[1,64,512]{2,1,0:T(8,128)S(1)}, f32[1,64,512]{2,1,0:T(8,128)S(1)}, u32[]{:S(2)}, u32[]{:S(2)}) collective-permute-start(f32[1,64,512]{2,1,0:T(8,128)S(1)} %reshape.245), channel_id=1, source_target_pairs={{0,32},{16,48},{32,64},{48,80},{64,96},{80,112},{96,0},{112,16},{1... | collective-permute-start | bytes 393224 | tf_op jit(solution)/shard_map/ppermute | solution.py:317
  49.9 13.7 %collective-permute-start.1 = (f32[1,64,512]{2,1,0:T(8,128)S(1)}, f32[1,64,512]{2,1,0:T(8,128)S(1)}, u32[]{:S(2)}, u32[]{:S(2)}) collective-permute-start(f32[1,64,512]{2,1,0:T(8,128)S(1)} %reshape.245), channel_id=1, source_target_pairs={{0,64},{16,80},{32,96},{48,112},{64,0},{80,16},{96,32},{112,48},{1... | collective-permute-start | bytes 393224 | tf_op jit(solution)/shard_map/ppermute | solution.py:317
  52.3 11.2 %collective-permute-start.2 = (f32[1,64,512]{2,1,0:T(8,128)S(1)}, f32[1,64,512]{2,1,0:T(8,128)S(1)}, u32[]{:S(2)}, u32[]{:S(2)}) collective-permute-start(f32[1,64,512]{2,1,0:T(8,128)S(1)} %reshape.245), channel_id=1, source_target_pairs={{0,96},{16,112},{32,0},{48,16},{64,32},{80,48},{96,64},{112,80},{1... | collective-permute-start | bytes 393224 | tf_op jit(solution)/shard_map/ppermute | solution.py:317
  63.6 9.9 %collective-permute-start.3 = (f32[4,64,512]{2,1,0:T(8,128)S(1)}, f32[4,64,512]{2,1,0:T(8,128)S(1)}, u32[]{:S(2)}, u32[]{:S(2)}) collective-permute-start(f32[4,64,512]{2,1,0:T(8,128)S(1)} %pad_maximum_fusion), channel_id=1, source_target_pairs={{0,16},{16,0},{32,48},{48,32},{64,80},{80,64},{96,112},{112,96},{1... | collective-permute-start | bytes 1572872 | tf_op jit(solution)/shard_map/ppermute | solution.py:321
  69.3 30.6 %all-to-all-start.2 = ((f32[8,64,512]{2,1,0:T(8,128)}), f32[8,64,512]{2,1,0:T(8,128)S(1)}, u32[]{:S(2)}, u32[]{:S(2)}) async-start(f32[8,64,512]{2,1,0:T(8,128)} %fusion), calls=%async_computation.2 | async-start | bytes 2097152 | tf_op jit(solution)/shard_map/all_to_all | solution.py:311
  102.0 19.9 %all-to-all-start.3 = ((f32[8,64,512]{2,1,0:T(8,128)}), f32[8,64,512]{2,1,0:T(8,128)S(1)}, u32[]{:S(2)}, u32[]{:S(2)}) async-start(f32[8,64,512]{2,1,0:T(8,128)} %bitcast.12), calls=%async_computation.3 | async-start | bytes 2097152 | tf_op jit(solution)/shard_map/all_to_all | solution.py:346
Sparse Core Ops, SparseCore 0:
  19.3 58.8 all-gather.1

commit v3 on v1

v3 whole, which is shorter than its diff:
```python
import functools

import jax
import jax.numpy as jnp
from jax import lax
from jax.experimental import pallas as pl
from jax.experimental.pallas import tpu as pltpu
from jax.sharding import PartitionSpec as P

SAMPLE_TOTAL = 512
NOBS = 128
ALL_OBS = 512
HIGHEST = lax.Precision.HIGHEST
NT = (((1,), (1,)), ((), ()))
TN = (((0,), (0,)), ((), ()))
NN = (((1,), (0,)), ((), ()))
LARGE = 60 * 1024 * 1024
MEDIUM = 20 * 1024 * 1024
SMALL = 8 * 1024 * 1024


def halves(value):
    high = value.astype(jnp.bfloat16)
    low = (value - high.astype(jnp.float32)).astype(jnp.bfloat16)
    return high, low


def dot_split(left, right, dims):
    f32 = jnp.float32
    left_high, left_low = left
    right_high, right_low = right
    small = lax.dot_general(left_low, right_high, dims, preferred_element_type=f32)
    small = small + lax.dot_general(left_high, right_low, dims, preferred_element_type=f32)
    return small + lax.dot_general(left_high, right_high, dims, preferred_element_type=f32)


def dot3(left, right, dims):
    return dot_split(halves(left), halves(right), dims)


def dot6(left, right, dims):
    return lax.dot_general(
        left, right, dims, precision=HIGHEST, preferred_element_type=jnp.float32
    )


def forecast_kernel(order_ref, base_ref, x_ref, weight_ref, cell_ref, piece_ref, own_ref, pick_ref, flat_ref):
    members, rows, width = x_ref.shape
    col_at = lax.broadcasted_iota(jnp.int32, (rows, width), 1)
    row_at = lax.broadcasted_iota(jnp.int32, (rows, width), 0)
    east, west, north, south = [weight_ref[i] for i in range(4)]
    cell = jnp.concatenate([cell_ref[pl.ds(order_ref[j], 1), :] for j in range(order_ref.shape[0])], axis=1)
    at_row = (cell >> 9) - base_ref[0]

    @pl.when(pl.program_id(0) == 0)
    def _():
        at_col = cell & (width - 1)
        pick = lax.broadcasted_iota(jnp.int32, (width, ALL_OBS), 0) == at_col
        pick_ref[...] = pick.astype(jnp.bfloat16)

    def member(m, carry):
        x = x_ref[m]
        to_east = jnp.where(col_at == width - 1, 0.0, pltpu.roll(x, width - 1, 1))
        to_west = jnp.where(col_at == 0, 0.0, pltpu.roll(x, 1, 1))
        to_north = jnp.where(row_at == 0, 0.0, pltpu.roll(x, 1, 0))
        to_south = jnp.where(row_at == rows - 1, 0.0, pltpu.roll(x, rows - 1, 0))
        f = (
            x
            + east * (to_east - x)
            + west * (to_west - x)
            + north * (to_north - x)
            + south * (to_south - x)
        )
        flat_ref[pl.ds(pl.multiple_of(m * rows, rows), rows), :] = f
        for h in range(2):
            for q in range(4):
                piece_ref[4 * h + q, m] = f[8 * h : 8 * h + 8, 128 * q : 128 * q + 128]
        return carry

    lax.fori_loop(0, members, member, 0, unroll=4)
    own_row = (lax.broadcasted_iota(jnp.int32, (rows, ALL_OBS), 0) == at_row).astype(jnp.float32)
    pick = pick_ref[...]
    part = 8
    for g in range(members // part):
        value = flat_ref[g * part * rows : (g + 1) * part * rows, :]
        total = picked(value, pick).reshape(part, rows, ALL_OBS) * own_row[None]
        own_ref[part * g : part * g + part, :] = jnp.sum(total, axis=1)


def picked(value, pick):
    total = None
    for _ in range(3):
        cut = value.astype(jnp.bfloat16)
        value = value - cut.astype(jnp.float32)
        term = lax.dot_general(cut, pick, NN, preferred_element_type=jnp.float32)
        total = term if total is None else total + term
    return total


def halo_kernel(order_ref, base_ref, own_ref, low_ref, high_ref, weight_ref, cell_ref, out_ref):
    members, width = low_ref.shape
    rows = weight_ref.shape[1]
    cell = jnp.concatenate([cell_ref[pl.ds(order_ref[j], 1), :] for j in range(order_ref.shape[0])], axis=1)
    at_row = (cell >> 9) - base_ref[0]
    pick = lax.broadcasted_iota(jnp.int32, (width, ALL_OBS), 0) == (cell & (width - 1))
    edges = [low_ref[...], high_ref[...], weight_ref[2, 0:8, :], weight_ref[3, rows - 8 :, :]]
    edges = picked(jnp.concatenate(edges, axis=0), pick.astype(jnp.bfloat16))
    first = edges[2 * members : 2 * members + 1] * edges[0:members]
    last = edges[2 * members + 15 : 2 * members + 16] * edges[members : 2 * members]
    out_ref[...] = own_ref[...] + jnp.where(at_row == 0, first, 0.0) + jnp.where(at_row == rows - 1, last, 0.0)


def edge_kernel(piece_ref, weight_ref, low_ref, high_ref, out_ref):
    members = low_ref.shape[0]
    rows = weight_ref.shape[1]
    out_ref[...] = piece_ref[...]

    @pl.when(pl.program_id(0) < 4)
    def _():
        at = pl.ds(0, members, stride=8)
        out_ref[at, :] = out_ref[at, :] + weight_ref[2, 0:1, :] * low_ref[...]

    @pl.when(pl.program_id(0) >= 4)
    def _():
        at = pl.ds(7, members, stride=8)
        out_ref[at, :] = out_ref[at, :] + weight_ref[3, rows - 1 : rows, :] * high_ref[...]


def sum_kernel(*refs):
    total = refs[0][...]
    for ref in refs[1:-1]:
        total = total + ref[...]
    refs[-1][...] = total


def over_rows(value, row):
    return jnp.broadcast_to(value[row : row + 1, :], (8, NOBS))


def over_lanes(value, lane):
    return jnp.broadcast_to(value[:, lane : lane + 1], (8, NOBS))


def factor(block, root):
    count = NOBS // 8
    sub = lax.broadcasted_iota(jnp.int32, (8, NOBS), 0)
    lane = lax.broadcasted_iota(jnp.int32, (8, NOBS), 1)
    rows = [block[8 * i : 8 * i + 8, :] for i in range(count)]
    shifted = [(lane == sub + 8 * i).astype(jnp.float32) for i in range(count)]
    inverse = [None] * count
    for b in range(count):
        panel = rows[b]
        column = [over_lanes(panel, 8 * b + k) for k in range(8)]
        done = jnp.zeros((8, NOBS), jnp.float32)
        plus = shifted[b]
        inv_roots = []
        for k in range(8):
            at = 8 * b + k
            pivot = over_rows(column[k], k)
            inv_root = lax.rsqrt(pivot)
            inv = inv_root * inv_root
            inv_roots.append(inv_root)
            row = jnp.where(lane == at, 1.0, over_rows(panel, k))
            done = jnp.where(sub == k, row * inv_root, done)
            scaled = row * inv
            away = jnp.where(sub == k, -1.0, column[k])
            panel = jnp.where((sub == k) | (lane == at), 0.0, panel) - away * scaled
            plus_row = over_rows(plus, k) / (pivot * inv_root + over_rows(root[8 * b : 8 * b + 8, :], k))
            below = jnp.where(sub > k, column[k] * inv_root, 0.0)
            plus = jnp.where(sub == k, plus_row, plus - below * plus_row)
            for j in range(k + 1, 8):
                step = over_rows(column[j], k) * inv
                column[j] = jnp.where(sub == k, 0.0, column[j]) - away * step
        inverse[b] = jnp.where(lane <= sub + 8 * b, done, 0.0)
        shifted[b] = plus
        if b == count - 1:
            break
        for k in reversed(range(8)):
            above = jnp.where(sub < k, over_lanes(done, 8 * b + k), 0.0)
            row = over_rows(plus, k) * inv_roots[k]
            plus = jnp.where(sub == k, row, plus - above * row)
        panel_rows = [over_rows(panel, k) for k in range(8)]
        plus_rows = [over_rows(plus, k) for k in range(8)]
        inside = (lane >= 8 * b) & (lane < 8 * b + 8)
        for r in range(b + 1, count):
            left = [over_lanes(rows[r], 8 * b + k) for k in range(8)]
            new = jnp.where(inside, 0.0, rows[r])
            new_shifted = shifted[r]
            for k in range(8):
                new = new - left[k] * panel_rows[k]
                new_shifted = new_shifted - left[k] * plus_rows[k]
            rows[r] = new
            shifted[r] = new_shifted
    return jnp.concatenate(inverse, axis=0), jnp.concatenate(shifted, axis=0)


def transform_kernel(
    block_ref, me_ref, seen_ref, other_ref, value_ref, var_ref,
    out_ref, cov_ref, state_ref, gain_ref, minus_ref,
):
    n = ALL_OBS
    blocks = n // NOBS
    turns, share = seen_ref.shape[0], seen_ref.shape[1]
    value = jnp.concatenate([value_ref[pl.ds(block_ref[j], 1), :] for j in range(blocks)], axis=1)
    var = jnp.concatenate([var_ref[pl.ds(block_ref[j], 1), :] for j in range(blocks)], axis=1)
    total = seen_ref[0] + other_ref[0]
    for d in range(1, turns):
        total = total + seen_ref[d] + other_ref[d]
    mean = jnp.sum(total, axis=0, keepdims=True) / SAMPLE_TOTAL

    me = me_ref[0]

    def at(turn, other):
        place = (me + 2 * (turns - turn)) & (2 * turns - 1)
        place = place ^ 1 if other else place
        return pl.ds(pl.multiple_of(place * share, share), share)

    for d in range(turns):
        state_ref[at(d, False), :] = seen_ref[d] - mean
        state_ref[at(d, True), :] = other_ref[d] - mean
    state_ref[SAMPLE_TOTAL:, :] = jnp.broadcast_to(value - mean, (8, n))
    anomaly = state_ref[0:SAMPLE_TOTAL, :]
    minus_ref[...] = anomaly
    cov = dot6(anomaly, anomaly, TN) / (SAMPLE_TOTAL - 1)
    eye = lax.broadcasted_iota(jnp.int32, (n, n), 0) == lax.broadcasted_iota(jnp.int32, (n, n), 1)
    cov_ref[...] = cov + jnp.where(eye, var, 0.0)
    for j in range(blocks):
        low, high = NOBS * j, NOBS * (j + 1)
        root = jnp.sqrt(jnp.broadcast_to(var[:, low:high], (NOBS, NOBS))).T
        inv_low, inv_sum = factor(cov_ref[low:high, low:high], root)
        rest = high < n
        if rest:
            below = dot6(cov_ref[high:, low:high], inv_low, NT)
            cov_ref[high:, high:] = cov_ref[high:, high:] - dot6(below, below, NT)
            below = halves(below)
        inv_low, inv_sum = halves(inv_low), halves(inv_sum)
        gain = dot_split(halves(state_ref[:, low:high]), inv_low, NT)
        minus = dot_split(halves(minus_ref[:, low:high]), inv_sum, NT)
        gain_ref[:, low:high] = gain
        if rest:
            state_ref[:, high:] = state_ref[:, high:] - dot_split(halves(gain), below, NT)
            minus_ref[:, high:] = minus_ref[:, high:] - dot_split(halves(minus), below, NT)
        minus_ref[:, low:high] = minus
    mean_step = gain_ref[SAMPLE_TOTAL : SAMPLE_TOTAL + 1, :]
    left = (mean_step - minus_ref[...]) * (1.0 / (SAMPLE_TOTAL - 1))
    total = dot3(left, gain_ref[0:SAMPLE_TOTAL, :], NT)
    out_ref[...] = total


def update_kernel(transform_ref, cells_ref, out_ref):
    transform = halves(transform_ref[...])
    for r in range(0, 8, 2):
        at = [pl.ds(r + i, SAMPLE_TOTAL, stride=8) for i in range(2)]
        field = jnp.concatenate([cells_ref[a, :] for a in at], axis=1)
        new = field + dot_split(transform, halves(field), NN)
        for i in range(2):
            out_ref[at[i], :] = new[:, 128 * i : 128 * i + 128]


def stack_kernel(*refs):
    for i, ref in enumerate(refs[:-1]):
        refs[-1][i] = ref[...]


def join_kernel(parts_ref, out_ref):
    for h in range(2):
        for q in range(4):
            out_ref[:, 8 * h : 8 * h + 8, 128 * q : 128 * q + 128] = parts_ref[4 * h + q]


def call(kernel, out_shape, scratch=(), grid=(), scalars=0, in_specs=None, out_specs=None, flops=0, bytes_accessed=0, limit=MEDIUM):
    specs = {} if in_specs is None else {"in_specs": in_specs, "out_specs": out_specs}
    return pl.pallas_call(
        kernel,
        out_shape=out_shape,
        grid_spec=pltpu.PrefetchScalarGridSpec(
            num_scalar_prefetch=scalars, grid=grid, scratch_shapes=list(scratch), **specs
        ),
        compiler_params=pltpu.CompilerParams(vmem_limit_bytes=limit),
        cost_estimate=pl.CostEstimate(flops=flops, bytes_accessed=bytes_accessed, transcendentals=0),
    )


def spec(shape, *axes):
    places = tuple(axes) + (None,) * (len(shape) - len(axes))
    return pl.BlockSpec(shape, lambda i, *scalars: tuple(0 if p is None else i for p in places))


def body(prior_samples, neighbour_weights, obs_cell, obs_value, obs_var, block_order):
    f32 = jnp.float32
    members, rows, width = prior_samples.shape
    mem_count, cell_count = lax.axis_size("mem"), lax.axis_size("cell")
    me = lax.axis_index("mem")
    base = (lax.axis_index("cell") * rows).reshape(1)
    shape = jax.ShapeDtypeStruct
    steps = 4
    step = members // steps
    side = 4
    forward = [(i, i + 1) for i in range(cell_count - 1)]
    backward = [(i + 1, i) for i in range(cell_count - 1)]
    swap = [(i, i ^ 1) for i in range(mem_count)]

    def along_x(value, d):
        return lax.ppermute(value, "mem", [(i, (i + 2 * d) % mem_count) for i in range(mem_count)])

    near, far = [1, 0, 3, 2], [3, 2, 1, 0]
    z_near, z_far = [[(i, i // side * side + p[i % side]) for i in range(cell_count)] for p in (near, far)]
    y_near, y_far = [[(i, p[i // side] * side + i % side) for i in range(cell_count)] for p in (near, far)]

    low = lax.ppermute(prior_samples[:, rows - 1, :], "cell", forward)
    high = lax.ppermute(prior_samples[:, 0, :], "cell", backward)
    smem = pl.BlockSpec(memory_space=pltpu.SMEM)
    seen_shape = shape((members, ALL_OBS), f32)
    pieces, seen = call(
        forecast_kernel,
        (shape((mem_count, members, 8, 128), f32), seen_shape),
        [
            pltpu.VMEM((width, ALL_OBS), jnp.bfloat16),
            pltpu.VMEM((step * rows, width), f32),
        ],
        grid=(steps,),
        in_specs=[
            smem,
            smem,
            spec((step, rows, width), 0),
            spec((4, rows, width)),
            spec(obs_cell.shape),
        ],
        out_specs=[spec((mem_count, step, 8, 128), None, 0), spec((step, ALL_OBS), 0)],
        flops=2_000_000_000,
        bytes_accessed=4_000_000,
        limit=LARGE,
    )(block_order, base, prior_samples, neighbour_weights, obs_cell)
    seen = call(
        halo_kernel,
        seen_shape,
        in_specs=[smem, smem] + [pl.BlockSpec(memory_space=pltpu.VMEM)] * 5,
        out_specs=pl.BlockSpec(memory_space=pltpu.VMEM),
        limit=SMALL,
    )(block_order, base, seen, low, high, neighbour_weights, obs_cell)

    for pairs in (z_near, z_far, y_near, y_far):
        seen = call(sum_kernel, seen_shape, limit=SMALL)(seen, lax.ppermute(seen, "cell", pairs))
    lanes = pl.BlockSpec((members, 128), lambda i: (0, i % 4))
    tiles = spec((members * 8, 128), 0)
    pieces = pl.pallas_call(
        edge_kernel,
        out_shape=shape((mem_count * members * 8, 128), f32),
        grid=(mem_count,),
        in_specs=[tiles, pl.BlockSpec((4, rows, 128), lambda i: (0, 0, i % 4)), lanes, lanes],
        out_specs=tiles,
        input_output_aliases={0: 0},
        compiler_params=pltpu.CompilerParams(vmem_limit_bytes=SMALL),
    )(pieces.reshape(mem_count * members * 8, 128), neighbour_weights, low, high)
    pieces = pieces.reshape(mem_count, members, 8, 128)
    one, two, three = along_x(seen, 1), along_x(seen, 2), along_x(seen, 3)
    one, two, three, pieces = lax.optimization_barrier((one, two, three, pieces))
    cells = lax.all_to_all(pieces, "mem", 0, 0)
    seen = call(stack_kernel, shape((4, members, ALL_OBS), f32), limit=SMALL)(seen, one, two, three)
    other = lax.ppermute(seen, "mem", swap)

    square = (ALL_OBS, ALL_OBS)
    whole = pl.BlockSpec(memory_space=pltpu.VMEM)
    transform = call(
        transform_kernel,
        shape(square, f32),
        [
            pltpu.VMEM(square, f32),
            pltpu.VMEM((SAMPLE_TOTAL + 8, ALL_OBS), f32),
            pltpu.VMEM((SAMPLE_TOTAL + 8, ALL_OBS), f32),
            pltpu.VMEM(square, f32),
        ],
        scalars=2,
        in_specs=[whole] * 4,
        out_specs=whole,
        flops=20_000_000_000,
        bytes_accessed=2_000_000,
    )(block_order, me.reshape(1), seen, other, obs_value, obs_var)

    cells = cells.reshape(SAMPLE_TOTAL * 8, 128)
    new = call(update_kernel, shape(cells.shape, f32), flops=3_000_000_000, bytes_accessed=4_000_000)(
        transform, cells
    )
    new = lax.all_to_all(new.reshape(mem_count, members, 8, 128), "mem", 0, 0)
    return call(
        join_kernel,
        shape(prior_samples.shape, f32),
        grid=(4,),
        in_specs=[spec((mem_count, step, 8, 128), None, 0)],
        out_specs=spec((step, rows, width), 0),
        bytes_accessed=4_000_000,
    )(new)


def solution(mesh):
    return jax.shard_map(
        body,
        mesh=mesh,
        in_specs=(P("mem", "cell", None), P(None, "cell", None), P(), P(), P(), P()),
        out_specs=P("mem", "cell", None),
        check_vma=False,
    )
```

time: 140 us -> 122 us (0.87)
  blocking collectives: 57.9 us -> 30.8 us
  Pallas kernels: 32.6 us -> 44.2 us
  starting transfers between devices: 19.6 us -> 31 us
  local copies, waits for them, and re-layouts: 13.9 us -> 4.94 us
  waiting for transfers between devices: 14.8 us -> 9.89 us
    all_to_all x3 -> x1, blocking collectives: 57.9 us -> 30.8 us  [body(): new = lax.all_to_all(new.reshape(mem_count, members, 8, 128), 'mem', 0, 0)]
    ppermute x2 -> x10, starting transfers between devices: 6.3 us -> 27.2 us  [the longest x4 11.1 us: body(): lax.ppermute(seen, 'cell', pairs)]
    all_to_all x1 -> x0, waiting for transfers between devices: 14 us -> none  [body(): lax.all_to_all(jnp.broadcast_to(seen[None], (mem_count,) + seen.shape), '...]
    pallas_call x3 -> x11, Pallas kernels: 32.6 us -> 44.2 us  [the longest x1 26.3 us: body(): call(transform_kernel, shape(square, f32), [pltpu.VMEM(square, f32), pltp...]
    ppermute x2 -> x10, waiting for transfers between devices: 0.84 us -> 9.89 us  [the longest x4 9.87 us: body(): lax.ppermute(seen, 'cell', pairs)]
    all_to_all x1 -> x0, starting transfers between devices: 8.97 us -> none  [body(): lax.all_to_all(jnp.broadcast_to(seen[None], (mem_count,) + seen.shape), '...]
    unnamed x20 -> x18, local copies, waits for them, and re-layouts: 7.49 us -> 3.15 us
    gather x3 -> x0, local copies, waits for them, and re-layouts: 1.68 us -> none  [the longest x1 0.56 us: body(): cell = obs_cell[block_order].reshape(1, ALL_OBS)]
  transfers between devices with their start and end apart: 4 -> 11, of which waited for: 2 -> 4; matrix products, arithmetic and copies ran while one was open for 2% -> 0% of each run, Pallas kernels for 18% -> 32%
where the time goes in v3:
time: 122 us; the launch traced here: 121 us
  Pallas kernels  44.2 us (36%)
  starting transfers between devices  31 us (25%)
  blocking collectives  30.8 us (25%)
  waiting for transfers between devices  9.89 us (8%)
  local copies, waits for them, and re-layouts  4.94 us (4%)
    all_to_all x1, blocking collectives, body(): new = lax.all_to_all(new.reshape(mem_count, members, 8, 128), 'mem', 0, 0)  30.8 us
    pallas_call x1, Pallas kernels, body(): call(transform_kernel, shape(square, f32), [pltpu.VMEM(square, f32), pltp...  26.3 us
    ppermute x4, starting transfers between devices, body(): lax.ppermute(seen, 'cell', pairs)  11.1 us
    ppermute x4, waiting for transfers between devices, body(): lax.ppermute(seen, 'cell', pairs)  9.87 us
    pallas_call x1, Pallas kernels, body(): call(forecast_kernel, (shape((mem_count, members, 8, 128), f32), seen_sha...  7.04 us
    ppermute x1, starting transfers between devices, body(): other = lax.ppermute(seen, 'mem', swap)  6.68 us
    pallas_call x1, Pallas kernels, body(): pl.pallas_call(edge_kernel, out_shape=shape((mem_count * members * 8, 128...  5.69 us
    ppermute x1, starting transfers between devices, body(): low = lax.ppermute(prior_samples[:, rows - 1, :], 'cell', forward)  4.38 us
  transfers between devices with their start and end apart: 11, of which 4 were waited for; matrix products, arithmetic and copies ran while one was open for 0% of the time, Pallas kernels for 32%

profile of v3, /device:TPU:1, one launch (start us, length us, event | category | flops | bytes accessed | tf_op | source)
XLA Modules:
  0.0 121.1 jit_solution(13567384230121037109)
XLA Ops:
  0.0 1.8 %fusion = (f32[64,1,512]{2,1,0:T(1,128)S(1)}, f32[64,1,512]{2,1,0:T(1,128)S(1)}) fusion(f32[64,16,512]{2,1,0:T(8,128)} %x_ref.1), kind=kLoop, calls=%fused_computation.2 | loop fusion | bytes 524288 | tf_op jit(solution)/shard_map/slice | solution.py:311
  1.8 4.4 %collective-permute-start = (f32[64,512]{1,0:T(8,128)S(1)}, f32[64,512]{1,0:T(8,128)S(1)}, u32[]{:S(2)}, u32[]{:S(2)}) collective-permute-start(f32[64,512]{1,0:T(8,128)S(1)} %bitcast.14), channel_id=1, source_target_pairs={{0,1},{1,2},{2,3},{3,4},{4,5},{5,6},{6,7},{7,8},{8,9},{9,10},{10,1... | collective-permute-start | bytes 393224 | tf_op jit(solution)/shard_map/ppermute | solution.py:310
  6.2 1.3 %collective-permute-start.1 = (f32[64,512]{1,0:T(8,128)S(1)}, f32[64,512]{1,0:T(8,128)S(1)}, u32[]{:S(2)}, u32[]{:S(2)}) collective-permute-start(f32[64,512]{1,0:T(8,128)S(1)} %bitcast.15), channel_id=1, source_target_pairs={{1,0},{2,1},{3,2},{4,3},{5,4},{6,5},{7,6},{8,7},{9,8},{10,9},{11,1... | collective-permute-start | bytes 393224 | tf_op jit(solution)/shard_map/ppermute | solution.py:311
  7.6 7.0 %shard_map.64 = (f32[8,64,8,128]{3,2,1,0:T(8,128)}, f32[64,512]{1,0:T(8,128)}) custom-call(s32[4]{0:T(128)} %block_ref.1, s32[1]{0:T(128)} %bitcast.1.base_ref, f32[64,16,512]{2,1,0:T(8,128)} %x_ref.1, f32[4,16,512]{2,1,0:T(8,128)} %weight_ref.5, s32[4,128]{1,0:T(4,128)} %cell_ref.3), custom_call_target="tpu_custom_call" | custom-call | flops 2000000000 | bytes 4000000 | tf_op jit(solution)/shard_map/pallas_call | solution.py:314
  14.7 0.9 copy-done.1
  15.6 1.0 shard_map.65.refs_0_
  16.6 2.4 %collective-permute-start.2 = (f32[64,512]{1,0:T(8,128)S(1)}, f32[64,512]{1,0:T(8,128)S(1)}, u32[]{:S(2)}, u32[]{:S(2)}) collective-permute-start(f32[64,512]{1,0:T(8,128)S(1)} %shard_map.65.refs_0_), channel_id=1, source_target_pairs={{0,1},{1,0},{2,3},{3,2},{4,5},{5,4},{6,7},{7,6},{8,9},{9,8},{10,11... | collective-permute-start | bytes 393224 | tf_op jit(solution)/shard_map/ppermute | solution.py:343
  18.9 2.8 %collective-permute-done.2.refs_1_ = f32[64,512]{1,0:T(8,128)S(1)} collective-permute-done((f32[64,512]{1,0:T(8,128)S(1)}, f32[64,512]{1,0:T(8,128)S(1)}, u32[]{:S(2)}, u32[]{:S(2)}) %collective-permute-start.2) | collective-permute-done | bytes 131104 | tf_op jit(solution)/shard_map/ppermute | solution.py:343
  21.7 3.0 %collective-permute-start.3 = (f32[64,512]{1,0:T(8,128)S(1)}, f32[64,512]{1,0:T(8,128)S(1)}, u32[]{:S(2)}, u32[]{:S(2)}) collective-permute-start(f32[64,512]{1,0:T(8,128)S(1)} %shard_map.66.refs_0_), channel_id=1, source_target_pairs={{0,3},{1,2},{2,1},{3,0},{4,7},{5,6},{6,5},{7,4},{8,11},{9,10},{10,... | collective-permute-start | bytes 393224 | tf_op jit(solution)/shard_map/ppermute | solution.py:343
  24.8 2.4 %collective-permute-done.3.refs_1_ = f32[64,512]{1,0:T(8,128)S(1)} collective-permute-done((f32[64,512]{1,0:T(8,128)S(1)}, f32[64,512]{1,0:T(8,128)S(1)}, u32[]{:S(2)}, u32[]{:S(2)}) %collective-permute-start.3) | collective-permute-done | bytes 131104 | tf_op jit(solution)/shard_map/ppermute | solution.py:343
  27.1 2.5 %collective-permute-start.4 = (f32[64,512]{1,0:T(8,128)S(1)}, f32[64,512]{1,0:T(8,128)S(1)}, u32[]{:S(2)}, u32[]{:S(2)}) collective-permute-start(f32[64,512]{1,0:T(8,128)S(1)} %shard_map.67.refs_0_), channel_id=1, source_target_pairs={{0,4},{1,5},{2,6},{3,7},{4,0},{5,1},{6,2},{7,3},{8,12},{9,13},{10,... | collective-permute-start | bytes 393224 | tf_op jit(solution)/shard_map/ppermute | solution.py:343
  29.6 2.4 %collective-permute-done.4.refs_1_ = f32[64,512]{1,0:T(8,128)S(1)} collective-permute-done((f32[64,512]{1,0:T(8,128)S(1)}, f32[64,512]{1,0:T(8,128)S(1)}, u32[]{:S(2)}, u32[]{:S(2)}) %collective-permute-start.4) | collective-permute-done | bytes 131104 | tf_op jit(solution)/shard_map/ppermute | solution.py:343
  32.0 3.3 %collective-permute-start.5 = (f32[64,512]{1,0:T(8,128)S(1)}, f32[64,512]{1,0:T(8,128)S(1)}, u32[]{:S(2)}, u32[]{:S(2)}) collective-permute-start(f32[64,512]{1,0:T(8,128)S(1)} %shard_map.68.refs_0_), channel_id=1, source_target_pairs={{0,12},{1,13},{2,14},{3,15},{4,8},{5,9},{6,10},{7,11},{8,4},{9,5},... | collective-permute-start | bytes 393224 | tf_op jit(solution)/shard_map/ppermute | solution.py:343
  35.3 2.4 %collective-permute-done.5.refs_1_ = f32[64,512]{1,0:T(8,128)S(1)} collective-permute-done((f32[64,512]{1,0:T(8,128)S(1)}, f32[64,512]{1,0:T(8,128)S(1)}, u32[]{:S(2)}, u32[]{:S(2)}) %collective-permute-start.5) | collective-permute-done | bytes 131104 | tf_op jit(solution)/shard_map/ppermute | solution.py:343
  37.6 2.5 %collective-permute-start.8 = (f32[64,512]{1,0:T(8,128)S(1)}, f32[64,512]{1,0:T(8,128)S(1)}, u32[]{:S(2)}, u32[]{:S(2)}) collective-permute-start(f32[64,512]{1,0:T(8,128)S(1)} %shard_map.69.refs_0_), channel_id=1, source_target_pairs={{0,96},{16,112},{32,0},{48,16},{64,32},{80,48},{96,64},{112,80},{1... | collective-permute-start | bytes 393224 | tf_op jit(solution)/shard_map/ppermute | solution.py:304
  41.3 5.7 %shard_map.70 = f32[4096,128]{1,0:T(8,128)} custom-call(f32[4096,128]{1,0:T(8,128)} %bitcast.4.piece_ref, f32[4,16,512]{2,1,0:T(8,128)S(1)} %copy-done, f32[64,512]{1,0:T(8,128)S(1)} %collective-permute-done.low_ref, f32[64,512]{1,0:T(8,128)S(1)} %collective-permute-done.1.high_ref), custom_call_target="tpu_custom_call", output_to_operand_aliasing={{}: (0, {})} | custom-call | tf_op jit(solution)/shard_map/pallas_call | solution.py:346
  47.1 6.7 %collective-permute-start.9 = (f32[4,64,512]{2,1,0:T(8,128)S(1)}, f32[4,64,512]{2,1,0:T(8,128)S(1)}, u32[]{:S(2)}, u32[]{:S(2)}) collective-permute-start(f32[4,64,512]{2,1,0:T(8,128)S(1)} %shard_map.71.seen_ref), channel_id=1, source_target_pairs={{0,16},{16,0},{32,48},{48,32},{64,80},{80,64},{96,112},{112,96},{1... | collective-permute-start | bytes 1572872 | tf_op jit(solution)/shard_map/ppermute | solution.py:360
  53.8 3.9 %all-to-all-start = ((f32[8,64,8,128]{3,2,1,0:T(8,128)}), f32[8,64,8,128]{3,2,1,0:T(8,128)S(1)}, u32[]{:S(2)}, u32[]{:S(2)}) async-start(f32[8,64,8,128]{3,2,1,0:T(8,128)} %bitcast.5), calls=%async_computation | async-start | bytes 4194304 | tf_op jit(solution)/shard_map/all_to_all | solution.py:358
  57.7 26.3 %shard_map.72.transform_ref = f32[512,512]{1,0:T(8,128)S(1)} custom-call(s32[4]{0:T(128)S(1)} %copy-done.3, s32[1]{0:T(128)} %bitcast.me_ref, f32[4,64,512]{2,1,0:T(8,128)S(1)} %shard_map.71.seen_ref, f32[4,64,512]{2,1,0:T(8,128)S(1)} %collective-permute-done.9.other_ref, f32[4,128]{1,0:T(4,128)S(1)} %copy-done.4, f32[4,128]{1,0:T(4,128)S(1)} %copy-done.5), custom_call_target="tpu_custom_call" | custom-call | flops 20000000000 | bytes 2000000 | tf_op jit(solution)/shard_map/pallas_call | solution.py:364
  84.0 1.0 copy-done.6
  85.0 1.2 %copy-done.7 = f32[512,512]{1,0:T(8,128)S(1)} copy-done((f32[512,512]{1,0:T(8,128)S(1)}, f32[512,512]{1,0:T(8,128)}, u32[]{:S(2)}) %copy-start.7) | copy-done | bytes 1048600
  86.2 2.1 %shard_map.73 = f32[4096,128]{1,0:T(8,128)S(1)} custom-call(f32[512,512]{1,0:T(8,128)S(1)} %copy-done.7, f32[4096,128]{1,0:T(8,128)S(1)} %bitcast.12), custom_call_target="tpu_custom_call" | custom-call | flops 3000000000 | bytes 4000000 | tf_op jit(solution)/shard_map/pallas_call | solution.py:381
  88.3 30.8 %all_to_all.10.parts_ref = f32[8,64,8,128]{3,2,1,0:T(8,128)S(1)} all-to-all(f32[8,64,8,128]{3,2,1,0:T(8,128)S(1)} %bitcast.13), channel_id=1, replica_groups=mesh['mem'=8,'cell'=16] {'mem'}, dimensions={0} | all-to-all | bytes 4194304 | tf_op jit(solution)/shard_map/all_to_all | solution.py:384
  119.1 2.0 %shard_map.74 = f32[64,16,512]{2,1,0:T(8,128)} custom-call(f32[8,64,8,128]{3,2,1,0:T(8,128)S(1)} %all_to_all.10.parts_ref), custom_call_target="tpu_custom_call" | custom-call | bytes 4000000 | tf_op jit(solution)/shard_map/pallas_call | solution.py:385
  (29 shorter events, 1.3 us)
Async XLA Ops:
  1.8 12.8 %collective-permute-start = (f32[64,512]{1,0:T(8,128)S(1)}, f32[64,512]{1,0:T(8,128)S(1)}, u32[]{:S(2)}, u32[]{:S(2)}) collective-permute-start(f32[64,512]{1,0:T(8,128)S(1)} %bitcast.14), channel_id=1, source_target_pairs={{0,1},{1,2},{2,3},{3,4},{4,5},{5,6},{6,7},{7,8},{8,9},{9,10},{10,1... | collective-permute-start | bytes 393224 | tf_op jit(solution)/shard_map/ppermute | solution.py:310
  6.2 8.4 %collective-permute-start.1 = (f32[64,512]{1,0:T(8,128)S(1)}, f32[64,512]{1,0:T(8,128)S(1)}, u32[]{:S(2)}, u32[]{:S(2)}) collective-permute-start(f32[64,512]{1,0:T(8,128)S(1)} %bitcast.15), channel_id=1, source_target_pairs={{1,0},{2,1},{3,2},{4,3},{5,4},{6,5},{7,6},{8,7},{9,8},{10,9},{11,1... | collective-permute-start | bytes 393224 | tf_op jit(solution)/shard_map/ppermute | solution.py:311
  7.5 7.1 %copy-start = (f32[4,16,512]{2,1,0:T(8,128)S(1)}, f32[4,16,512]{2,1,0:T(8,128)}, u32[]{:S(2)}) copy-start(f32[4,16,512]{2,1,0:T(8,128)} %weight_ref.5) | copy-start | bytes 393220
  7.5 7.1 %copy-start.2 = (s32[4,128]{1,0:T(4,128)S(1)}, s32[4,128]{1,0:T(4,128)}, u32[]{:S(2)}) copy-start(s32[4,128]{1,0:T(4,128)} %cell_ref.3) | copy-start | bytes 6148
  7.5 7.1 %copy-start.3 = (s32[4]{0:T(128)S(1)}, s32[4]{0:T(128)}, u32[]{:S(2)}) copy-start(s32[4]{0:T(128)} %block_ref.1) | copy-start | bytes 52
  14.6 0.9 copy-start.1
  16.6 5.2 %collective-permute-start.2 = (f32[64,512]{1,0:T(8,128)S(1)}, f32[64,512]{1,0:T(8,128)S(1)}, u32[]{:S(2)}, u32[]{:S(2)}) collective-permute-start(f32[64,512]{1,0:T(8,128)S(1)} %shard_map.65.refs_0_), channel_id=1, source_target_pairs={{0,1},{1,0},{2,3},{3,2},{4,5},{5,4},{6,7},{7,6},{8,9},{9,8},{10,11... | collective-permute-start | bytes 393224 | tf_op jit(solution)/shard_map/ppermute | solution.py:343
  21.7 5.4 %collective-permute-start.3 = (f32[64,512]{1,0:T(8,128)S(1)}, f32[64,512]{1,0:T(8,128)S(1)}, u32[]{:S(2)}, u32[]{:S(2)}) collective-permute-start(f32[64,512]{1,0:T(8,128)S(1)} %shard_map.66.refs_0_), channel_id=1, source_target_pairs={{0,3},{1,2},{2,1},{3,0},{4,7},{5,6},{6,5},{7,4},{8,11},{9,10},{10,... | collective-permute-start | bytes 393224 | tf_op jit(solution)/shard_map/ppermute | solution.py:343
  27.1 4.8 %collective-permute-start.4 = (f32[64,512]{1,0:T(8,128)S(1)}, f32[64,512]{1,0:T(8,128)S(1)}, u32[]{:S(2)}, u32[]{:S(2)}) collective-permute-start(f32[64,512]{1,0:T(8,128)S(1)} %shard_map.67.refs_0_), channel_id=1, source_target_pairs={{0,4},{1,5},{2,6},{3,7},{4,0},{5,1},{6,2},{7,3},{8,12},{9,13},{10,... | collective-permute-start | bytes 393224 | tf_op jit(solution)/shard_map/ppermute | solution.py:343
  32.0 5.6 %collective-permute-start.5 = (f32[64,512]{1,0:T(8,128)S(1)}, f32[64,512]{1,0:T(8,128)S(1)}, u32[]{:S(2)}, u32[]{:S(2)}) collective-permute-start(f32[64,512]{1,0:T(8,128)S(1)} %shard_map.68.refs_0_), channel_id=1, source_target_pairs={{0,12},{1,13},{2,14},{3,15},{4,8},{5,9},{6,10},{7,11},{8,4},{9,5},... | collective-permute-start | bytes 393224 | tf_op jit(solution)/shard_map/ppermute | solution.py:343
  37.6 9.4 %collective-permute-start.8 = (f32[64,512]{1,0:T(8,128)S(1)}, f32[64,512]{1,0:T(8,128)S(1)}, u32[]{:S(2)}, u32[]{:S(2)}) collective-permute-start(f32[64,512]{1,0:T(8,128)S(1)} %shard_map.69.refs_0_), channel_id=1, source_target_pairs={{0,96},{16,112},{32,0},{48,16},{64,32},{80,48},{96,64},{112,80},{1... | collective-permute-start | bytes 393224 | tf_op jit(solution)/shard_map/ppermute | solution.py:304
  40.2 6.8 %collective-permute-start.7 = (f32[64,512]{1,0:T(8,128)S(1)}, f32[64,512]{1,0:T(8,128)S(1)}, u32[]{:S(2)}, u32[]{:S(2)}) collective-permute-start(f32[64,512]{1,0:T(8,128)S(1)} %shard_map.69.refs_0_), channel_id=1, source_target_pairs={{0,64},{16,80},{32,96},{48,112},{64,0},{80,16},{96,32},{112,48},{1... | collective-permute-start | bytes 393224 | tf_op jit(solution)/shard_map/ppermute | solution.py:304
  40.7 6.3 %collective-permute-start.6 = (f32[64,512]{1,0:T(8,128)S(1)}, f32[64,512]{1,0:T(8,128)S(1)}, u32[]{:S(2)}, u32[]{:S(2)}) collective-permute-start(f32[64,512]{1,0:T(8,128)S(1)} %shard_map.69.refs_0_), channel_id=1, source_target_pairs={{0,32},{16,48},{32,64},{48,80},{64,96},{80,112},{96,0},{112,16},{1... | collective-permute-start | bytes 393224 | tf_op jit(solution)/shard_map/ppermute | solution.py:304
  47.1 10.6 %collective-permute-start.9 = (f32[4,64,512]{2,1,0:T(8,128)S(1)}, f32[4,64,512]{2,1,0:T(8,128)S(1)}, u32[]{:S(2)}, u32[]{:S(2)}) collective-permute-start(f32[4,64,512]{2,1,0:T(8,128)S(1)} %shard_map.71.seen_ref), channel_id=1, source_target_pairs={{0,16},{16,0},{32,48},{48,32},{64,80},{80,64},{96,112},{112,96},{1... | collective-permute-start | bytes 1572872 | tf_op jit(solution)/shard_map/ppermute | solution.py:360
  53.7 3.9 %copy-start.4 = (f32[4,128]{1,0:T(4,128)S(1)}, f32[4,128]{1,0:T(4,128)}, u32[]{:S(2)}) copy-start(f32[4,128]{1,0:T(4,128)} %value_ref.1) | copy-start | bytes 6148
  53.7 3.9 %copy-start.5 = (f32[4,128]{1,0:T(4,128)S(1)}, f32[4,128]{1,0:T(4,128)}, u32[]{:S(2)}) copy-start(f32[4,128]{1,0:T(4,128)} %var_ref.1) | copy-start | bytes 6148
  53.8 31.2 %all-to-all-start = ((f32[8,64,8,128]{3,2,1,0:T(8,128)}), f32[8,64,8,128]{3,2,1,0:T(8,128)S(1)}, u32[]{:S(2)}, u32[]{:S(2)}) async-start(f32[8,64,8,128]{3,2,1,0:T(8,128)} %bitcast.5), calls=%async_computation | async-start | bytes 4194304 | tf_op jit(solution)/shard_map/all_to_all | solution.py:358
  84.0 1.0 copy-start.6
  85.0 1.2 %copy-start.7 = (f32[512,512]{1,0:T(8,128)S(1)}, f32[512,512]{1,0:T(8,128)}, u32[]{:S(2)}) copy-start(f32[512,512]{1,0:T(8,128)} %copy-done.6) | copy-start | bytes 3145732

commit v4 on v3

--- a/solution.py
+++ b/solution.py
@@ -113,17 +113,18 @@
 def edge_kernel(piece_ref, weight_ref, low_ref, high_ref, out_ref):
     members = low_ref.shape[0]
     rows = weight_ref.shape[1]
+    upper = pl.program_id(0) == 0
     out_ref[...] = piece_ref[...]
-
-    @pl.when(pl.program_id(0) < 4)
-    def _():
-        at = pl.ds(0, members, stride=8)
-        out_ref[at, :] = out_ref[at, :] + weight_ref[2, 0:1, :] * low_ref[...]
-
-    @pl.when(pl.program_id(0) >= 4)
-    def _():
-        at = pl.ds(7, members, stride=8)
-        out_ref[at, :] = out_ref[at, :] + weight_ref[3, rows - 1 : rows, :] * high_ref[...]
+    weight = jnp.where(upper, weight_ref[2, 0:1, :], weight_ref[3, rows - 1 : rows, :])
+    change = weight * jnp.where(upper, low_ref[...], high_ref[...])
+
+    def add(first):
+        for q in range(4):
+            at = pl.ds(members * 8 * q + first, members, stride=8)
+            out_ref[at, :] = out_ref[at, :] + change[:, 128 * q : 128 * q + 128]
+
+    pl.when(upper)(lambda: add(0))
+    pl.when(jnp.logical_not(upper))(lambda: add(7))
 
 
 def sum_kernel(*refs):
@@ -158,19 +159,18 @@
             at = 8 * b + k
             pivot = over_rows(column[k], k)
             inv_root = lax.rsqrt(pivot)
-            inv = inv_root * inv_root
+            inv = pl.reciprocal(pivot)
             inv_roots.append(inv_root)
             row = jnp.where(lane == at, 1.0, over_rows(panel, k))
             done = jnp.where(sub == k, row * inv_root, done)
-            scaled = row * inv
             away = jnp.where(sub == k, -1.0, column[k])
-            panel = jnp.where((sub == k) | (lane == at), 0.0, panel) - away * scaled
+            panel = jnp.where((sub == k) | (lane == at), 0.0, panel) - (away * row) * inv
             plus_row = over_rows(plus, k) / (pivot * inv_root + over_rows(root[8 * b : 8 * b + 8, :], k))
             below = jnp.where(sub > k, column[k] * inv_root, 0.0)
             plus = jnp.where(sub == k, plus_row, plus - below * plus_row)
             for j in range(k + 1, 8):
-                step = over_rows(column[j], k) * inv
-                column[j] = jnp.where(sub == k, 0.0, column[j]) - away * step
+                step = away * over_rows(column[j], k)
+                column[j] = jnp.where(sub == k, 0.0, column[j]) - step * inv
         inverse[b] = jnp.where(lane <= sub + 8 * b, done, 0.0)
         shifted[b] = plus
         if b == count - 1:
@@ -221,9 +221,13 @@
     state_ref[SAMPLE_TOTAL:, :] = jnp.broadcast_to(value - mean, (8, n))
     anomaly = state_ref[0:SAMPLE_TOTAL, :]
     minus_ref[...] = anomaly
-    cov = dot6(anomaly, anomaly, TN) / (SAMPLE_TOTAL - 1)
-    eye = lax.broadcasted_iota(jnp.int32, (n, n), 0) == lax.broadcasted_iota(jnp.int32, (n, n), 1)
-    cov_ref[...] = cov + jnp.where(eye, var, 0.0)
+    eye = lax.broadcasted_iota(jnp.int32, (NOBS, NOBS), 0) == lax.broadcasted_iota(jnp.int32, (NOBS, NOBS), 1)
+    for j in range(blocks):
+        low, high = NOBS * j, NOBS * (j + 1)
+        cov = dot6(anomaly[:, low:], anomaly[:, low:high], TN) / (SAMPLE_TOTAL - 1)
+        cov_ref[low:high, low:high] = cov[:NOBS] + jnp.where(eye, var[:, low:high], 0.0)
+        if high < n:
+            cov_ref[high:, low:high] = cov[NOBS:]
     for j in range(blocks):
         low, high = NOBS * j, NOBS * (j + 1)
         root = jnp.sqrt(jnp.broadcast_to(var[:, low:high], (NOBS, NOBS))).T
@@ -231,7 +235,9 @@
         rest = high < n
         if rest:
             below = dot6(cov_ref[high:, low:high], inv_low, NT)
-            cov_ref[high:, high:] = cov_ref[high:, high:] - dot6(below, below, NT)
+            for at in range(high, n, NOBS):
+                change = dot6(below[at - high :], below[at - high : at - high + NOBS], NT)
+                cov_ref[at:, at : at + NOBS] = cov_ref[at:, at : at + NOBS] - change
             below = halves(below)
         inv_low, inv_sum = halves(inv_low), halves(inv_sum)
         gain = dot_split(halves(state_ref[:, low:high]), inv_low, NT)
@@ -303,9 +309,17 @@
     def along_x(value, d):
         return lax.ppermute(value, "mem", [(i, (i + 2 * d) % mem_count) for i in range(mem_count)])
 
-    near, far = [1, 0, 3, 2], [3, 2, 1, 0]
-    z_near, z_far = [[(i, i // side * side + p[i % side]) for i in range(cell_count)] for p in (near, far)]
-    y_near, y_far = [[(i, p[i // side] * side + i % side) for i in range(cell_count)] for p in (near, far)]
+    def ring(value, phase, d):
+        def target(m, i):
+            z, y = i % side, i // side
+            if (m + phase) % 2 == 0:
+                z = (z + d) % side
+            else:
+                y = (y + d) % side
+            return m * cell_count + y * side + z
+
+        places = [(m, i) for m in range(mem_count) for i in range(cell_count)]
+        return lax.ppermute(value, ("mem", "cell"), [(m * cell_count + i, target(m, i)) for m, i in places])
 
     low = lax.ppermute(prior_samples[:, rows - 1, :], "cell", forward)
     high = lax.ppermute(prior_samples[:, 0, :], "cell", backward)
@@ -334,25 +348,37 @@
     seen = call(
         halo_kernel,
         seen_shape,
-        in_specs=[smem, smem] + [pl.BlockSpec(memory_space=pltpu.VMEM)] * 5,
-        out_specs=pl.BlockSpec(memory_space=pltpu.VMEM),
+        grid=(1,),
+        in_specs=[
+            smem,
+            smem,
+            spec((members, ALL_OBS)),
+            spec((members, width)),
+            spec((members, width)),
+            spec((4, rows, width)),
+            spec(obs_cell.shape),
+        ],
+        out_specs=spec((members, ALL_OBS)),
         limit=SMALL,
     )(block_order, base, seen, low, high, neighbour_weights, obs_cell)
 
-    for pairs in (z_near, z_far, y_near, y_far):
-        seen = call(sum_kernel, seen_shape, limit=SMALL)(seen, lax.ppermute(seen, "cell", pairs))
-    lanes = pl.BlockSpec((members, 128), lambda i: (0, i % 4))
-    tiles = spec((members * 8, 128), 0)
+    tiles = spec((4 * members * 8, 128), 0)
     pieces = pl.pallas_call(
         edge_kernel,
         out_shape=shape((mem_count * members * 8, 128), f32),
-        grid=(mem_count,),
-        in_specs=[tiles, pl.BlockSpec((4, rows, 128), lambda i: (0, 0, i % 4)), lanes, lanes],
+        grid=(2,),
+        in_specs=[tiles, spec((4, rows, width)), spec((members, width)), spec((members, width))],
         out_specs=tiles,
         input_output_aliases={0: 0},
-        compiler_params=pltpu.CompilerParams(vmem_limit_bytes=SMALL),
+        compiler_params=pltpu.CompilerParams(vmem_limit_bytes=MEDIUM),
     )(pieces.reshape(mem_count * members * 8, 128), neighbour_weights, low, high)
     pieces = pieces.reshape(mem_count, members, 8, 128)
+
+    for phase in range(2):
+        others = [ring(seen, phase, d) for d in (2, 1, 3)]
+        if phase == 0:
+            pieces, *others = lax.optimization_barrier([pieces] + others)
+        seen = call(sum_kernel, seen_shape, limit=SMALL)(seen, *others)
     one, two, three = along_x(seen, 1), along_x(seen, 2), along_x(seen, 3)
     one, two, three, pieces = lax.optimization_barrier((one, two, three, pieces))
     cells = lax.all_to_all(pieces, "mem", 0, 0)
@@ -360,7 +386,6 @@
     other = lax.ppermute(seen, "mem", swap)
 
     square = (ALL_OBS, ALL_OBS)
-    whole = pl.BlockSpec(memory_space=pltpu.VMEM)
     transform = call(
         transform_kernel,
         shape(square, f32),
@@ -370,9 +395,15 @@
             pltpu.VMEM((SAMPLE_TOTAL + 8, ALL_OBS), f32),
             pltpu.VMEM(square, f32),
         ],
+        grid=(1,),
         scalars=2,
-        in_specs=[whole] * 4,
-        out_specs=whole,
+        in_specs=[
+            spec((4, members, ALL_OBS)),
+            spec((4, members, ALL_OBS)),
+            spec(obs_value.shape),
+            spec(obs_var.shape),
+        ],
+        out_specs=spec(square),
         flops=20_000_000_000,
         bytes_accessed=2_000_000,
     )(block_order, me.reshape(1), seen, other, obs_value, obs_var)

time: 122 us -> 117 us (0.959)
  Pallas kernels: 44.2 us -> 38.9 us
  waiting for transfers between devices: 9.89 us -> 14.5 us
  starting transfers between devices: 31 us -> 28.2 us
    ppermute x3, waiting for transfers between devices: 0.01 us -> 5.6 us  [along_x(): lax.ppermute(value, 'mem', [(i, (i + 2 * d) % mem_count) for i in range(m...]
    pallas_call x1, Pallas kernels: 5.69 us -> 2.66 us  [body(): pl.pallas_call(edge_kernel, out_shape=shape((mem_count * members * 8, 128...]
    pallas_call x1, Pallas kernels: 26.3 us -> 24 us  [body(): call(transform_kernel, shape(square, f32), [pltpu.VMEM(square, f32), pltp...]
    ppermute x4 -> x6, waiting for transfers between devices: 9.87 us -> 7.89 us  [ring(): lax.ppermute(value, ('mem', 'cell'), [(m * cell_count + i, target(m, i))...]
    ppermute x4 -> x6, starting transfers between devices: 11.1 us -> 9.71 us  [ring(): lax.ppermute(value, ('mem', 'cell'), [(m * cell_count + i, target(m, i))...]
    ppermute x1, starting transfers between devices: 6.68 us -> 5.31 us  [body(): other = lax.ppermute(seen, 'mem', swap)]
  transfers between devices with their start and end apart: 11 -> 13, of which waited for: 4 -> 7; matrix products, arithmetic and copies ran while one was open for 0% -> 0% of each run, Pallas kernels for 32% -> 29%
where the time goes in v4:
time: 117 us
  Pallas kernels  38.9 us (33%)
  blocking collectives  29.8 us (25%)
  starting transfers between devices  28.2 us (24%)
  waiting for transfers between devices  14.5 us (12%)
  local copies, waits for them, and re-layouts  4.95 us (4%)
    all_to_all x1, blocking collectives, body(): new = lax.all_to_all(new.reshape(mem_count, members, 8, 128), 'mem', 0, 0)  29.8 us
    pallas_call x1, Pallas kernels, body(): call(transform_kernel, shape(square, f32), [pltpu.VMEM(square, f32), pltp...  24 us
    ppermute x6, starting transfers between devices, ring(): lax.ppermute(value, ('mem', 'cell'), [(m * cell_count + i, target(m, i))...  9.71 us
    ppermute x6, waiting for transfers between devices, ring(): lax.ppermute(value, ('mem', 'cell'), [(m * cell_count + i, target(m, i))...  7.89 us
    pallas_call x1, Pallas kernels, body(): call(forecast_kernel, (shape((mem_count, members, 8, 128), f32), seen_sha...  7.04 us
    ppermute x3, waiting for transfers between devices, along_x(): lax.ppermute(value, 'mem', [(i, (i + 2 * d) % mem_count) for i in range(m...  5.6 us
    ppermute x1, starting transfers between devices, body(): other = lax.ppermute(seen, 'mem', swap)  5.31 us
    ppermute x1, starting transfers between devices, body(): low = lax.ppermute(prior_samples[:, rows - 1, :], 'cell', forward)  4.38 us
  transfers between devices with their start and end apart: 13, of which 7 were waited for; matrix products, arithmetic and copies ran while one was open for 0% of the time, Pallas kernels for 29%

profile of v4, /device:TPU:1, one launch (start us, length us, event | category | flops | bytes accessed | tf_op | source)
XLA Modules:
  0.0 116.5 jit_solution(12776348694520047908)
XLA Ops:
  0.0 1.8 %fusion = (f32[64,1,512]{2,1,0:T(1,128)S(1)}, f32[64,1,512]{2,1,0:T(1,128)S(1)}) fusion(f32[64,16,512]{2,1,0:T(8,128)} %x_ref.1), kind=kLoop, calls=%fused_computation.2 | loop fusion | bytes 524288 | tf_op jit(solution)/shard_map/slice | solution.py:325
  1.8 4.4 %collective-permute-start = (f32[64,512]{1,0:T(8,128)S(1)}, f32[64,512]{1,0:T(8,128)S(1)}, u32[]{:S(2)}, u32[]{:S(2)}) collective-permute-start(f32[64,512]{1,0:T(8,128)S(1)} %bitcast.14), channel_id=1, source_target_pairs={{0,1},{1,2},{2,3},{3,4},{4,5},{5,6},{6,7},{7,8},{8,9},{9,10},{10,1... | collective-permute-start | bytes 393224 | tf_op jit(solution)/shard_map/ppermute | solution.py:324
  6.2 1.3 %collective-permute-start.1 = (f32[64,512]{1,0:T(8,128)S(1)}, f32[64,512]{1,0:T(8,128)S(1)}, u32[]{:S(2)}, u32[]{:S(2)}) collective-permute-start(f32[64,512]{1,0:T(8,128)S(1)} %bitcast.15), channel_id=1, source_target_pairs={{1,0},{2,1},{3,2},{4,3},{5,4},{6,5},{7,6},{8,7},{9,8},{10,9},{11,1... | collective-permute-start | bytes 393224 | tf_op jit(solution)/shard_map/ppermute | solution.py:325
  7.6 7.0 %shard_map.64 = (f32[8,64,8,128]{3,2,1,0:T(8,128)}, f32[64,512]{1,0:T(8,128)}) custom-call(s32[4]{0:T(128)} %block_ref.1, s32[1]{0:T(128)} %bitcast.1.base_ref, f32[64,16,512]{2,1,0:T(8,128)} %x_ref.1, f32[4,16,512]{2,1,0:T(8,128)} %weight_ref.5, s32[4,128]{1,0:T(4,128)} %cell_ref.3), custom_call_target="tpu_custom_call" | custom-call | flops 2000000000 | bytes 4000000 | tf_op jit(solution)/shard_map/pallas_call | solution.py:328
  15.6 1.0 shard_map.65.refs_0_
  16.6 5.7 %collective-permute-start.4 = (f32[64,512]{1,0:T(8,128)S(1)}, f32[64,512]{1,0:T(8,128)S(1)}, u32[]{:S(2)}, u32[]{:S(2)}) collective-permute-start(f32[64,512]{1,0:T(8,128)S(1)} %shard_map.65.refs_0_), channel_id=1, source_target_pairs={{0,3},{1,0},{2,1},{3,2},{4,7},{5,4},{6,5},{7,6},{8,11},{9,8},{10,9... | collective-permute-start | bytes 393224 | tf_op jit(solution)/shard_map/ppermute | solution.py:322
  22.3 1.4 %collective-permute-start.2 = (f32[64,512]{1,0:T(8,128)S(1)}, f32[64,512]{1,0:T(8,128)S(1)}, u32[]{:S(2)}, u32[]{:S(2)}) collective-permute-start(f32[64,512]{1,0:T(8,128)S(1)} %shard_map.65.refs_0_), channel_id=1, source_target_pairs={{0,2},{1,3},{2,0},{3,1},{4,6},{5,7},{6,4},{7,5},{8,10},{9,11},{10,... | collective-permute-start | bytes 393224 | tf_op jit(solution)/shard_map/ppermute | solution.py:322
  23.6 2.7 %shard_map.66 = f32[4096,128]{1,0:T(8,128)} custom-call(f32[4096,128]{1,0:T(8,128)} %bitcast.4.piece_ref, f32[4,16,512]{2,1,0:T(8,128)S(1)} %copy-done, f32[64,512]{1,0:T(8,128)S(1)} %collective-permute-done.low_ref, f32[64,512]{1,0:T(8,128)S(1)} %collective-permute-done.1.high_ref), custom_call_target="tpu_custom_call", output_to_operand_aliasing={{}: (0, {})} | custom-call | tf_op jit(solution)/shard_map/pallas_call | solution.py:366
  26.3 2.7 %collective-permute-done.3.refs_2_ = f32[64,512]{1,0:T(8,128)S(1)} collective-permute-done((f32[64,512]{1,0:T(8,128)S(1)}, f32[64,512]{1,0:T(8,128)S(1)}, u32[]{:S(2)}, u32[]{:S(2)}) %collective-permute-start.3) | collective-permute-done | bytes 131104 | tf_op jit(solution)/shard_map/ppermute | solution.py:322
  29.0 1.4 %collective-permute-start.7 = (f32[64,512]{1,0:T(8,128)S(1)}, f32[64,512]{1,0:T(8,128)S(1)}, u32[]{:S(2)}, u32[]{:S(2)}) collective-permute-start(f32[64,512]{1,0:T(8,128)S(1)} %shard_map.67.refs_0_), channel_id=1, source_target_pairs={{0,12},{1,13},{2,14},{3,15},{4,0},{5,1},{6,2},{7,3},{8,4},{9,5},{1... | collective-permute-start | bytes 393224 | tf_op jit(solution)/shard_map/ppermute | solution.py:322
  30.6 1.1 collective-permute-start.5
  31.7 1.6 %collective-permute-done.7.refs_3_ = f32[64,512]{1,0:T(8,128)S(1)} collective-permute-done((f32[64,512]{1,0:T(8,128)S(1)}, f32[64,512]{1,0:T(8,128)S(1)}, u32[]{:S(2)}, u32[]{:S(2)}) %collective-permute-start.7) | collective-permute-done | bytes 131104 | tf_op jit(solution)/shard_map/ppermute | solution.py:322
  33.2 3.6 %collective-permute-done.6.refs_2_ = f32[64,512]{1,0:T(8,128)S(1)} collective-permute-done((f32[64,512]{1,0:T(8,128)S(1)}, f32[64,512]{1,0:T(8,128)S(1)}, u32[]{:S(2)}, u32[]{:S(2)}) %collective-permute-start.6) | collective-permute-done | bytes 131104 | tf_op jit(solution)/shard_map/ppermute | solution.py:322
  36.9 2.5 %collective-permute-start.10 = (f32[64,512]{1,0:T(8,128)S(1)}, f32[64,512]{1,0:T(8,128)S(1)}, u32[]{:S(2)}, u32[]{:S(2)}) collective-permute-start(f32[64,512]{1,0:T(8,128)S(1)} %shard_map.68.refs_0_), channel_id=1, source_target_pairs={{0,96},{16,112},{32,0},{48,16},{64,32},{80,48},{96,64},{112,80},{1... | collective-permute-start | bytes 393224 | tf_op jit(solution)/shard_map/ppermute | solution.py:310
  40.5 2.2 %collective-permute-done.10.refs_3_ = f32[64,512]{1,0:T(8,128)S(1)} collective-permute-done((f32[64,512]{1,0:T(8,128)S(1)}, f32[64,512]{1,0:T(8,128)S(1)}, u32[]{:S(2)}, u32[]{:S(2)}) %collective-permute-start.10) | collective-permute-done | bytes 131104 | tf_op jit(solution)/shard_map/ppermute | solution.py:310
  42.7 2.1 %collective-permute-done.9.refs_2_ = f32[64,512]{1,0:T(8,128)S(1)} collective-permute-done((f32[64,512]{1,0:T(8,128)S(1)}, f32[64,512]{1,0:T(8,128)S(1)}, u32[]{:S(2)}, u32[]{:S(2)}) %collective-permute-start.9) | collective-permute-done | bytes 131104 | tf_op jit(solution)/shard_map/ppermute | solution.py:310
  44.8 1.3 %collective-permute-done.8.refs_1_ = f32[64,512]{1,0:T(8,128)S(1)} collective-permute-done((f32[64,512]{1,0:T(8,128)S(1)}, f32[64,512]{1,0:T(8,128)S(1)}, u32[]{:S(2)}, u32[]{:S(2)}) %collective-permute-start.8) | collective-permute-done | bytes 131104 | tf_op jit(solution)/shard_map/ppermute | solution.py:310
  46.2 5.3 %collective-permute-start.11 = (f32[4,64,512]{2,1,0:T(8,128)S(1)}, f32[4,64,512]{2,1,0:T(8,128)S(1)}, u32[]{:S(2)}, u32[]{:S(2)}) collective-permute-start(f32[4,64,512]{2,1,0:T(8,128)S(1)} %shard_map.69.seen_ref), channel_id=1, source_target_pairs={{0,16},{16,0},{32,48},{48,32},{64,80},{80,64},{96,112},{112,96},{1... | collective-permute-start | bytes 1572872 | tf_op jit(solution)/shard_map/ppermute | solution.py:386
  51.5 3.9 %all-to-all-start = ((f32[8,64,8,128]{3,2,1,0:T(8,128)}), f32[8,64,8,128]{3,2,1,0:T(8,128)S(1)}, u32[]{:S(2)}, u32[]{:S(2)}) async-start(f32[8,64,8,128]{3,2,1,0:T(8,128)} %bitcast.5), calls=%async_computation | async-start | bytes 4194304 | tf_op jit(solution)/shard_map/all_to_all | solution.py:384
  55.4 24.0 %shard_map.70.transform_ref = f32[512,512]{1,0:T(8,128)S(1)} custom-call(s32[4]{0:T(128)S(1)} %copy-done.3, s32[1]{0:T(128)} %bitcast.me_ref, f32[4,64,512]{2,1,0:T(8,128)S(1)} %shard_map.69.seen_ref, f32[4,64,512]{2,1,0:T(8,128)S(1)} %collective-permute-done.11.other_ref, f32[4,128]{1,0:T(4,128)S(1)} %copy-done.4, f32[4,128]{1,0:T(4,128)S(1)} %copy-done.5), custom_call_target="tpu_custom_call" | custom-call | flops 20000000000 | bytes 2000000 | tf_op jit(solution)/shard_map/pallas_call | solution.py:389
  81.4 1.2 %copy-done.7 = f32[512,512]{1,0:T(8,128)S(1)} copy-done((f32[512,512]{1,0:T(8,128)S(1)}, f32[512,512]{1,0:T(8,128)}, u32[]{:S(2)}) %copy-start.7) | copy-done | bytes 1048600
  82.6 2.1 %shard_map.71 = f32[4096,128]{1,0:T(8,128)S(1)} custom-call(f32[512,512]{1,0:T(8,128)S(1)} %copy-done.7, f32[4096,128]{1,0:T(8,128)S(1)} %bitcast.12), custom_call_target="tpu_custom_call" | custom-call | flops 3000000000 | bytes 4000000 | tf_op jit(solution)/shard_map/pallas_call | solution.py:412
  84.7 29.8 %all_to_all.10.parts_ref = f32[8,64,8,128]{3,2,1,0:T(8,128)S(1)} all-to-all(f32[8,64,8,128]{3,2,1,0:T(8,128)S(1)} %bitcast.13), channel_id=1, replica_groups=mesh['mem'=8,'cell'=16] {'mem'}, dimensions={0} | all-to-all | bytes 4194304 | tf_op jit(solution)/shard_map/all_to_all | solution.py:415
  114.5 2.0 %shard_map.72 = f32[64,16,512]{2,1,0:T(8,128)} custom-call(f32[8,64,8,128]{3,2,1,0:T(8,128)S(1)} %all_to_all.10.parts_ref), custom_call_target="tpu_custom_call" | custom-call | bytes 4000000 | tf_op jit(solution)/shard_map/pallas_call | solution.py:416
  (31 shorter events, 4.3 us)
Async XLA Ops:
  1.8 12.8 %collective-permute-start = (f32[64,512]{1,0:T(8,128)S(1)}, f32[64,512]{1,0:T(8,128)S(1)}, u32[]{:S(2)}, u32[]{:S(2)}) collective-permute-start(f32[64,512]{1,0:T(8,128)S(1)} %bitcast.14), channel_id=1, source_target_pairs={{0,1},{1,2},{2,3},{3,4},{4,5},{5,6},{6,7},{7,8},{8,9},{9,10},{10,1... | collective-permute-start | bytes 393224 | tf_op jit(solution)/shard_map/ppermute | solution.py:324
  6.2 8.4 %collective-permute-start.1 = (f32[64,512]{1,0:T(8,128)S(1)}, f32[64,512]{1,0:T(8,128)S(1)}, u32[]{:S(2)}, u32[]{:S(2)}) collective-permute-start(f32[64,512]{1,0:T(8,128)S(1)} %bitcast.15), channel_id=1, source_target_pairs={{1,0},{2,1},{3,2},{4,3},{5,4},{6,5},{7,6},{8,7},{9,8},{10,9},{11,1... | collective-permute-start | bytes 393224 | tf_op jit(solution)/shard_map/ppermute | solution.py:325
  7.5 7.1 %copy-start = (f32[4,16,512]{2,1,0:T(8,128)S(1)}, f32[4,16,512]{2,1,0:T(8,128)}, u32[]{:S(2)}) copy-start(f32[4,16,512]{2,1,0:T(8,128)} %weight_ref.5) | copy-start | bytes 393220
  7.5 7.1 %copy-start.2 = (s32[4,128]{1,0:T(4,128)S(1)}, s32[4,128]{1,0:T(4,128)}, u32[]{:S(2)}) copy-start(s32[4,128]{1,0:T(4,128)} %cell_ref.3) | copy-start | bytes 6148
  7.5 7.1 %copy-start.3 = (s32[4]{0:T(128)S(1)}, s32[4]{0:T(128)}, u32[]{:S(2)}) copy-start(s32[4]{0:T(128)} %block_ref.1) | copy-start | bytes 52
  14.6 0.9 copy-start.1
  16.6 9.7 %collective-permute-start.4 = (f32[64,512]{1,0:T(8,128)S(1)}, f32[64,512]{1,0:T(8,128)S(1)}, u32[]{:S(2)}, u32[]{:S(2)}) collective-permute-start(f32[64,512]{1,0:T(8,128)S(1)} %shard_map.65.refs_0_), channel_id=1, source_target_pairs={{0,3},{1,0},{2,1},{3,2},{4,7},{5,4},{6,5},{7,6},{8,11},{9,8},{10,9... | collective-permute-start | bytes 393224 | tf_op jit(solution)/shard_map/ppermute | solution.py:322
  22.3 6.7 %collective-permute-start.3 = (f32[64,512]{1,0:T(8,128)S(1)}, f32[64,512]{1,0:T(8,128)S(1)}, u32[]{:S(2)}, u32[]{:S(2)}) collective-permute-start(f32[64,512]{1,0:T(8,128)S(1)} %shard_map.65.refs_0_), channel_id=1, source_target_pairs={{0,1},{1,2},{2,3},{3,0},{4,5},{5,6},{6,7},{7,4},{8,9},{9,10},{10,1... | collective-permute-start | bytes 393224 | tf_op jit(solution)/shard_map/ppermute | solution.py:322
  22.3 6.7 %collective-permute-start.2 = (f32[64,512]{1,0:T(8,128)S(1)}, f32[64,512]{1,0:T(8,128)S(1)}, u32[]{:S(2)}, u32[]{:S(2)}) collective-permute-start(f32[64,512]{1,0:T(8,128)S(1)} %shard_map.65.refs_0_), channel_id=1, source_target_pairs={{0,2},{1,3},{2,0},{3,1},{4,6},{5,7},{6,4},{7,5},{8,10},{9,11},{10,... | collective-permute-start | bytes 393224 | tf_op jit(solution)/shard_map/ppermute | solution.py:322
  29.0 4.2 %collective-permute-start.7 = (f32[64,512]{1,0:T(8,128)S(1)}, f32[64,512]{1,0:T(8,128)S(1)}, u32[]{:S(2)}, u32[]{:S(2)}) collective-permute-start(f32[64,512]{1,0:T(8,128)S(1)} %shard_map.67.refs_0_), channel_id=1, source_target_pairs={{0,12},{1,13},{2,14},{3,15},{4,0},{5,1},{6,2},{7,3},{8,4},{9,5},{1... | collective-permute-start | bytes 393224 | tf_op jit(solution)/shard_map/ppermute | solution.py:322
  30.4 6.4 %collective-permute-start.6 = (f32[64,512]{1,0:T(8,128)S(1)}, f32[64,512]{1,0:T(8,128)S(1)}, u32[]{:S(2)}, u32[]{:S(2)}) collective-permute-start(f32[64,512]{1,0:T(8,128)S(1)} %shard_map.67.refs_0_), channel_id=1, source_target_pairs={{0,4},{1,5},{2,6},{3,7},{4,8},{5,9},{6,10},{7,11},{8,12},{9,13},{1... | collective-permute-start | bytes 393224 | tf_op jit(solution)/shard_map/ppermute | solution.py:322
  30.6 6.3 %collective-permute-start.5 = (f32[64,512]{1,0:T(8,128)S(1)}, f32[64,512]{1,0:T(8,128)S(1)}, u32[]{:S(2)}, u32[]{:S(2)}) collective-permute-start(f32[64,512]{1,0:T(8,128)S(1)} %shard_map.67.refs_0_), channel_id=1, source_target_pairs={{0,8},{1,9},{2,10},{3,11},{4,12},{5,13},{6,14},{7,15},{8,0},{9,1},... | collective-permute-start | bytes 393224 | tf_op jit(solution)/shard_map/ppermute | solution.py:322
  36.9 5.9 %collective-permute-start.10 = (f32[64,512]{1,0:T(8,128)S(1)}, f32[64,512]{1,0:T(8,128)S(1)}, u32[]{:S(2)}, u32[]{:S(2)}) collective-permute-start(f32[64,512]{1,0:T(8,128)S(1)} %shard_map.68.refs_0_), channel_id=1, source_target_pairs={{0,96},{16,112},{32,0},{48,16},{64,32},{80,48},{96,64},{112,80},{1... | collective-permute-start | bytes 393224 | tf_op jit(solution)/shard_map/ppermute | solution.py:310
  39.4 5.4 %collective-permute-start.9 = (f32[64,512]{1,0:T(8,128)S(1)}, f32[64,512]{1,0:T(8,128)S(1)}, u32[]{:S(2)}, u32[]{:S(2)}) collective-permute-start(f32[64,512]{1,0:T(8,128)S(1)} %shard_map.68.refs_0_), channel_id=1, source_target_pairs={{0,64},{16,80},{32,96},{48,112},{64,0},{80,16},{96,32},{112,48},{1... | collective-permute-start | bytes 393224 | tf_op jit(solution)/shard_map/ppermute | solution.py:310
  39.9 6.2 %collective-permute-start.8 = (f32[64,512]{1,0:T(8,128)S(1)}, f32[64,512]{1,0:T(8,128)S(1)}, u32[]{:S(2)}, u32[]{:S(2)}) collective-permute-start(f32[64,512]{1,0:T(8,128)S(1)} %shard_map.68.refs_0_), channel_id=1, source_target_pairs={{0,32},{16,48},{32,64},{48,80},{64,96},{80,112},{96,0},{112,16},{1... | collective-permute-start | bytes 393224 | tf_op jit(solution)/shard_map/ppermute | solution.py:310
  46.2 9.2 %collective-permute-start.11 = (f32[4,64,512]{2,1,0:T(8,128)S(1)}, f32[4,64,512]{2,1,0:T(8,128)S(1)}, u32[]{:S(2)}, u32[]{:S(2)}) collective-permute-start(f32[4,64,512]{2,1,0:T(8,128)S(1)} %shard_map.69.seen_ref), channel_id=1, source_target_pairs={{0,16},{16,0},{32,48},{48,32},{64,80},{80,64},{96,112},{112,96},{1... | collective-permute-start | bytes 1572872 | tf_op jit(solution)/shard_map/ppermute | solution.py:386
  51.5 3.9 %copy-start.4 = (f32[4,128]{1,0:T(4,128)S(1)}, f32[4,128]{1,0:T(4,128)}, u32[]{:S(2)}) copy-start(f32[4,128]{1,0:T(4,128)} %value_ref.1) | copy-start | bytes 6148
  51.5 3.9 %copy-start.5 = (f32[4,128]{1,0:T(4,128)S(1)}, f32[4,128]{1,0:T(4,128)}, u32[]{:S(2)}) copy-start(f32[4,128]{1,0:T(4,128)} %var_ref.1) | copy-start | bytes 6148
  51.5 29.9 %all-to-all-start = ((f32[8,64,8,128]{3,2,1,0:T(8,128)}), f32[8,64,8,128]{3,2,1,0:T(8,128)S(1)}, u32[]{:S(2)}, u32[]{:S(2)}) async-start(f32[8,64,8,128]{3,2,1,0:T(8,128)} %bitcast.5), calls=%async_computation | async-start | bytes 4194304 | tf_op jit(solution)/shard_map/all_to_all | solution.py:384
  79.4 1.0 copy-start.6
  81.4 1.2 %copy-start.7 = (f32[512,512]{1,0:T(8,128)S(1)}, f32[512,512]{1,0:T(8,128)}, u32[]{:S(2)}) copy-start(f32[512,512]{1,0:T(8,128)} %copy-done.6) | copy-start | bytes 3145732

commit v5 on v4

--- a/solution.py
+++ b/solution.py
@@ -77,7 +77,7 @@
                 piece_ref[4 * h + q, m] = f[8 * h : 8 * h + 8, 128 * q : 128 * q + 128]
         return carry
 
-    lax.fori_loop(0, members, member, 0, unroll=4)
+    lax.fori_loop(0, members, member, 0, unroll=8)
     own_row = (lax.broadcasted_iota(jnp.int32, (rows, ALL_OBS), 0) == at_row).astype(jnp.float32)
     pick = pick_ref[...]
     part = 8
@@ -196,7 +196,7 @@
 
 def transform_kernel(
     block_ref, me_ref, seen_ref, other_ref, value_ref, var_ref,
-    out_ref, cov_ref, state_ref, gain_ref, minus_ref,
+    out_ref, cov_ref, state_ref, gain_ref, minus_ref, total_ref,
 ):
     n = ALL_OBS
     blocks = n // NOBS
@@ -230,6 +230,10 @@
             cov_ref[high:, low:high] = cov[NOBS:]
     for j in range(blocks):
         low, high = NOBS * j, NOBS * (j + 1)
+        if j == blocks - 1:
+            mean_step = gain_ref[SAMPLE_TOTAL : SAMPLE_TOTAL + 1, :low]
+            left = (mean_step - minus_ref[:, :low]) * (1.0 / (SAMPLE_TOTAL - 1))
+            total_ref[...] = dot3(left, gain_ref[0:SAMPLE_TOTAL, :low], NT)
         root = jnp.sqrt(jnp.broadcast_to(var[:, low:high], (NOBS, NOBS))).T
         inv_low, inv_sum = factor(cov_ref[low:high, low:high], root)
         rest = high < n
@@ -247,10 +251,9 @@
             state_ref[:, high:] = state_ref[:, high:] - dot_split(halves(gain), below, NT)
             minus_ref[:, high:] = minus_ref[:, high:] - dot_split(halves(minus), below, NT)
         minus_ref[:, low:high] = minus
-    mean_step = gain_ref[SAMPLE_TOTAL : SAMPLE_TOTAL + 1, :]
-    left = (mean_step - minus_ref[...]) * (1.0 / (SAMPLE_TOTAL - 1))
-    total = dot3(left, gain_ref[0:SAMPLE_TOTAL, :], NT)
-    out_ref[...] = total
+    low = n - NOBS
+    left = (gain_ref[SAMPLE_TOTAL : SAMPLE_TOTAL + 1, low:] - minus_ref[:, low:]) * (1.0 / (SAMPLE_TOTAL - 1))
+    out_ref[...] = total_ref[...] + dot3(left, gain_ref[0:SAMPLE_TOTAL, low:], NT)
 
 
 def update_kernel(transform_ref, cells_ref, out_ref):
@@ -268,10 +271,16 @@
         refs[-1][i] = ref[...]
 
 
-def join_kernel(parts_ref, out_ref):
+def join_kernel(parts_ref, out_ref, arrived):
+    copies = []
     for h in range(2):
         for q in range(4):
-            out_ref[:, 8 * h : 8 * h + 8, 128 * q : 128 * q + 128] = parts_ref[4 * h + q]
+            place = out_ref.at[:, 8 * h : 8 * h + 8, 128 * q : 128 * q + 128]
+            copies.append(pltpu.make_async_copy(parts_ref.at[4 * h + q], place, arrived.at[4 * h + q]))
+    for copy in copies:
+        copy.start()
+    for copy in copies:
+        copy.wait()
 
 
 def call(kernel, out_shape, scratch=(), grid=(), scalars=0, in_specs=None, out_specs=None, flops=0, bytes_accessed=0, limit=MEDIUM):
@@ -299,7 +308,7 @@
     me = lax.axis_index("mem")
     base = (lax.axis_index("cell") * rows).reshape(1)
     shape = jax.ShapeDtypeStruct
-    steps = 4
+    steps = 2
     step = members // steps
     side = 4
     forward = [(i, i + 1) for i in range(cell_count - 1)]
@@ -375,11 +384,11 @@
     pieces = pieces.reshape(mem_count, members, 8, 128)
 
     for phase in range(2):
-        others = [ring(seen, phase, d) for d in (2, 1, 3)]
+        others = [ring(seen, phase, d) for d in (1, 3, 2)]
         if phase == 0:
             pieces, *others = lax.optimization_barrier([pieces] + others)
         seen = call(sum_kernel, seen_shape, limit=SMALL)(seen, *others)
-    one, two, three = along_x(seen, 1), along_x(seen, 2), along_x(seen, 3)
+    one, three, two = along_x(seen, 1), along_x(seen, 3), along_x(seen, 2)
     one, two, three, pieces = lax.optimization_barrier((one, two, three, pieces))
     cells = lax.all_to_all(pieces, "mem", 0, 0)
     seen = call(stack_kernel, shape((4, members, ALL_OBS), f32), limit=SMALL)(seen, one, two, three)
@@ -393,6 +402,7 @@
             pltpu.VMEM(square, f32),
             pltpu.VMEM((SAMPLE_TOTAL + 8, ALL_OBS), f32),
             pltpu.VMEM((SAMPLE_TOTAL + 8, ALL_OBS), f32),
+            pltpu.VMEM(square, f32),
             pltpu.VMEM(square, f32),
         ],
         grid=(1,),
@@ -413,13 +423,16 @@
         transform, cells
     )
     new = lax.all_to_all(new.reshape(mem_count, members, 8, 128), "mem", 0, 0)
+    anywhere = pl.BlockSpec(memory_space=pl.ANY)
     return call(
         join_kernel,
         shape(prior_samples.shape, f32),
-        grid=(4,),
-        in_specs=[spec((mem_count, step, 8, 128), None, 0)],
-        out_specs=spec((step, rows, width), 0),
+        [pltpu.SemaphoreType.DMA((8,))],
+        grid=(1,),
+        in_specs=[anywhere],
+        out_specs=anywhere,
         bytes_accessed=4_000_000,
+        limit=SMALL,
     )(new)
 
 

time: 117 us -> 115 us (0.983)
  waiting for transfers between devices: 14.5 us -> 12.9 us
  Pallas kernels: 38.9 us -> 37.7 us
    ppermute x6, waiting for transfers between devices: 7.89 us -> 6.27 us  [ring(): lax.ppermute(value, ('mem', 'cell'), [(m * cell_count + i, target(m, i))...]
  transfers between devices with their start and end apart: 13 -> 13, of which waited for: 7 -> 9; matrix products, arithmetic and copies ran while one was open for 0% -> 0% of each run, Pallas kernels for 29% -> 29%
where the time goes in v5:
time: 115 us
  Pallas kernels  37.7 us (33%)
  blocking collectives  29.8 us (26%)
  starting transfers between devices  28.8 us (25%)
  waiting for transfers between devices  12.9 us (11%)
  local copies, waits for them, and re-layouts  4.94 us (4%)
    all_to_all x1, blocking collectives, body(): new = lax.all_to_all(new.reshape(mem_count, members, 8, 128), 'mem', 0, 0)  29.8 us
    pallas_call x1, Pallas kernels, body(): call(transform_kernel, shape(square, f32), [pltpu.VMEM(square, f32), pltp...  24 us
    ppermute x6, starting transfers between devices, ring(): lax.ppermute(value, ('mem', 'cell'), [(m * cell_count + i, target(m, i))...  9.75 us
    pallas_call x1, Pallas kernels, body(): call(forecast_kernel, (shape((mem_count, members, 8, 128), f32), seen_sha...  6.55 us
    ppermute x6, waiting for transfers between devices, ring(): lax.ppermute(value, ('mem', 'cell'), [(m * cell_count + i, target(m, i))...  6.27 us
    ppermute x1, starting transfers between devices, body(): other = lax.ppermute(seen, 'mem', swap)  5.85 us
    ppermute x3, waiting for transfers between devices, along_x(): lax.ppermute(value, 'mem', [(i, (i + 2 * d) % mem_count) for i in range(m...  5.6 us
    ppermute x1, starting transfers between devices, body(): low = lax.ppermute(prior_samples[:, rows - 1, :], 'cell', forward)  4.38 us
  transfers between devices with their start and end apart: 13, of which 9 were waited for; matrix products, arithmetic and copies ran while one was open for 0% of the time, Pallas kernels for 29%

profile of v5, /device:TPU:1, one launch (start us, length us, event | category | flops | bytes accessed | tf_op | source)
XLA Modules:
  0.0 114.5 jit_solution(301771641655693093)
XLA Ops:
  0.0 1.8 %fusion = (f32[64,1,512]{2,1,0:T(1,128)S(1)}, f32[64,1,512]{2,1,0:T(1,128)S(1)}) fusion(f32[64,16,512]{2,1,0:T(8,128)} %x_ref.1), kind=kLoop, calls=%fused_computation.2 | loop fusion | bytes 524288 | tf_op jit(solution)/shard_map/slice | solution.py:334
  1.8 4.4 %collective-permute-start = (f32[64,512]{1,0:T(8,128)S(1)}, f32[64,512]{1,0:T(8,128)S(1)}, u32[]{:S(2)}, u32[]{:S(2)}) collective-permute-start(f32[64,512]{1,0:T(8,128)S(1)} %bitcast.14), channel_id=1, source_target_pairs={{0,1},{1,2},{2,3},{3,4},{4,5},{5,6},{6,7},{7,8},{8,9},{9,10},{10,1... | collective-permute-start | bytes 393224 | tf_op jit(solution)/shard_map/ppermute | solution.py:333
  6.2 1.3 %collective-permute-start.1 = (f32[64,512]{1,0:T(8,128)S(1)}, f32[64,512]{1,0:T(8,128)S(1)}, u32[]{:S(2)}, u32[]{:S(2)}) collective-permute-start(f32[64,512]{1,0:T(8,128)S(1)} %bitcast.15), channel_id=1, source_target_pairs={{1,0},{2,1},{3,2},{4,3},{5,4},{6,5},{7,6},{8,7},{9,8},{10,9},{11,1... | collective-permute-start | bytes 393224 | tf_op jit(solution)/shard_map/ppermute | solution.py:334
  7.6 6.5 %shard_map.64 = (f32[8,64,8,128]{3,2,1,0:T(8,128)}, f32[64,512]{1,0:T(8,128)}) custom-call(s32[4]{0:T(128)} %block_ref.1, s32[1]{0:T(128)} %bitcast.1.base_ref, f32[64,16,512]{2,1,0:T(8,128)} %x_ref.1, f32[4,16,512]{2,1,0:T(8,128)} %weight_ref.5, s32[4,128]{1,0:T(4,128)} %cell_ref.3), custom_call_target="tpu_custom_call" | custom-call | flops 2000000000 | bytes 4000000 | tf_op jit(solution)/shard_map/pallas_call | solution.py:337
  15.1 1.0 shard_map.65.refs_0_
  16.1 5.6 %collective-permute-start.4 = (f32[64,512]{1,0:T(8,128)S(1)}, f32[64,512]{1,0:T(8,128)S(1)}, u32[]{:S(2)}, u32[]{:S(2)}) collective-permute-start(f32[64,512]{1,0:T(8,128)S(1)} %shard_map.65.refs_0_), channel_id=1, source_target_pairs={{0,2},{1,3},{2,0},{3,1},{4,6},{5,7},{6,4},{7,5},{8,10},{9,11},{10,... | collective-permute-start | bytes 393224 | tf_op jit(solution)/shard_map/ppermute | solution.py:331
  23.2 2.7 %shard_map.66 = f32[4096,128]{1,0:T(8,128)} custom-call(f32[4096,128]{1,0:T(8,128)} %bitcast.4.piece_ref, f32[4,16,512]{2,1,0:T(8,128)S(1)} %copy-done, f32[64,512]{1,0:T(8,128)S(1)} %collective-permute-done.low_ref, f32[64,512]{1,0:T(8,128)S(1)} %collective-permute-done.1.high_ref), custom_call_target="tpu_custom_call", output_to_operand_aliasing={{}: (0, {})} | custom-call | tf_op jit(solution)/shard_map/pallas_call | solution.py:375
  26.4 1.4 %collective-permute-done.2.refs_1_ = f32[64,512]{1,0:T(8,128)S(1)} collective-permute-done((f32[64,512]{1,0:T(8,128)S(1)}, f32[64,512]{1,0:T(8,128)S(1)}, u32[]{:S(2)}, u32[]{:S(2)}) %collective-permute-start.2) | collective-permute-done | bytes 131104 | tf_op jit(solution)/shard_map/ppermute | solution.py:331
  27.8 1.2 %collective-permute-start.7 = (f32[64,512]{1,0:T(8,128)S(1)}, f32[64,512]{1,0:T(8,128)S(1)}, u32[]{:S(2)}, u32[]{:S(2)}) collective-permute-start(f32[64,512]{1,0:T(8,128)S(1)} %shard_map.67.refs_0_), channel_id=1, source_target_pairs={{0,8},{1,9},{2,10},{3,11},{4,12},{5,13},{6,14},{7,15},{8,0},{9,1},... | collective-permute-start | bytes 393224 | tf_op jit(solution)/shard_map/ppermute | solution.py:331
  30.5 3.0 %collective-permute-done.7.refs_3_ = f32[64,512]{1,0:T(8,128)S(1)} collective-permute-done((f32[64,512]{1,0:T(8,128)S(1)}, f32[64,512]{1,0:T(8,128)S(1)}, u32[]{:S(2)}, u32[]{:S(2)}) %collective-permute-start.7) | collective-permute-done | bytes 131104 | tf_op jit(solution)/shard_map/ppermute | solution.py:331
  33.8 1.0 collective-permute-done.5.refs_1_
  34.8 2.5 %collective-permute-start.10 = (f32[64,512]{1,0:T(8,128)S(1)}, f32[64,512]{1,0:T(8,128)S(1)}, u32[]{:S(2)}, u32[]{:S(2)}) collective-permute-start(f32[64,512]{1,0:T(8,128)S(1)} %shard_map.68.refs_0_), channel_id=1, source_target_pairs={{0,96},{16,112},{32,0},{48,16},{64,32},{80,48},{96,64},{112,80},{1... | collective-permute-start | bytes 393224 | tf_op jit(solution)/shard_map/ppermute | solution.py:319
  38.5 2.2 %collective-permute-done.10.refs_3_ = f32[64,512]{1,0:T(8,128)S(1)} collective-permute-done((f32[64,512]{1,0:T(8,128)S(1)}, f32[64,512]{1,0:T(8,128)S(1)}, u32[]{:S(2)}, u32[]{:S(2)}) %collective-permute-start.10) | collective-permute-done | bytes 131104 | tf_op jit(solution)/shard_map/ppermute | solution.py:319
  40.7 2.1 %collective-permute-done.9.refs_2_ = f32[64,512]{1,0:T(8,128)S(1)} collective-permute-done((f32[64,512]{1,0:T(8,128)S(1)}, f32[64,512]{1,0:T(8,128)S(1)}, u32[]{:S(2)}, u32[]{:S(2)}) %collective-permute-start.9) | collective-permute-done | bytes 131104 | tf_op jit(solution)/shard_map/ppermute | solution.py:319
  42.8 1.3 %collective-permute-done.8.refs_1_ = f32[64,512]{1,0:T(8,128)S(1)} collective-permute-done((f32[64,512]{1,0:T(8,128)S(1)}, f32[64,512]{1,0:T(8,128)S(1)}, u32[]{:S(2)}, u32[]{:S(2)}) %collective-permute-start.8) | collective-permute-done | bytes 131104 | tf_op jit(solution)/shard_map/ppermute | solution.py:319
  44.1 5.9 %collective-permute-start.11 = (f32[4,64,512]{2,1,0:T(8,128)S(1)}, f32[4,64,512]{2,1,0:T(8,128)S(1)}, u32[]{:S(2)}, u32[]{:S(2)}) collective-permute-start(f32[4,64,512]{2,1,0:T(8,128)S(1)} %shard_map.69.seen_ref), channel_id=1, source_target_pairs={{0,16},{16,0},{32,48},{48,32},{64,80},{80,64},{96,112},{112,96},{1... | collective-permute-start | bytes 1572872 | tf_op jit(solution)/shard_map/ppermute | solution.py:395
  50.0 3.9 %all-to-all-start = ((f32[8,64,8,128]{3,2,1,0:T(8,128)}), f32[8,64,8,128]{3,2,1,0:T(8,128)S(1)}, u32[]{:S(2)}, u32[]{:S(2)}) async-start(f32[8,64,8,128]{3,2,1,0:T(8,128)} %bitcast.5), calls=%async_computation | async-start | bytes 4194304 | tf_op jit(solution)/shard_map/all_to_all | solution.py:393
  53.9 24.0 %shard_map.70.transform_ref = f32[512,512]{1,0:T(8,128)S(1)} custom-call(s32[4]{0:T(128)S(1)} %copy-done.3, s32[1]{0:T(128)} %bitcast.me_ref, f32[4,64,512]{2,1,0:T(8,128)S(1)} %shard_map.69.seen_ref, f32[4,64,512]{2,1,0:T(8,128)S(1)} %collective-permute-done.11.other_ref, f32[4,128]{1,0:T(4,128)S(1)} %copy-done.4, f32[4,128]{1,0:T(4,128)S(1)} %copy-done.5), custom_call_target="tpu_custom_call" | custom-call | flops 20000000000 | bytes 2000000 | tf_op jit(solution)/shard_map/pallas_call | solution.py:398
  77.9 1.0 copy-done.6
  78.9 1.0 all-to-all-done
  79.9 1.2 %copy-done.7 = f32[512,512]{1,0:T(8,128)S(1)} copy-done((f32[512,512]{1,0:T(8,128)S(1)}, f32[512,512]{1,0:T(8,128)}, u32[]{:S(2)}) %copy-start.7) | copy-done | bytes 1048600
  81.1 2.1 %shard_map.71 = f32[4096,128]{1,0:T(8,128)S(1)} custom-call(f32[512,512]{1,0:T(8,128)S(1)} %copy-done.7, f32[4096,128]{1,0:T(8,128)S(1)} %bitcast.12), custom_call_target="tpu_custom_call" | custom-call | flops 3000000000 | bytes 4000000 | tf_op jit(solution)/shard_map/pallas_call | solution.py:422
  83.2 29.8 %all_to_all.10.parts_ref = f32[8,64,8,128]{3,2,1,0:T(8,128)S(1)} all-to-all(f32[8,64,8,128]{3,2,1,0:T(8,128)S(1)} %bitcast.13), channel_id=1, replica_groups=mesh['mem'=8,'cell'=16] {'mem'}, dimensions={0} | all-to-all | bytes 4194304 | tf_op jit(solution)/shard_map/all_to_all | solution.py:425
  113.0 1.4 %shard_map.72 = f32[64,16,512]{2,1,0:T(8,128)} custom-call(f32[8,64,8,128]{3,2,1,0:T(8,128)S(1)} %all_to_all.10.parts_ref), custom_call_target="tpu_custom_call" | custom-call | bytes 4000000 | tf_op jit(solution)/shard_map/pallas_call | solution.py:427
  (31 shorter events, 6.0 us)
Async XLA Ops:
  1.8 12.3 %collective-permute-start = (f32[64,512]{1,0:T(8,128)S(1)}, f32[64,512]{1,0:T(8,128)S(1)}, u32[]{:S(2)}, u32[]{:S(2)}) collective-permute-start(f32[64,512]{1,0:T(8,128)S(1)} %bitcast.14), channel_id=1, source_target_pairs={{0,1},{1,2},{2,3},{3,4},{4,5},{5,6},{6,7},{7,8},{8,9},{9,10},{10,1... | collective-permute-start | bytes 393224 | tf_op jit(solution)/shard_map/ppermute | solution.py:333
  6.2 7.9 %collective-permute-start.1 = (f32[64,512]{1,0:T(8,128)S(1)}, f32[64,512]{1,0:T(8,128)S(1)}, u32[]{:S(2)}, u32[]{:S(2)}) collective-permute-start(f32[64,512]{1,0:T(8,128)S(1)} %bitcast.15), channel_id=1, source_target_pairs={{1,0},{2,1},{3,2},{4,3},{5,4},{6,5},{7,6},{8,7},{9,8},{10,9},{11,1... | collective-permute-start | bytes 393224 | tf_op jit(solution)/shard_map/ppermute | solution.py:334
  7.5 6.6 %copy-start = (f32[4,16,512]{2,1,0:T(8,128)S(1)}, f32[4,16,512]{2,1,0:T(8,128)}, u32[]{:S(2)}) copy-start(f32[4,16,512]{2,1,0:T(8,128)} %weight_ref.5) | copy-start | bytes 393220
  7.5 6.6 %copy-start.2 = (s32[4,128]{1,0:T(4,128)S(1)}, s32[4,128]{1,0:T(4,128)}, u32[]{:S(2)}) copy-start(s32[4,128]{1,0:T(4,128)} %cell_ref.3) | copy-start | bytes 6148
  7.5 6.6 %copy-start.3 = (s32[4]{0:T(128)S(1)}, s32[4]{0:T(128)}, u32[]{:S(2)}) copy-start(s32[4]{0:T(128)} %block_ref.1) | copy-start | bytes 52
  14.1 0.9 copy-start.1
  16.1 9.8 %collective-permute-start.4 = (f32[64,512]{1,0:T(8,128)S(1)}, f32[64,512]{1,0:T(8,128)S(1)}, u32[]{:S(2)}, u32[]{:S(2)}) collective-permute-start(f32[64,512]{1,0:T(8,128)S(1)} %shard_map.65.refs_0_), channel_id=1, source_target_pairs={{0,2},{1,3},{2,0},{3,1},{4,6},{5,7},{6,4},{7,5},{8,10},{9,11},{10,... | collective-permute-start | bytes 393224 | tf_op jit(solution)/shard_map/ppermute | solution.py:331
  21.7 4.7 %collective-permute-start.3 = (f32[64,512]{1,0:T(8,128)S(1)}, f32[64,512]{1,0:T(8,128)S(1)}, u32[]{:S(2)}, u32[]{:S(2)}) collective-permute-start(f32[64,512]{1,0:T(8,128)S(1)} %shard_map.65.refs_0_), channel_id=1, source_target_pairs={{0,3},{1,0},{2,1},{3,2},{4,7},{5,4},{6,5},{7,6},{8,11},{9,8},{10,9... | collective-permute-start | bytes 393224 | tf_op jit(solution)/shard_map/ppermute | solution.py:331
  22.5 5.3 %collective-permute-start.2 = (f32[64,512]{1,0:T(8,128)S(1)}, f32[64,512]{1,0:T(8,128)S(1)}, u32[]{:S(2)}, u32[]{:S(2)}) collective-permute-start(f32[64,512]{1,0:T(8,128)S(1)} %shard_map.65.refs_0_), channel_id=1, source_target_pairs={{0,1},{1,2},{2,3},{3,0},{4,5},{5,6},{6,7},{7,4},{8,9},{9,10},{10,1... | collective-permute-start | bytes 393224 | tf_op jit(solution)/shard_map/ppermute | solution.py:331
  27.8 5.7 %collective-permute-start.7 = (f32[64,512]{1,0:T(8,128)S(1)}, f32[64,512]{1,0:T(8,128)S(1)}, u32[]{:S(2)}, u32[]{:S(2)}) collective-permute-start(f32[64,512]{1,0:T(8,128)S(1)} %shard_map.67.refs_0_), channel_id=1, source_target_pairs={{0,8},{1,9},{2,10},{3,11},{4,12},{5,13},{6,14},{7,15},{8,0},{9,1},... | collective-permute-start | bytes 393224 | tf_op jit(solution)/shard_map/ppermute | solution.py:331
  29.0 4.8 %collective-permute-start.6 = (f32[64,512]{1,0:T(8,128)S(1)}, f32[64,512]{1,0:T(8,128)S(1)}, u32[]{:S(2)}, u32[]{:S(2)}) collective-permute-start(f32[64,512]{1,0:T(8,128)S(1)} %shard_map.67.refs_0_), channel_id=1, source_target_pairs={{0,12},{1,13},{2,14},{3,15},{4,0},{5,1},{6,2},{7,3},{8,4},{9,5},{1... | collective-permute-start | bytes 393224 | tf_op jit(solution)/shard_map/ppermute | solution.py:331
  29.6 5.2 %collective-permute-start.5 = (f32[64,512]{1,0:T(8,128)S(1)}, f32[64,512]{1,0:T(8,128)S(1)}, u32[]{:S(2)}, u32[]{:S(2)}) collective-permute-start(f32[64,512]{1,0:T(8,128)S(1)} %shard_map.67.refs_0_), channel_id=1, source_target_pairs={{0,4},{1,5},{2,6},{3,7},{4,8},{5,9},{6,10},{7,11},{8,12},{9,13},{1... | collective-permute-start | bytes 393224 | tf_op jit(solution)/shard_map/ppermute | solution.py:331
  34.8 5.9 %collective-permute-start.10 = (f32[64,512]{1,0:T(8,128)S(1)}, f32[64,512]{1,0:T(8,128)S(1)}, u32[]{:S(2)}, u32[]{:S(2)}) collective-permute-start(f32[64,512]{1,0:T(8,128)S(1)} %shard_map.68.refs_0_), channel_id=1, source_target_pairs={{0,96},{16,112},{32,0},{48,16},{64,32},{80,48},{96,64},{112,80},{1... | collective-permute-start | bytes 393224 | tf_op jit(solution)/shard_map/ppermute | solution.py:319
  37.4 5.4 %collective-permute-start.9 = (f32[64,512]{1,0:T(8,128)S(1)}, f32[64,512]{1,0:T(8,128)S(1)}, u32[]{:S(2)}, u32[]{:S(2)}) collective-permute-start(f32[64,512]{1,0:T(8,128)S(1)} %shard_map.68.refs_0_), channel_id=1, source_target_pairs={{0,64},{16,80},{32,96},{48,112},{64,0},{80,16},{96,32},{112,48},{1... | collective-permute-start | bytes 393224 | tf_op jit(solution)/shard_map/ppermute | solution.py:319
  37.9 6.2 %collective-permute-start.8 = (f32[64,512]{1,0:T(8,128)S(1)}, f32[64,512]{1,0:T(8,128)S(1)}, u32[]{:S(2)}, u32[]{:S(2)}) collective-permute-start(f32[64,512]{1,0:T(8,128)S(1)} %shard_map.68.refs_0_), channel_id=1, source_target_pairs={{0,32},{16,48},{32,64},{48,80},{64,96},{80,112},{96,0},{112,16},{1... | collective-permute-start | bytes 393224 | tf_op jit(solution)/shard_map/ppermute | solution.py:319
  44.1 9.7 %collective-permute-start.11 = (f32[4,64,512]{2,1,0:T(8,128)S(1)}, f32[4,64,512]{2,1,0:T(8,128)S(1)}, u32[]{:S(2)}, u32[]{:S(2)}) collective-permute-start(f32[4,64,512]{2,1,0:T(8,128)S(1)} %shard_map.69.seen_ref), channel_id=1, source_target_pairs={{0,16},{16,0},{32,48},{48,32},{64,80},{80,64},{96,112},{112,96},{1... | collective-permute-start | bytes 1572872 | tf_op jit(solution)/shard_map/ppermute | solution.py:395
  50.0 3.9 %copy-start.4 = (f32[4,128]{1,0:T(4,128)S(1)}, f32[4,128]{1,0:T(4,128)}, u32[]{:S(2)}) copy-start(f32[4,128]{1,0:T(4,128)} %value_ref.1) | copy-start | bytes 6148
  50.0 3.9 %copy-start.5 = (f32[4,128]{1,0:T(4,128)S(1)}, f32[4,128]{1,0:T(4,128)}, u32[]{:S(2)}) copy-start(f32[4,128]{1,0:T(4,128)} %var_ref.1) | copy-start | bytes 6148
  50.0 29.9 %all-to-all-start = ((f32[8,64,8,128]{3,2,1,0:T(8,128)}), f32[8,64,8,128]{3,2,1,0:T(8,128)S(1)}, u32[]{:S(2)}, u32[]{:S(2)}) async-start(f32[8,64,8,128]{3,2,1,0:T(8,128)} %bitcast.5), calls=%async_computation | async-start | bytes 4194304 | tf_op jit(solution)/shard_map/all_to_all | solution.py:393
  77.9 1.0 copy-start.6
  79.9 1.2 %copy-start.7 = (f32[512,512]{1,0:T(8,128)S(1)}, f32[512,512]{1,0:T(8,128)}, u32[]{:S(2)}) copy-start(f32[512,512]{1,0:T(8,128)} %copy-done.6) | copy-start | bytes 3145732

commit v6 on v5

--- a/solution.py
+++ b/solution.py
@@ -242,14 +242,12 @@
             for at in range(high, n, NOBS):
                 change = dot6(below[at - high :], below[at - high : at - high + NOBS], NT)
                 cov_ref[at:, at : at + NOBS] = cov_ref[at:, at : at + NOBS] - change
-            below = halves(below)
-        inv_low, inv_sum = halves(inv_low), halves(inv_sum)
-        gain = dot_split(halves(state_ref[:, low:high]), inv_low, NT)
-        minus = dot_split(halves(minus_ref[:, low:high]), inv_sum, NT)
+        gain = dot6(state_ref[:, low:high], inv_low, NT)
+        minus = dot6(minus_ref[:, low:high], inv_sum, NT)
         gain_ref[:, low:high] = gain
         if rest:
-            state_ref[:, high:] = state_ref[:, high:] - dot_split(halves(gain), below, NT)
-            minus_ref[:, high:] = minus_ref[:, high:] - dot_split(halves(minus), below, NT)
+            state_ref[:, high:] = state_ref[:, high:] - dot6(gain, below, NT)
+            minus_ref[:, high:] = minus_ref[:, high:] - dot6(minus, below, NT)
         minus_ref[:, low:high] = minus
     low = n - NOBS
     left = (gain_ref[SAMPLE_TOTAL : SAMPLE_TOTAL + 1, low:] - minus_ref[:, low:]) * (1.0 / (SAMPLE_TOTAL - 1))
@@ -261,7 +259,8 @@
     for r in range(0, 8, 2):
         at = [pl.ds(r + i, SAMPLE_TOTAL, stride=8) for i in range(2)]
         field = jnp.concatenate([cells_ref[a, :] for a in at], axis=1)
-        new = field + dot_split(transform, halves(field), NN)
+        mean = jnp.sum(field, axis=0, keepdims=True) / SAMPLE_TOTAL
+        new = field + dot_split(transform, halves(field - mean), NN)
         for i in range(2):
             out_ref[at[i], :] = new[:, 128 * i : 128 * i + 128]
 

time: 115 us -> 116 us (level)
  Pallas kernels: 37.7 us -> 39 us
  transfers between devices with their start and end apart: 13 -> 13, of which waited for: 9 -> 8; matrix products, arithmetic and copies ran while one was open for 0% -> 0% of each run, Pallas kernels for 29% -> 30%
where the time goes in v6:
time: 116 us
  Pallas kernels  39 us (34%)
  blocking collectives  30.8 us (27%)
  starting transfers between devices  28.8 us (25%)
  waiting for transfers between devices  11.9 us (10%)
  local copies, waits for them, and re-layouts  4.95 us (4%)
    all_to_all x1, blocking collectives, body(): new = lax.all_to_all(new.reshape(mem_count, members, 8, 128), 'mem', 0, 0)  30.8 us
    pallas_call x1, Pallas kernels, body(): call(transform_kernel, shape(square, f32), [pltpu.VMEM(square, f32), pltp...  25.1 us
    ppermute x6, starting transfers between devices, ring(): lax.ppermute(value, ('mem', 'cell'), [(m * cell_count + i, target(m, i))...  9.75 us
    pallas_call x1, Pallas kernels, body(): call(forecast_kernel, (shape((mem_count, members, 8, 128), f32), seen_sha...  6.55 us
    ppermute x6, waiting for transfers between devices, ring(): lax.ppermute(value, ('mem', 'cell'), [(m * cell_count + i, target(m, i))...  6.27 us
    ppermute x1, starting transfers between devices, body(): other = lax.ppermute(seen, 'mem', swap)  5.85 us
    ppermute x3, waiting for transfers between devices, along_x(): lax.ppermute(value, 'mem', [(i, (i + 2 * d) % mem_count) for i in range(m...  5.6 us
    ppermute x1, starting transfers between devices, body(): low = lax.ppermute(prior_samples[:, rows - 1, :], 'cell', forward)  4.38 us
  transfers between devices with their start and end apart: 13, of which 8 were waited for; matrix products, arithmetic and copies ran while one was open for 0% of the time, Pallas kernels for 30%

profile of v6, /device:TPU:1, one launch (start us, length us, event | category | flops | bytes accessed | tf_op | source)
XLA Modules:
  0.0 115.8 jit_solution(10035028922560029762)
XLA Ops:
  0.0 1.8 %fusion = (f32[64,1,512]{2,1,0:T(1,128)S(1)}, f32[64,1,512]{2,1,0:T(1,128)S(1)}) fusion(f32[64,16,512]{2,1,0:T(8,128)} %x_ref.1), kind=kLoop, calls=%fused_computation.2 | loop fusion | bytes 524288 | tf_op jit(solution)/shard_map/slice | solution.py:333
  1.8 4.4 %collective-permute-start = (f32[64,512]{1,0:T(8,128)S(1)}, f32[64,512]{1,0:T(8,128)S(1)}, u32[]{:S(2)}, u32[]{:S(2)}) collective-permute-start(f32[64,512]{1,0:T(8,128)S(1)} %bitcast.14), channel_id=1, source_target_pairs={{0,1},{1,2},{2,3},{3,4},{4,5},{5,6},{6,7},{7,8},{8,9},{9,10},{10,1... | collective-permute-start | bytes 393224 | tf_op jit(solution)/shard_map/ppermute | solution.py:332
  6.2 1.3 %collective-permute-start.1 = (f32[64,512]{1,0:T(8,128)S(1)}, f32[64,512]{1,0:T(8,128)S(1)}, u32[]{:S(2)}, u32[]{:S(2)}) collective-permute-start(f32[64,512]{1,0:T(8,128)S(1)} %bitcast.15), channel_id=1, source_target_pairs={{1,0},{2,1},{3,2},{4,3},{5,4},{6,5},{7,6},{8,7},{9,8},{10,9},{11,1... | collective-permute-start | bytes 393224 | tf_op jit(solution)/shard_map/ppermute | solution.py:333
  7.6 6.5 %shard_map.64 = (f32[8,64,8,128]{3,2,1,0:T(8,128)}, f32[64,512]{1,0:T(8,128)}) custom-call(s32[4]{0:T(128)} %block_ref.1, s32[1]{0:T(128)} %bitcast.1.base_ref, f32[64,16,512]{2,1,0:T(8,128)} %x_ref.1, f32[4,16,512]{2,1,0:T(8,128)} %weight_ref.5, s32[4,128]{1,0:T(4,128)} %cell_ref.3), custom_call_target="tpu_custom_call" | custom-call | flops 2000000000 | bytes 4000000 | tf_op jit(solution)/shard_map/pallas_call | solution.py:336
  14.2 0.9 copy-done.1
  15.1 1.0 shard_map.65.refs_0_
  16.1 5.6 %collective-permute-start.4 = (f32[64,512]{1,0:T(8,128)S(1)}, f32[64,512]{1,0:T(8,128)S(1)}, u32[]{:S(2)}, u32[]{:S(2)}) collective-permute-start(f32[64,512]{1,0:T(8,128)S(1)} %shard_map.65.refs_0_), channel_id=1, source_target_pairs={{0,2},{1,3},{2,0},{3,1},{4,6},{5,7},{6,4},{7,5},{8,10},{9,11},{10,... | collective-permute-start | bytes 393224 | tf_op jit(solution)/shard_map/ppermute | solution.py:330
  23.2 2.7 %shard_map.66 = f32[4096,128]{1,0:T(8,128)} custom-call(f32[4096,128]{1,0:T(8,128)} %bitcast.4.piece_ref, f32[4,16,512]{2,1,0:T(8,128)S(1)} %copy-done, f32[64,512]{1,0:T(8,128)S(1)} %collective-permute-done.low_ref, f32[64,512]{1,0:T(8,128)S(1)} %collective-permute-done.1.high_ref), custom_call_target="tpu_custom_call", output_to_operand_aliasing={{}: (0, {})} | custom-call | tf_op jit(solution)/shard_map/pallas_call | solution.py:374
  26.4 1.4 %collective-permute-done.2.refs_1_ = f32[64,512]{1,0:T(8,128)S(1)} collective-permute-done((f32[64,512]{1,0:T(8,128)S(1)}, f32[64,512]{1,0:T(8,128)S(1)}, u32[]{:S(2)}, u32[]{:S(2)}) %collective-permute-start.2) | collective-permute-done | bytes 131104 | tf_op jit(solution)/shard_map/ppermute | solution.py:330
  27.8 1.2 %collective-permute-start.7 = (f32[64,512]{1,0:T(8,128)S(1)}, f32[64,512]{1,0:T(8,128)S(1)}, u32[]{:S(2)}, u32[]{:S(2)}) collective-permute-start(f32[64,512]{1,0:T(8,128)S(1)} %shard_map.67.refs_0_), channel_id=1, source_target_pairs={{0,8},{1,9},{2,10},{3,11},{4,12},{5,13},{6,14},{7,15},{8,0},{9,1},... | collective-permute-start | bytes 393224 | tf_op jit(solution)/shard_map/ppermute | solution.py:330
  30.5 3.0 %collective-permute-done.7.refs_3_ = f32[64,512]{1,0:T(8,128)S(1)} collective-permute-done((f32[64,512]{1,0:T(8,128)S(1)}, f32[64,512]{1,0:T(8,128)S(1)}, u32[]{:S(2)}, u32[]{:S(2)}) %collective-permute-start.7) | collective-permute-done | bytes 131104 | tf_op jit(solution)/shard_map/ppermute | solution.py:330
  33.8 1.0 collective-permute-done.5.refs_1_
  34.8 2.5 %collective-permute-start.10 = (f32[64,512]{1,0:T(8,128)S(1)}, f32[64,512]{1,0:T(8,128)S(1)}, u32[]{:S(2)}, u32[]{:S(2)}) collective-permute-start(f32[64,512]{1,0:T(8,128)S(1)} %shard_map.68.refs_0_), channel_id=1, source_target_pairs={{0,96},{16,112},{32,0},{48,16},{64,32},{80,48},{96,64},{112,80},{1... | collective-permute-start | bytes 393224 | tf_op jit(solution)/shard_map/ppermute | solution.py:318
  38.5 2.2 %collective-permute-done.10.refs_3_ = f32[64,512]{1,0:T(8,128)S(1)} collective-permute-done((f32[64,512]{1,0:T(8,128)S(1)}, f32[64,512]{1,0:T(8,128)S(1)}, u32[]{:S(2)}, u32[]{:S(2)}) %collective-permute-start.10) | collective-permute-done | bytes 131104 | tf_op jit(solution)/shard_map/ppermute | solution.py:318
  40.7 2.1 %collective-permute-done.9.refs_2_ = f32[64,512]{1,0:T(8,128)S(1)} collective-permute-done((f32[64,512]{1,0:T(8,128)S(1)}, f32[64,512]{1,0:T(8,128)S(1)}, u32[]{:S(2)}, u32[]{:S(2)}) %collective-permute-start.9) | collective-permute-done | bytes 131104 | tf_op jit(solution)/shard_map/ppermute | solution.py:318
  42.8 1.3 %collective-permute-done.8.refs_1_ = f32[64,512]{1,0:T(8,128)S(1)} collective-permute-done((f32[64,512]{1,0:T(8,128)S(1)}, f32[64,512]{1,0:T(8,128)S(1)}, u32[]{:S(2)}, u32[]{:S(2)}) %collective-permute-start.8) | collective-permute-done | bytes 131104 | tf_op jit(solution)/shard_map/ppermute | solution.py:318
  44.1 5.9 %collective-permute-start.11 = (f32[4,64,512]{2,1,0:T(8,128)S(1)}, f32[4,64,512]{2,1,0:T(8,128)S(1)}, u32[]{:S(2)}, u32[]{:S(2)}) collective-permute-start(f32[4,64,512]{2,1,0:T(8,128)S(1)} %shard_map.69.seen_ref), channel_id=1, source_target_pairs={{0,16},{16,0},{32,48},{48,32},{64,80},{80,64},{96,112},{112,96},{1... | collective-permute-start | bytes 1572872 | tf_op jit(solution)/shard_map/ppermute | solution.py:394
  50.0 3.9 %all-to-all-start = ((f32[8,64,8,128]{3,2,1,0:T(8,128)}), f32[8,64,8,128]{3,2,1,0:T(8,128)S(1)}, u32[]{:S(2)}, u32[]{:S(2)}) async-start(f32[8,64,8,128]{3,2,1,0:T(8,128)} %bitcast.5), calls=%async_computation | async-start | bytes 4194304 | tf_op jit(solution)/shard_map/all_to_all | solution.py:392
  53.9 25.1 %shard_map.70.transform_ref = f32[512,512]{1,0:T(8,128)S(1)} custom-call(s32[4]{0:T(128)S(1)} %copy-done.3, s32[1]{0:T(128)} %bitcast.me_ref, f32[4,64,512]{2,1,0:T(8,128)S(1)} %shard_map.69.seen_ref, f32[4,64,512]{2,1,0:T(8,128)S(1)} %collective-permute-done.11.other_ref, f32[4,128]{1,0:T(4,128)S(1)} %copy-done.4, f32[4,128]{1,0:T(4,128)S(1)} %copy-done.5), custom_call_target="tpu_custom_call" | custom-call | flops 20000000000 | bytes 2000000 | tf_op jit(solution)/shard_map/pallas_call | solution.py:397
  79.0 1.0 copy-done.6
  79.9 1.2 %copy-done.7 = f32[512,512]{1,0:T(8,128)S(1)} copy-done((f32[512,512]{1,0:T(8,128)S(1)}, f32[512,512]{1,0:T(8,128)}, u32[]{:S(2)}) %copy-start.7) | copy-done | bytes 1048600
  81.2 2.3 %shard_map.71 = f32[4096,128]{1,0:T(8,128)S(1)} custom-call(f32[512,512]{1,0:T(8,128)S(1)} %copy-done.7, f32[4096,128]{1,0:T(8,128)S(1)} %bitcast.12), custom_call_target="tpu_custom_call" | custom-call | flops 3000000000 | bytes 4000000 | tf_op jit(solution)/shard_map/pallas_call | solution.py:421
  83.4 30.8 %all_to_all.10.parts_ref = f32[8,64,8,128]{3,2,1,0:T(8,128)S(1)} all-to-all(f32[8,64,8,128]{3,2,1,0:T(8,128)S(1)} %bitcast.13), channel_id=1, replica_groups=mesh['mem'=8,'cell'=16] {'mem'}, dimensions={0} | all-to-all | bytes 4194304 | tf_op jit(solution)/shard_map/all_to_all | solution.py:424
  114.2 1.4 %shard_map.72 = f32[64,16,512]{2,1,0:T(8,128)} custom-call(f32[8,64,8,128]{3,2,1,0:T(8,128)S(1)} %all_to_all.10.parts_ref), custom_call_target="tpu_custom_call" | custom-call | bytes 4000000 | tf_op jit(solution)/shard_map/pallas_call | solution.py:426
  (31 shorter events, 5.1 us)
Async XLA Ops:
  1.8 12.3 %collective-permute-start = (f32[64,512]{1,0:T(8,128)S(1)}, f32[64,512]{1,0:T(8,128)S(1)}, u32[]{:S(2)}, u32[]{:S(2)}) collective-permute-start(f32[64,512]{1,0:T(8,128)S(1)} %bitcast.14), channel_id=1, source_target_pairs={{0,1},{1,2},{2,3},{3,4},{4,5},{5,6},{6,7},{7,8},{8,9},{9,10},{10,1... | collective-permute-start | bytes 393224 | tf_op jit(solution)/shard_map/ppermute | solution.py:332
  6.2 7.9 %collective-permute-start.1 = (f32[64,512]{1,0:T(8,128)S(1)}, f32[64,512]{1,0:T(8,128)S(1)}, u32[]{:S(2)}, u32[]{:S(2)}) collective-permute-start(f32[64,512]{1,0:T(8,128)S(1)} %bitcast.15), channel_id=1, source_target_pairs={{1,0},{2,1},{3,2},{4,3},{5,4},{6,5},{7,6},{8,7},{9,8},{10,9},{11,1... | collective-permute-start | bytes 393224 | tf_op jit(solution)/shard_map/ppermute | solution.py:333
  7.5 6.6 %copy-start = (f32[4,16,512]{2,1,0:T(8,128)S(1)}, f32[4,16,512]{2,1,0:T(8,128)}, u32[]{:S(2)}) copy-start(f32[4,16,512]{2,1,0:T(8,128)} %weight_ref.5) | copy-start | bytes 393220
  7.5 6.6 %copy-start.2 = (s32[4,128]{1,0:T(4,128)S(1)}, s32[4,128]{1,0:T(4,128)}, u32[]{:S(2)}) copy-start(s32[4,128]{1,0:T(4,128)} %cell_ref.3) | copy-start | bytes 6148
  7.5 6.6 %copy-start.3 = (s32[4]{0:T(128)S(1)}, s32[4]{0:T(128)}, u32[]{:S(2)}) copy-start(s32[4]{0:T(128)} %block_ref.1) | copy-start | bytes 52
  14.1 0.9 copy-start.1
  16.1 9.8 %collective-permute-start.4 = (f32[64,512]{1,0:T(8,128)S(1)}, f32[64,512]{1,0:T(8,128)S(1)}, u32[]{:S(2)}, u32[]{:S(2)}) collective-permute-start(f32[64,512]{1,0:T(8,128)S(1)} %shard_map.65.refs_0_), channel_id=1, source_target_pairs={{0,2},{1,3},{2,0},{3,1},{4,6},{5,7},{6,4},{7,5},{8,10},{9,11},{10,... | collective-permute-start | bytes 393224 | tf_op jit(solution)/shard_map/ppermute | solution.py:330
  21.7 4.7 %collective-permute-start.3 = (f32[64,512]{1,0:T(8,128)S(1)}, f32[64,512]{1,0:T(8,128)S(1)}, u32[]{:S(2)}, u32[]{:S(2)}) collective-permute-start(f32[64,512]{1,0:T(8,128)S(1)} %shard_map.65.refs_0_), channel_id=1, source_target_pairs={{0,3},{1,0},{2,1},{3,2},{4,7},{5,4},{6,5},{7,6},{8,11},{9,8},{10,9... | collective-permute-start | bytes 393224 | tf_op jit(solution)/shard_map/ppermute | solution.py:330
  22.5 5.3 %collective-permute-start.2 = (f32[64,512]{1,0:T(8,128)S(1)}, f32[64,512]{1,0:T(8,128)S(1)}, u32[]{:S(2)}, u32[]{:S(2)}) collective-permute-start(f32[64,512]{1,0:T(8,128)S(1)} %shard_map.65.refs_0_), channel_id=1, source_target_pairs={{0,1},{1,2},{2,3},{3,0},{4,5},{5,6},{6,7},{7,4},{8,9},{9,10},{10,1... | collective-permute-start | bytes 393224 | tf_op jit(solution)/shard_map/ppermute | solution.py:330
  27.8 5.7 %collective-permute-start.7 = (f32[64,512]{1,0:T(8,128)S(1)}, f32[64,512]{1,0:T(8,128)S(1)}, u32[]{:S(2)}, u32[]{:S(2)}) collective-permute-start(f32[64,512]{1,0:T(8,128)S(1)} %shard_map.67.refs_0_), channel_id=1, source_target_pairs={{0,8},{1,9},{2,10},{3,11},{4,12},{5,13},{6,14},{7,15},{8,0},{9,1},... | collective-permute-start | bytes 393224 | tf_op jit(solution)/shard_map/ppermute | solution.py:330
  29.0 4.8 %collective-permute-start.6 = (f32[64,512]{1,0:T(8,128)S(1)}, f32[64,512]{1,0:T(8,128)S(1)}, u32[]{:S(2)}, u32[]{:S(2)}) collective-permute-start(f32[64,512]{1,0:T(8,128)S(1)} %shard_map.67.refs_0_), channel_id=1, source_target_pairs={{0,12},{1,13},{2,14},{3,15},{4,0},{5,1},{6,2},{7,3},{8,4},{9,5},{1... | collective-permute-start | bytes 393224 | tf_op jit(solution)/shard_map/ppermute | solution.py:330
  29.6 5.2 %collective-permute-start.5 = (f32[64,512]{1,0:T(8,128)S(1)}, f32[64,512]{1,0:T(8,128)S(1)}, u32[]{:S(2)}, u32[]{:S(2)}) collective-permute-start(f32[64,512]{1,0:T(8,128)S(1)} %shard_map.67.refs_0_), channel_id=1, source_target_pairs={{0,4},{1,5},{2,6},{3,7},{4,8},{5,9},{6,10},{7,11},{8,12},{9,13},{1... | collective-permute-start | bytes 393224 | tf_op jit(solution)/shard_map/ppermute | solution.py:330
  34.8 5.9 %collective-permute-start.10 = (f32[64,512]{1,0:T(8,128)S(1)}, f32[64,512]{1,0:T(8,128)S(1)}, u32[]{:S(2)}, u32[]{:S(2)}) collective-permute-start(f32[64,512]{1,0:T(8,128)S(1)} %shard_map.68.refs_0_), channel_id=1, source_target_pairs={{0,96},{16,112},{32,0},{48,16},{64,32},{80,48},{96,64},{112,80},{1... | collective-permute-start | bytes 393224 | tf_op jit(solution)/shard_map/ppermute | solution.py:318
  37.4 5.4 %collective-permute-start.9 = (f32[64,512]{1,0:T(8,128)S(1)}, f32[64,512]{1,0:T(8,128)S(1)}, u32[]{:S(2)}, u32[]{:S(2)}) collective-permute-start(f32[64,512]{1,0:T(8,128)S(1)} %shard_map.68.refs_0_), channel_id=1, source_target_pairs={{0,64},{16,80},{32,96},{48,112},{64,0},{80,16},{96,32},{112,48},{1... | collective-permute-start | bytes 393224 | tf_op jit(solution)/shard_map/ppermute | solution.py:318
  37.9 6.2 %collective-permute-start.8 = (f32[64,512]{1,0:T(8,128)S(1)}, f32[64,512]{1,0:T(8,128)S(1)}, u32[]{:S(2)}, u32[]{:S(2)}) collective-permute-start(f32[64,512]{1,0:T(8,128)S(1)} %shard_map.68.refs_0_), channel_id=1, source_target_pairs={{0,32},{16,48},{32,64},{48,80},{64,96},{80,112},{96,0},{112,16},{1... | collective-permute-start | bytes 393224 | tf_op jit(solution)/shard_map/ppermute | solution.py:318
  44.1 9.7 %collective-permute-start.11 = (f32[4,64,512]{2,1,0:T(8,128)S(1)}, f32[4,64,512]{2,1,0:T(8,128)S(1)}, u32[]{:S(2)}, u32[]{:S(2)}) collective-permute-start(f32[4,64,512]{2,1,0:T(8,128)S(1)} %shard_map.69.seen_ref), channel_id=1, source_target_pairs={{0,16},{16,0},{32,48},{48,32},{64,80},{80,64},{96,112},{112,96},{1... | collective-permute-start | bytes 1572872 | tf_op jit(solution)/shard_map/ppermute | solution.py:394
  50.0 3.9 %copy-start.4 = (f32[4,128]{1,0:T(4,128)S(1)}, f32[4,128]{1,0:T(4,128)}, u32[]{:S(2)}) copy-start(f32[4,128]{1,0:T(4,128)} %value_ref.1) | copy-start | bytes 6148
  50.0 3.9 %copy-start.5 = (f32[4,128]{1,0:T(4,128)S(1)}, f32[4,128]{1,0:T(4,128)}, u32[]{:S(2)}) copy-start(f32[4,128]{1,0:T(4,128)} %var_ref.1) | copy-start | bytes 6148
  50.0 30.0 %all-to-all-start = ((f32[8,64,8,128]{3,2,1,0:T(8,128)}), f32[8,64,8,128]{3,2,1,0:T(8,128)S(1)}, u32[]{:S(2)}, u32[]{:S(2)}) async-start(f32[8,64,8,128]{3,2,1,0:T(8,128)} %bitcast.5), calls=%async_computation | async-start | bytes 4194304 | tf_op jit(solution)/shard_map/all_to_all | solution.py:392
  78.9 1.0 copy-start.6
  79.9 1.2 %copy-start.7 = (f32[512,512]{1,0:T(8,128)S(1)}, f32[512,512]{1,0:T(8,128)}, u32[]{:S(2)}) copy-start(f32[512,512]{1,0:T(8,128)} %copy-done.6) | copy-start | bytes 3145732

commit v7 on v6

--- a/solution.py
+++ b/solution.py
@@ -77,7 +77,7 @@
                 piece_ref[4 * h + q, m] = f[8 * h : 8 * h + 8, 128 * q : 128 * q + 128]
         return carry
 
-    lax.fori_loop(0, members, member, 0, unroll=8)
+    lax.fori_loop(0, members, member, 0, unroll=32)
     own_row = (lax.broadcasted_iota(jnp.int32, (rows, ALL_OBS), 0) == at_row).astype(jnp.float32)
     pick = pick_ref[...]
     part = 8

time: 116 us -> 115 us (level)
  transfers between devices with their start and end apart: 13 -> 13, of which waited for: 8 -> 8; matrix products, arithmetic and copies ran while one was open for 0% -> 0% of each run, Pallas kernels for 30% -> 29%
where the time goes in v7:
time: 115 us
  Pallas kernels  38 us (33%)
  blocking collectives  30.8 us (27%)
  starting transfers between devices  28.9 us (25%)
  waiting for transfers between devices  11.8 us (10%)
  local copies, waits for them, and re-layouts  4.95 us (4%)
    all_to_all x1, blocking collectives, body(): new = lax.all_to_all(new.reshape(mem_count, members, 8, 128), 'mem', 0, 0)  30.8 us
    pallas_call x1, Pallas kernels, body(): call(transform_kernel, shape(square, f32), [pltpu.VMEM(square, f32), pltp...  25.1 us
    ppermute x6, starting transfers between devices, ring(): lax.ppermute(value, ('mem', 'cell'), [(m * cell_count + i, target(m, i))...  9.81 us
    ppermute x6, waiting for transfers between devices, ring(): lax.ppermute(value, ('mem', 'cell'), [(m * cell_count + i, target(m, i))...  6.21 us
    ppermute x1, starting transfers between devices, body(): other = lax.ppermute(seen, 'mem', swap)  5.89 us
    pallas_call x1, Pallas kernels, body(): call(forecast_kernel, (shape((mem_count, members, 8, 128), f32), seen_sha...  5.62 us
    ppermute x3, waiting for transfers between devices, along_x(): lax.ppermute(value, 'mem', [(i, (i + 2 * d) % mem_count) for i in range(m...  5.6 us
    ppermute x1, starting transfers between devices, body(): low = lax.ppermute(prior_samples[:, rows - 1, :], 'cell', forward)  4.38 us
  transfers between devices with their start and end apart: 13, of which 8 were waited for; matrix products, arithmetic and copies ran while one was open for 0% of the time, Pallas kernels for 29%

profile of v7, /device:TPU:1, one launch (start us, length us, event | category | flops | bytes accessed | tf_op | source)
XLA Modules:
  0.0 114.9 jit_solution(2589011010461435803)
XLA Ops:
  0.0 1.8 %fusion = (f32[64,1,512]{2,1,0:T(1,128)S(1)}, f32[64,1,512]{2,1,0:T(1,128)S(1)}) fusion(f32[64,16,512]{2,1,0:T(8,128)} %x_ref.1), kind=kLoop, calls=%fused_computation.2 | loop fusion | bytes 524288 | tf_op jit(solution)/shard_map/slice | solution.py:333
  1.8 4.4 %collective-permute-start = (f32[64,512]{1,0:T(8,128)S(1)}, f32[64,512]{1,0:T(8,128)S(1)}, u32[]{:S(2)}, u32[]{:S(2)}) collective-permute-start(f32[64,512]{1,0:T(8,128)S(1)} %bitcast.14), channel_id=1, source_target_pairs={{0,1},{1,2},{2,3},{3,4},{4,5},{5,6},{6,7},{7,8},{8,9},{9,10},{10,1... | collective-permute-start | bytes 393224 | tf_op jit(solution)/shard_map/ppermute | solution.py:332
  6.2 1.3 %collective-permute-start.1 = (f32[64,512]{1,0:T(8,128)S(1)}, f32[64,512]{1,0:T(8,128)S(1)}, u32[]{:S(2)}, u32[]{:S(2)}) collective-permute-start(f32[64,512]{1,0:T(8,128)S(1)} %bitcast.15), channel_id=1, source_target_pairs={{1,0},{2,1},{3,2},{4,3},{5,4},{6,5},{7,6},{8,7},{9,8},{10,9},{11,1... | collective-permute-start | bytes 393224 | tf_op jit(solution)/shard_map/ppermute | solution.py:333
  7.6 5.6 %shard_map.64 = (f32[8,64,8,128]{3,2,1,0:T(8,128)}, f32[64,512]{1,0:T(8,128)}) custom-call(s32[4]{0:T(128)} %block_ref.1, s32[1]{0:T(128)} %bitcast.1.base_ref, f32[64,16,512]{2,1,0:T(8,128)} %x_ref.1, f32[4,16,512]{2,1,0:T(8,128)} %weight_ref.5, s32[4,128]{1,0:T(4,128)} %cell_ref.3), custom_call_target="tpu_custom_call" | custom-call | flops 2000000000 | bytes 4000000 | tf_op jit(solution)/shard_map/pallas_call | solution.py:336
  13.2 0.9 copy-done.1
  14.1 1.0 shard_map.65.refs_0_
  15.1 5.7 %collective-permute-start.4 = (f32[64,512]{1,0:T(8,128)S(1)}, f32[64,512]{1,0:T(8,128)S(1)}, u32[]{:S(2)}, u32[]{:S(2)}) collective-permute-start(f32[64,512]{1,0:T(8,128)S(1)} %shard_map.65.refs_0_), channel_id=1, source_target_pairs={{0,2},{1,3},{2,0},{3,1},{4,6},{5,7},{6,4},{7,5},{8,10},{9,11},{10,... | collective-permute-start | bytes 393224 | tf_op jit(solution)/shard_map/ppermute | solution.py:330
  22.3 2.7 %shard_map.66 = f32[4096,128]{1,0:T(8,128)} custom-call(f32[4096,128]{1,0:T(8,128)} %bitcast.4.piece_ref, f32[4,16,512]{2,1,0:T(8,128)S(1)} %copy-done, f32[64,512]{1,0:T(8,128)S(1)} %collective-permute-done.low_ref, f32[64,512]{1,0:T(8,128)S(1)} %collective-permute-done.1.high_ref), custom_call_target="tpu_custom_call", output_to_operand_aliasing={{}: (0, {})} | custom-call | tf_op jit(solution)/shard_map/pallas_call | solution.py:374
  25.5 1.3 %collective-permute-done.2.refs_1_ = f32[64,512]{1,0:T(8,128)S(1)} collective-permute-done((f32[64,512]{1,0:T(8,128)S(1)}, f32[64,512]{1,0:T(8,128)S(1)}, u32[]{:S(2)}, u32[]{:S(2)}) %collective-permute-start.2) | collective-permute-done | bytes 131104 | tf_op jit(solution)/shard_map/ppermute | solution.py:330
  26.9 1.2 %collective-permute-start.7 = (f32[64,512]{1,0:T(8,128)S(1)}, f32[64,512]{1,0:T(8,128)S(1)}, u32[]{:S(2)}, u32[]{:S(2)}) collective-permute-start(f32[64,512]{1,0:T(8,128)S(1)} %shard_map.67.refs_0_), channel_id=1, source_target_pairs={{0,8},{1,9},{2,10},{3,11},{4,12},{5,13},{6,14},{7,15},{8,0},{9,1},... | collective-permute-start | bytes 393224 | tf_op jit(solution)/shard_map/ppermute | solution.py:330
  29.6 3.0 %collective-permute-done.7.refs_3_ = f32[64,512]{1,0:T(8,128)S(1)} collective-permute-done((f32[64,512]{1,0:T(8,128)S(1)}, f32[64,512]{1,0:T(8,128)S(1)}, u32[]{:S(2)}, u32[]{:S(2)}) %collective-permute-start.7) | collective-permute-done | bytes 131104 | tf_op jit(solution)/shard_map/ppermute | solution.py:330
  32.9 1.0 collective-permute-done.5.refs_1_
  33.9 2.5 %collective-permute-start.10 = (f32[64,512]{1,0:T(8,128)S(1)}, f32[64,512]{1,0:T(8,128)S(1)}, u32[]{:S(2)}, u32[]{:S(2)}) collective-permute-start(f32[64,512]{1,0:T(8,128)S(1)} %shard_map.68.refs_0_), channel_id=1, source_target_pairs={{0,96},{16,112},{32,0},{48,16},{64,32},{80,48},{96,64},{112,80},{1... | collective-permute-start | bytes 393224 | tf_op jit(solution)/shard_map/ppermute | solution.py:318
  37.6 2.2 %collective-permute-done.10.refs_3_ = f32[64,512]{1,0:T(8,128)S(1)} collective-permute-done((f32[64,512]{1,0:T(8,128)S(1)}, f32[64,512]{1,0:T(8,128)S(1)}, u32[]{:S(2)}, u32[]{:S(2)}) %collective-permute-start.10) | collective-permute-done | bytes 131104 | tf_op jit(solution)/shard_map/ppermute | solution.py:318
  39.7 2.1 %collective-permute-done.9.refs_2_ = f32[64,512]{1,0:T(8,128)S(1)} collective-permute-done((f32[64,512]{1,0:T(8,128)S(1)}, f32[64,512]{1,0:T(8,128)S(1)}, u32[]{:S(2)}, u32[]{:S(2)}) %collective-permute-start.9) | collective-permute-done | bytes 131104 | tf_op jit(solution)/shard_map/ppermute | solution.py:318
  41.9 1.3 %collective-permute-done.8.refs_1_ = f32[64,512]{1,0:T(8,128)S(1)} collective-permute-done((f32[64,512]{1,0:T(8,128)S(1)}, f32[64,512]{1,0:T(8,128)S(1)}, u32[]{:S(2)}, u32[]{:S(2)}) %collective-permute-start.8) | collective-permute-done | bytes 131104 | tf_op jit(solution)/shard_map/ppermute | solution.py:318
  43.2 5.9 %collective-permute-start.11 = (f32[4,64,512]{2,1,0:T(8,128)S(1)}, f32[4,64,512]{2,1,0:T(8,128)S(1)}, u32[]{:S(2)}, u32[]{:S(2)}) collective-permute-start(f32[4,64,512]{2,1,0:T(8,128)S(1)} %shard_map.69.seen_ref), channel_id=1, source_target_pairs={{0,16},{16,0},{32,48},{48,32},{64,80},{80,64},{96,112},{112,96},{1... | collective-permute-start | bytes 1572872 | tf_op jit(solution)/shard_map/ppermute | solution.py:394
  49.1 3.9 %all-to-all-start = ((f32[8,64,8,128]{3,2,1,0:T(8,128)}), f32[8,64,8,128]{3,2,1,0:T(8,128)S(1)}, u32[]{:S(2)}, u32[]{:S(2)}) async-start(f32[8,64,8,128]{3,2,1,0:T(8,128)} %bitcast.5), calls=%async_computation | async-start | bytes 4194304 | tf_op jit(solution)/shard_map/all_to_all | solution.py:392
  53.0 25.1 %shard_map.70.transform_ref = f32[512,512]{1,0:T(8,128)S(1)} custom-call(s32[4]{0:T(128)S(1)} %copy-done.3, s32[1]{0:T(128)} %bitcast.me_ref, f32[4,64,512]{2,1,0:T(8,128)S(1)} %shard_map.69.seen_ref, f32[4,64,512]{2,1,0:T(8,128)S(1)} %collective-permute-done.11.other_ref, f32[4,128]{1,0:T(4,128)S(1)} %copy-done.4, f32[4,128]{1,0:T(4,128)S(1)} %copy-done.5), custom_call_target="tpu_custom_call" | custom-call | flops 20000000000 | bytes 2000000 | tf_op jit(solution)/shard_map/pallas_call | solution.py:397
  78.1 1.0 copy-done.6
  79.1 1.2 %copy-done.7 = f32[512,512]{1,0:T(8,128)S(1)} copy-done((f32[512,512]{1,0:T(8,128)S(1)}, f32[512,512]{1,0:T(8,128)}, u32[]{:S(2)}) %copy-start.7) | copy-done | bytes 1048600
  80.3 2.3 %shard_map.71 = f32[4096,128]{1,0:T(8,128)S(1)} custom-call(f32[512,512]{1,0:T(8,128)S(1)} %copy-done.7, f32[4096,128]{1,0:T(8,128)S(1)} %bitcast.12), custom_call_target="tpu_custom_call" | custom-call | flops 3000000000 | bytes 4000000 | tf_op jit(solution)/shard_map/pallas_call | solution.py:421
  82.5 30.8 %all_to_all.10.parts_ref = f32[8,64,8,128]{3,2,1,0:T(8,128)S(1)} all-to-all(f32[8,64,8,128]{3,2,1,0:T(8,128)S(1)} %bitcast.13), channel_id=1, replica_groups=mesh['mem'=8,'cell'=16] {'mem'}, dimensions={0} | all-to-all | bytes 4194304 | tf_op jit(solution)/shard_map/all_to_all | solution.py:424
  113.3 1.4 %shard_map.72 = f32[64,16,512]{2,1,0:T(8,128)} custom-call(f32[8,64,8,128]{3,2,1,0:T(8,128)S(1)} %all_to_all.10.parts_ref), custom_call_target="tpu_custom_call" | custom-call | bytes 4000000 | tf_op jit(solution)/shard_map/pallas_call | solution.py:426
  (31 shorter events, 5.1 us)
Async XLA Ops:
  1.8 11.4 %collective-permute-start = (f32[64,512]{1,0:T(8,128)S(1)}, f32[64,512]{1,0:T(8,128)S(1)}, u32[]{:S(2)}, u32[]{:S(2)}) collective-permute-start(f32[64,512]{1,0:T(8,128)S(1)} %bitcast.14), channel_id=1, source_target_pairs={{0,1},{1,2},{2,3},{3,4},{4,5},{5,6},{6,7},{7,8},{8,9},{9,10},{10,1... | collective-permute-start | bytes 393224 | tf_op jit(solution)/shard_map/ppermute | solution.py:332
  6.2 7.0 %collective-permute-start.1 = (f32[64,512]{1,0:T(8,128)S(1)}, f32[64,512]{1,0:T(8,128)S(1)}, u32[]{:S(2)}, u32[]{:S(2)}) collective-permute-start(f32[64,512]{1,0:T(8,128)S(1)} %bitcast.15), channel_id=1, source_target_pairs={{1,0},{2,1},{3,2},{4,3},{5,4},{6,5},{7,6},{8,7},{9,8},{10,9},{11,1... | collective-permute-start | bytes 393224 | tf_op jit(solution)/shard_map/ppermute | solution.py:333
  7.5 5.7 %copy-start = (f32[4,16,512]{2,1,0:T(8,128)S(1)}, f32[4,16,512]{2,1,0:T(8,128)}, u32[]{:S(2)}) copy-start(f32[4,16,512]{2,1,0:T(8,128)} %weight_ref.5) | copy-start | bytes 393220
  7.5 5.7 %copy-start.2 = (s32[4,128]{1,0:T(4,128)S(1)}, s32[4,128]{1,0:T(4,128)}, u32[]{:S(2)}) copy-start(s32[4,128]{1,0:T(4,128)} %cell_ref.3) | copy-start | bytes 6148
  7.5 5.7 %copy-start.3 = (s32[4]{0:T(128)S(1)}, s32[4]{0:T(128)}, u32[]{:S(2)}) copy-start(s32[4]{0:T(128)} %block_ref.1) | copy-start | bytes 52
  13.2 0.9 copy-start.1
  15.1 9.8 %collective-permute-start.4 = (f32[64,512]{1,0:T(8,128)S(1)}, f32[64,512]{1,0:T(8,128)S(1)}, u32[]{:S(2)}, u32[]{:S(2)}) collective-permute-start(f32[64,512]{1,0:T(8,128)S(1)} %shard_map.65.refs_0_), channel_id=1, source_target_pairs={{0,2},{1,3},{2,0},{3,1},{4,6},{5,7},{6,4},{7,5},{8,10},{9,11},{10,... | collective-permute-start | bytes 393224 | tf_op jit(solution)/shard_map/ppermute | solution.py:330
  20.8 4.7 %collective-permute-start.3 = (f32[64,512]{1,0:T(8,128)S(1)}, f32[64,512]{1,0:T(8,128)S(1)}, u32[]{:S(2)}, u32[]{:S(2)}) collective-permute-start(f32[64,512]{1,0:T(8,128)S(1)} %shard_map.65.refs_0_), channel_id=1, source_target_pairs={{0,3},{1,0},{2,1},{3,2},{4,7},{5,4},{6,5},{7,6},{8,11},{9,8},{10,9... | collective-permute-start | bytes 393224 | tf_op jit(solution)/shard_map/ppermute | solution.py:330
  21.5 5.3 %collective-permute-start.2 = (f32[64,512]{1,0:T(8,128)S(1)}, f32[64,512]{1,0:T(8,128)S(1)}, u32[]{:S(2)}, u32[]{:S(2)}) collective-permute-start(f32[64,512]{1,0:T(8,128)S(1)} %shard_map.65.refs_0_), channel_id=1, source_target_pairs={{0,1},{1,2},{2,3},{3,0},{4,5},{5,6},{6,7},{7,4},{8,9},{9,10},{10,1... | collective-permute-start | bytes 393224 | tf_op jit(solution)/shard_map/ppermute | solution.py:330
  26.9 5.7 %collective-permute-start.7 = (f32[64,512]{1,0:T(8,128)S(1)}, f32[64,512]{1,0:T(8,128)S(1)}, u32[]{:S(2)}, u32[]{:S(2)}) collective-permute-start(f32[64,512]{1,0:T(8,128)S(1)} %shard_map.67.refs_0_), channel_id=1, source_target_pairs={{0,8},{1,9},{2,10},{3,11},{4,12},{5,13},{6,14},{7,15},{8,0},{9,1},... | collective-permute-start | bytes 393224 | tf_op jit(solution)/shard_map/ppermute | solution.py:330
  28.1 4.8 %collective-permute-start.6 = (f32[64,512]{1,0:T(8,128)S(1)}, f32[64,512]{1,0:T(8,128)S(1)}, u32[]{:S(2)}, u32[]{:S(2)}) collective-permute-start(f32[64,512]{1,0:T(8,128)S(1)} %shard_map.67.refs_0_), channel_id=1, source_target_pairs={{0,12},{1,13},{2,14},{3,15},{4,0},{5,1},{6,2},{7,3},{8,4},{9,5},{1... | collective-permute-start | bytes 393224 | tf_op jit(solution)/shard_map/ppermute | solution.py:330
  28.7 5.1 %collective-permute-start.5 = (f32[64,512]{1,0:T(8,128)S(1)}, f32[64,512]{1,0:T(8,128)S(1)}, u32[]{:S(2)}, u32[]{:S(2)}) collective-permute-start(f32[64,512]{1,0:T(8,128)S(1)} %shard_map.67.refs_0_), channel_id=1, source_target_pairs={{0,4},{1,5},{2,6},{3,7},{4,8},{5,9},{6,10},{7,11},{8,12},{9,13},{1... | collective-permute-start | bytes 393224 | tf_op jit(solution)/shard_map/ppermute | solution.py:330
  33.9 5.9 %collective-permute-start.10 = (f32[64,512]{1,0:T(8,128)S(1)}, f32[64,512]{1,0:T(8,128)S(1)}, u32[]{:S(2)}, u32[]{:S(2)}) collective-permute-start(f32[64,512]{1,0:T(8,128)S(1)} %shard_map.68.refs_0_), channel_id=1, source_target_pairs={{0,96},{16,112},{32,0},{48,16},{64,32},{80,48},{96,64},{112,80},{1... | collective-permute-start | bytes 393224 | tf_op jit(solution)/shard_map/ppermute | solution.py:318
  36.4 5.4 %collective-permute-start.9 = (f32[64,512]{1,0:T(8,128)S(1)}, f32[64,512]{1,0:T(8,128)S(1)}, u32[]{:S(2)}, u32[]{:S(2)}) collective-permute-start(f32[64,512]{1,0:T(8,128)S(1)} %shard_map.68.refs_0_), channel_id=1, source_target_pairs={{0,64},{16,80},{32,96},{48,112},{64,0},{80,16},{96,32},{112,48},{1... | collective-permute-start | bytes 393224 | tf_op jit(solution)/shard_map/ppermute | solution.py:318
  37.0 6.2 %collective-permute-start.8 = (f32[64,512]{1,0:T(8,128)S(1)}, f32[64,512]{1,0:T(8,128)S(1)}, u32[]{:S(2)}, u32[]{:S(2)}) collective-permute-start(f32[64,512]{1,0:T(8,128)S(1)} %shard_map.68.refs_0_), channel_id=1, source_target_pairs={{0,32},{16,48},{32,64},{48,80},{64,96},{80,112},{96,0},{112,16},{1... | collective-permute-start | bytes 393224 | tf_op jit(solution)/shard_map/ppermute | solution.py:318
  43.2 9.8 %collective-permute-start.11 = (f32[4,64,512]{2,1,0:T(8,128)S(1)}, f32[4,64,512]{2,1,0:T(8,128)S(1)}, u32[]{:S(2)}, u32[]{:S(2)}) collective-permute-start(f32[4,64,512]{2,1,0:T(8,128)S(1)} %shard_map.69.seen_ref), channel_id=1, source_target_pairs={{0,16},{16,0},{32,48},{48,32},{64,80},{80,64},{96,112},{112,96},{1... | collective-permute-start | bytes 1572872 | tf_op jit(solution)/shard_map/ppermute | solution.py:394
  49.1 3.9 %copy-start.4 = (f32[4,128]{1,0:T(4,128)S(1)}, f32[4,128]{1,0:T(4,128)}, u32[]{:S(2)}) copy-start(f32[4,128]{1,0:T(4,128)} %value_ref.1) | copy-start | bytes 6148
  49.1 3.9 %copy-start.5 = (f32[4,128]{1,0:T(4,128)S(1)}, f32[4,128]{1,0:T(4,128)}, u32[]{:S(2)}) copy-start(f32[4,128]{1,0:T(4,128)} %var_ref.1) | copy-start | bytes 6148
  49.1 30.0 %all-to-all-start = ((f32[8,64,8,128]{3,2,1,0:T(8,128)}), f32[8,64,8,128]{3,2,1,0:T(8,128)S(1)}, u32[]{:S(2)}, u32[]{:S(2)}) async-start(f32[8,64,8,128]{3,2,1,0:T(8,128)} %bitcast.5), calls=%async_computation | async-start | bytes 4194304 | tf_op jit(solution)/shard_map/all_to_all | solution.py:392
  78.1 1.0 copy-start.6
  79.1 1.2 %copy-start.7 = (f32[512,512]{1,0:T(8,128)S(1)}, f32[512,512]{1,0:T(8,128)}, u32[]{:S(2)}) copy-start(f32[512,512]{1,0:T(8,128)} %copy-done.6) | copy-start | bytes 3145732

commit v8 on v7

--- a/solution.py
+++ b/solution.py
@@ -255,12 +255,16 @@
 
 
 def update_kernel(transform_ref, cells_ref, out_ref):
-    transform = halves(transform_ref[...])
+    high, low = halves(transform_ref[...])
+    both = jnp.concatenate([high, low], axis=0)
     for r in range(0, 8, 2):
         at = [pl.ds(r + i, SAMPLE_TOTAL, stride=8) for i in range(2)]
         field = jnp.concatenate([cells_ref[a, :] for a in at], axis=1)
         mean = jnp.sum(field, axis=0, keepdims=True) / SAMPLE_TOTAL
-        new = field + dot_split(transform, halves(field - mean), NN)
+        field_high, field_low = halves(field - mean)
+        change = lax.dot_general(both, field_high, NN, preferred_element_type=jnp.float32)
+        small = lax.dot_general(high, field_low, NN, preferred_element_type=jnp.float32)
+        new = field + ((change[SAMPLE_TOTAL:] + small) + change[:SAMPLE_TOTAL])
         for i in range(2):
             out_ref[at[i], :] = new[:, 128 * i : 128 * i + 128]
 

time: 115 us -> 115 us (level)
  no operation moved by 1% of the time
where the time goes in v8:
time: 115 us
  Pallas kernels  37.9 us (33%)
  blocking collectives  30.8 us (27%)
  starting transfers between devices  28.9 us (25%)
  waiting for transfers between devices  11.8 us (10%)
  local copies, waits for them, and re-layouts  4.95 us (4%)
    all_to_all x1, blocking collectives, body(): new = lax.all_to_all(new.reshape(mem_count, members, 8, 128), 'mem', 0, 0)  30.8 us
    pallas_call x1, Pallas kernels, body(): call(transform_kernel, shape(square, f32), [pltpu.VMEM(square, f32), pltp...  25.1 us
    ppermute x6, starting transfers between devices, ring(): lax.ppermute(value, ('mem', 'cell'), [(m * cell_count + i, target(m, i))...  9.81 us
    ppermute x6, waiting for transfers between devices, ring(): lax.ppermute(value, ('mem', 'cell'), [(m * cell_count + i, target(m, i))...  6.21 us
    ppermute x1, starting transfers between devices, body(): other = lax.ppermute(seen, 'mem', swap)  5.89 us
    pallas_call x1, Pallas kernels, body(): call(forecast_kernel, (shape((mem_count, members, 8, 128), f32), seen_sha...  5.62 us
    ppermute x3, waiting for transfers between devices, along_x(): lax.ppermute(value, 'mem', [(i, (i + 2 * d) % mem_count) for i in range(m...  5.6 us
    ppermute x1, starting transfers between devices, body(): low = lax.ppermute(prior_samples[:, rows - 1, :], 'cell', forward)  4.38 us
  transfers between devices with their start and end apart: 13, of which 8 were waited for; matrix products, arithmetic and copies ran while one was open for 0% of the time, Pallas kernels for 29%

profile of v8, /device:TPU:1, one launch (start us, length us, event | category | flops | bytes accessed | tf_op | source)
XLA Modules:
  0.0 114.8 jit_solution(11575779133994147619)
XLA Ops:
  0.0 1.8 %fusion = (f32[64,1,512]{2,1,0:T(1,128)S(1)}, f32[64,1,512]{2,1,0:T(1,128)S(1)}) fusion(f32[64,16,512]{2,1,0:T(8,128)} %x_ref.1), kind=kLoop, calls=%fused_computation.2 | loop fusion | bytes 524288 | tf_op jit(solution)/shard_map/slice | solution.py:337
  1.8 4.4 %collective-permute-start = (f32[64,512]{1,0:T(8,128)S(1)}, f32[64,512]{1,0:T(8,128)S(1)}, u32[]{:S(2)}, u32[]{:S(2)}) collective-permute-start(f32[64,512]{1,0:T(8,128)S(1)} %bitcast.14), channel_id=1, source_target_pairs={{0,1},{1,2},{2,3},{3,4},{4,5},{5,6},{6,7},{7,8},{8,9},{9,10},{10,1... | collective-permute-start | bytes 393224 | tf_op jit(solution)/shard_map/ppermute | solution.py:336
  6.2 1.3 %collective-permute-start.1 = (f32[64,512]{1,0:T(8,128)S(1)}, f32[64,512]{1,0:T(8,128)S(1)}, u32[]{:S(2)}, u32[]{:S(2)}) collective-permute-start(f32[64,512]{1,0:T(8,128)S(1)} %bitcast.15), channel_id=1, source_target_pairs={{1,0},{2,1},{3,2},{4,3},{5,4},{6,5},{7,6},{8,7},{9,8},{10,9},{11,1... | collective-permute-start | bytes 393224 | tf_op jit(solution)/shard_map/ppermute | solution.py:337
  7.6 5.6 %shard_map.64 = (f32[8,64,8,128]{3,2,1,0:T(8,128)}, f32[64,512]{1,0:T(8,128)}) custom-call(s32[4]{0:T(128)} %block_ref.1, s32[1]{0:T(128)} %bitcast.1.base_ref, f32[64,16,512]{2,1,0:T(8,128)} %x_ref.1, f32[4,16,512]{2,1,0:T(8,128)} %weight_ref.5, s32[4,128]{1,0:T(4,128)} %cell_ref.3), custom_call_target="tpu_custom_call" | custom-call | flops 2000000000 | bytes 4000000 | tf_op jit(solution)/shard_map/pallas_call | solution.py:340
  13.2 0.9 copy-done.1
  14.1 1.0 shard_map.65.refs_0_
  15.1 5.7 %collective-permute-start.4 = (f32[64,512]{1,0:T(8,128)S(1)}, f32[64,512]{1,0:T(8,128)S(1)}, u32[]{:S(2)}, u32[]{:S(2)}) collective-permute-start(f32[64,512]{1,0:T(8,128)S(1)} %shard_map.65.refs_0_), channel_id=1, source_target_pairs={{0,2},{1,3},{2,0},{3,1},{4,6},{5,7},{6,4},{7,5},{8,10},{9,11},{10,... | collective-permute-start | bytes 393224 | tf_op jit(solution)/shard_map/ppermute | solution.py:334
  22.3 2.7 %shard_map.66 = f32[4096,128]{1,0:T(8,128)} custom-call(f32[4096,128]{1,0:T(8,128)} %bitcast.4.piece_ref, f32[4,16,512]{2,1,0:T(8,128)S(1)} %copy-done, f32[64,512]{1,0:T(8,128)S(1)} %collective-permute-done.low_ref, f32[64,512]{1,0:T(8,128)S(1)} %collective-permute-done.1.high_ref), custom_call_target="tpu_custom_call", output_to_operand_aliasing={{}: (0, {})} | custom-call | tf_op jit(solution)/shard_map/pallas_call | solution.py:378
  25.5 1.3 %collective-permute-done.2.refs_1_ = f32[64,512]{1,0:T(8,128)S(1)} collective-permute-done((f32[64,512]{1,0:T(8,128)S(1)}, f32[64,512]{1,0:T(8,128)S(1)}, u32[]{:S(2)}, u32[]{:S(2)}) %collective-permute-start.2) | collective-permute-done | bytes 131104 | tf_op jit(solution)/shard_map/ppermute | solution.py:334
  26.9 1.2 %collective-permute-start.7 = (f32[64,512]{1,0:T(8,128)S(1)}, f32[64,512]{1,0:T(8,128)S(1)}, u32[]{:S(2)}, u32[]{:S(2)}) collective-permute-start(f32[64,512]{1,0:T(8,128)S(1)} %shard_map.67.refs_0_), channel_id=1, source_target_pairs={{0,8},{1,9},{2,10},{3,11},{4,12},{5,13},{6,14},{7,15},{8,0},{9,1},... | collective-permute-start | bytes 393224 | tf_op jit(solution)/shard_map/ppermute | solution.py:334
  29.6 3.0 %collective-permute-done.7.refs_3_ = f32[64,512]{1,0:T(8,128)S(1)} collective-permute-done((f32[64,512]{1,0:T(8,128)S(1)}, f32[64,512]{1,0:T(8,128)S(1)}, u32[]{:S(2)}, u32[]{:S(2)}) %collective-permute-start.7) | collective-permute-done | bytes 131104 | tf_op jit(solution)/shard_map/ppermute | solution.py:334
  32.9 1.0 collective-permute-done.5.refs_1_
  33.9 2.5 %collective-permute-start.10 = (f32[64,512]{1,0:T(8,128)S(1)}, f32[64,512]{1,0:T(8,128)S(1)}, u32[]{:S(2)}, u32[]{:S(2)}) collective-permute-start(f32[64,512]{1,0:T(8,128)S(1)} %shard_map.68.refs_0_), channel_id=1, source_target_pairs={{0,96},{16,112},{32,0},{48,16},{64,32},{80,48},{96,64},{112,80},{1... | collective-permute-start | bytes 393224 | tf_op jit(solution)/shard_map/ppermute | solution.py:322
  37.6 2.2 %collective-permute-done.10.refs_3_ = f32[64,512]{1,0:T(8,128)S(1)} collective-permute-done((f32[64,512]{1,0:T(8,128)S(1)}, f32[64,512]{1,0:T(8,128)S(1)}, u32[]{:S(2)}, u32[]{:S(2)}) %collective-permute-start.10) | collective-permute-done | bytes 131104 | tf_op jit(solution)/shard_map/ppermute | solution.py:322
  39.7 2.1 %collective-permute-done.9.refs_2_ = f32[64,512]{1,0:T(8,128)S(1)} collective-permute-done((f32[64,512]{1,0:T(8,128)S(1)}, f32[64,512]{1,0:T(8,128)S(1)}, u32[]{:S(2)}, u32[]{:S(2)}) %collective-permute-start.9) | collective-permute-done | bytes 131104 | tf_op jit(solution)/shard_map/ppermute | solution.py:322
  41.9 1.3 %collective-permute-done.8.refs_1_ = f32[64,512]{1,0:T(8,128)S(1)} collective-permute-done((f32[64,512]{1,0:T(8,128)S(1)}, f32[64,512]{1,0:T(8,128)S(1)}, u32[]{:S(2)}, u32[]{:S(2)}) %collective-permute-start.8) | collective-permute-done | bytes 131104 | tf_op jit(solution)/shard_map/ppermute | solution.py:322
  43.2 5.9 %collective-permute-start.11 = (f32[4,64,512]{2,1,0:T(8,128)S(1)}, f32[4,64,512]{2,1,0:T(8,128)S(1)}, u32[]{:S(2)}, u32[]{:S(2)}) collective-permute-start(f32[4,64,512]{2,1,0:T(8,128)S(1)} %shard_map.69.seen_ref), channel_id=1, source_target_pairs={{0,16},{16,0},{32,48},{48,32},{64,80},{80,64},{96,112},{112,96},{1... | collective-permute-start | bytes 1572872 | tf_op jit(solution)/shard_map/ppermute | solution.py:398
  49.1 3.9 %all-to-all-start = ((f32[8,64,8,128]{3,2,1,0:T(8,128)}), f32[8,64,8,128]{3,2,1,0:T(8,128)S(1)}, u32[]{:S(2)}, u32[]{:S(2)}) async-start(f32[8,64,8,128]{3,2,1,0:T(8,128)} %bitcast.5), calls=%async_computation | async-start | bytes 4194304 | tf_op jit(solution)/shard_map/all_to_all | solution.py:396
  53.0 25.1 %shard_map.70.transform_ref = f32[512,512]{1,0:T(8,128)S(1)} custom-call(s32[4]{0:T(128)S(1)} %copy-done.3, s32[1]{0:T(128)} %bitcast.me_ref, f32[4,64,512]{2,1,0:T(8,128)S(1)} %shard_map.69.seen_ref, f32[4,64,512]{2,1,0:T(8,128)S(1)} %collective-permute-done.11.other_ref, f32[4,128]{1,0:T(4,128)S(1)} %copy-done.4, f32[4,128]{1,0:T(4,128)S(1)} %copy-done.5), custom_call_target="tpu_custom_call" | custom-call | flops 20000000000 | bytes 2000000 | tf_op jit(solution)/shard_map/pallas_call | solution.py:401
  78.1 1.0 copy-done.6
  79.1 1.2 %copy-done.7 = f32[512,512]{1,0:T(8,128)S(1)} copy-done((f32[512,512]{1,0:T(8,128)S(1)}, f32[512,512]{1,0:T(8,128)}, u32[]{:S(2)}) %copy-start.7) | copy-done | bytes 1048600
  80.3 2.2 %shard_map.71 = f32[4096,128]{1,0:T(8,128)S(1)} custom-call(f32[512,512]{1,0:T(8,128)S(1)} %copy-done.7, f32[4096,128]{1,0:T(8,128)S(1)} %bitcast.12), custom_call_target="tpu_custom_call" | custom-call | flops 3000000000 | bytes 4000000 | tf_op jit(solution)/shard_map/pallas_call | solution.py:425
  82.4 30.8 %all_to_all.10.parts_ref = f32[8,64,8,128]{3,2,1,0:T(8,128)S(1)} all-to-all(f32[8,64,8,128]{3,2,1,0:T(8,128)S(1)} %bitcast.13), channel_id=1, replica_groups=mesh['mem'=8,'cell'=16] {'mem'}, dimensions={0} | all-to-all | bytes 4194304 | tf_op jit(solution)/shard_map/all_to_all | solution.py:428
  113.2 1.4 %shard_map.72 = f32[64,16,512]{2,1,0:T(8,128)} custom-call(f32[8,64,8,128]{3,2,1,0:T(8,128)S(1)} %all_to_all.10.parts_ref), custom_call_target="tpu_custom_call" | custom-call | bytes 4000000 | tf_op jit(solution)/shard_map/pallas_call | solution.py:430
  (31 shorter events, 5.1 us)
Async XLA Ops:
  1.8 11.4 %collective-permute-start = (f32[64,512]{1,0:T(8,128)S(1)}, f32[64,512]{1,0:T(8,128)S(1)}, u32[]{:S(2)}, u32[]{:S(2)}) collective-permute-start(f32[64,512]{1,0:T(8,128)S(1)} %bitcast.14), channel_id=1, source_target_pairs={{0,1},{1,2},{2,3},{3,4},{4,5},{5,6},{6,7},{7,8},{8,9},{9,10},{10,1... | collective-permute-start | bytes 393224 | tf_op jit(solution)/shard_map/ppermute | solution.py:336
  6.2 7.0 %collective-permute-start.1 = (f32[64,512]{1,0:T(8,128)S(1)}, f32[64,512]{1,0:T(8,128)S(1)}, u32[]{:S(2)}, u32[]{:S(2)}) collective-permute-start(f32[64,512]{1,0:T(8,128)S(1)} %bitcast.15), channel_id=1, source_target_pairs={{1,0},{2,1},{3,2},{4,3},{5,4},{6,5},{7,6},{8,7},{9,8},{10,9},{11,1... | collective-permute-start | bytes 393224 | tf_op jit(solution)/shard_map/ppermute | solution.py:337
  7.5 5.7 %copy-start = (f32[4,16,512]{2,1,0:T(8,128)S(1)}, f32[4,16,512]{2,1,0:T(8,128)}, u32[]{:S(2)}) copy-start(f32[4,16,512]{2,1,0:T(8,128)} %weight_ref.5) | copy-start | bytes 393220
  7.5 5.7 %copy-start.2 = (s32[4,128]{1,0:T(4,128)S(1)}, s32[4,128]{1,0:T(4,128)}, u32[]{:S(2)}) copy-start(s32[4,128]{1,0:T(4,128)} %cell_ref.3) | copy-start | bytes 6148
  7.5 5.7 %copy-start.3 = (s32[4]{0:T(128)S(1)}, s32[4]{0:T(128)}, u32[]{:S(2)}) copy-start(s32[4]{0:T(128)} %block_ref.1) | copy-start | bytes 52
  13.2 0.9 copy-start.1
  15.1 9.8 %collective-permute-start.4 = (f32[64,512]{1,0:T(8,128)S(1)}, f32[64,512]{1,0:T(8,128)S(1)}, u32[]{:S(2)}, u32[]{:S(2)}) collective-permute-start(f32[64,512]{1,0:T(8,128)S(1)} %shard_map.65.refs_0_), channel_id=1, source_target_pairs={{0,2},{1,3},{2,0},{3,1},{4,6},{5,7},{6,4},{7,5},{8,10},{9,11},{10,... | collective-permute-start | bytes 393224 | tf_op jit(solution)/shard_map/ppermute | solution.py:334
  20.8 4.7 %collective-permute-start.3 = (f32[64,512]{1,0:T(8,128)S(1)}, f32[64,512]{1,0:T(8,128)S(1)}, u32[]{:S(2)}, u32[]{:S(2)}) collective-permute-start(f32[64,512]{1,0:T(8,128)S(1)} %shard_map.65.refs_0_), channel_id=1, source_target_pairs={{0,3},{1,0},{2,1},{3,2},{4,7},{5,4},{6,5},{7,6},{8,11},{9,8},{10,9... | collective-permute-start | bytes 393224 | tf_op jit(solution)/shard_map/ppermute | solution.py:334
  21.5 5.3 %collective-permute-start.2 = (f32[64,512]{1,0:T(8,128)S(1)}, f32[64,512]{1,0:T(8,128)S(1)}, u32[]{:S(2)}, u32[]{:S(2)}) collective-permute-start(f32[64,512]{1,0:T(8,128)S(1)} %shard_map.65.refs_0_), channel_id=1, source_target_pairs={{0,1},{1,2},{2,3},{3,0},{4,5},{5,6},{6,7},{7,4},{8,9},{9,10},{10,1... | collective-permute-start | bytes 393224 | tf_op jit(solution)/shard_map/ppermute | solution.py:334
  26.9 5.7 %collective-permute-start.7 = (f32[64,512]{1,0:T(8,128)S(1)}, f32[64,512]{1,0:T(8,128)S(1)}, u32[]{:S(2)}, u32[]{:S(2)}) collective-permute-start(f32[64,512]{1,0:T(8,128)S(1)} %shard_map.67.refs_0_), channel_id=1, source_target_pairs={{0,8},{1,9},{2,10},{3,11},{4,12},{5,13},{6,14},{7,15},{8,0},{9,1},... | collective-permute-start | bytes 393224 | tf_op jit(solution)/shard_map/ppermute | solution.py:334
  28.1 4.8 %collective-permute-start.6 = (f32[64,512]{1,0:T(8,128)S(1)}, f32[64,512]{1,0:T(8,128)S(1)}, u32[]{:S(2)}, u32[]{:S(2)}) collective-permute-start(f32[64,512]{1,0:T(8,128)S(1)} %shard_map.67.refs_0_), channel_id=1, source_target_pairs={{0,12},{1,13},{2,14},{3,15},{4,0},{5,1},{6,2},{7,3},{8,4},{9,5},{1... | collective-permute-start | bytes 393224 | tf_op jit(solution)/shard_map/ppermute | solution.py:334
  28.7 5.1 %collective-permute-start.5 = (f32[64,512]{1,0:T(8,128)S(1)}, f32[64,512]{1,0:T(8,128)S(1)}, u32[]{:S(2)}, u32[]{:S(2)}) collective-permute-start(f32[64,512]{1,0:T(8,128)S(1)} %shard_map.67.refs_0_), channel_id=1, source_target_pairs={{0,4},{1,5},{2,6},{3,7},{4,8},{5,9},{6,10},{7,11},{8,12},{9,13},{1... | collective-permute-start | bytes 393224 | tf_op jit(solution)/shard_map/ppermute | solution.py:334
  33.9 5.9 %collective-permute-start.10 = (f32[64,512]{1,0:T(8,128)S(1)}, f32[64,512]{1,0:T(8,128)S(1)}, u32[]{:S(2)}, u32[]{:S(2)}) collective-permute-start(f32[64,512]{1,0:T(8,128)S(1)} %shard_map.68.refs_0_), channel_id=1, source_target_pairs={{0,96},{16,112},{32,0},{48,16},{64,32},{80,48},{96,64},{112,80},{1... | collective-permute-start | bytes 393224 | tf_op jit(solution)/shard_map/ppermute | solution.py:322
  36.4 5.4 %collective-permute-start.9 = (f32[64,512]{1,0:T(8,128)S(1)}, f32[64,512]{1,0:T(8,128)S(1)}, u32[]{:S(2)}, u32[]{:S(2)}) collective-permute-start(f32[64,512]{1,0:T(8,128)S(1)} %shard_map.68.refs_0_), channel_id=1, source_target_pairs={{0,64},{16,80},{32,96},{48,112},{64,0},{80,16},{96,32},{112,48},{1... | collective-permute-start | bytes 393224 | tf_op jit(solution)/shard_map/ppermute | solution.py:322
  37.0 6.2 %collective-permute-start.8 = (f32[64,512]{1,0:T(8,128)S(1)}, f32[64,512]{1,0:T(8,128)S(1)}, u32[]{:S(2)}, u32[]{:S(2)}) collective-permute-start(f32[64,512]{1,0:T(8,128)S(1)} %shard_map.68.refs_0_), channel_id=1, source_target_pairs={{0,32},{16,48},{32,64},{48,80},{64,96},{80,112},{96,0},{112,16},{1... | collective-permute-start | bytes 393224 | tf_op jit(solution)/shard_map/ppermute | solution.py:322
  43.2 9.8 %collective-permute-start.11 = (f32[4,64,512]{2,1,0:T(8,128)S(1)}, f32[4,64,512]{2,1,0:T(8,128)S(1)}, u32[]{:S(2)}, u32[]{:S(2)}) collective-permute-start(f32[4,64,512]{2,1,0:T(8,128)S(1)} %shard_map.69.seen_ref), channel_id=1, source_target_pairs={{0,16},{16,0},{32,48},{48,32},{64,80},{80,64},{96,112},{112,96},{1... | collective-permute-start | bytes 1572872 | tf_op jit(solution)/shard_map/ppermute | solution.py:398
  49.1 3.9 %copy-start.4 = (f32[4,128]{1,0:T(4,128)S(1)}, f32[4,128]{1,0:T(4,128)}, u32[]{:S(2)}) copy-start(f32[4,128]{1,0:T(4,128)} %value_ref.1) | copy-start | bytes 6148
  49.1 3.9 %copy-start.5 = (f32[4,128]{1,0:T(4,128)S(1)}, f32[4,128]{1,0:T(4,128)}, u32[]{:S(2)}) copy-start(f32[4,128]{1,0:T(4,128)} %var_ref.1) | copy-start | bytes 6148
  49.1 30.0 %all-to-all-start = ((f32[8,64,8,128]{3,2,1,0:T(8,128)}), f32[8,64,8,128]{3,2,1,0:T(8,128)S(1)}, u32[]{:S(2)}, u32[]{:S(2)}) async-start(f32[8,64,8,128]{3,2,1,0:T(8,128)} %bitcast.5), calls=%async_computation | async-start | bytes 4194304 | tf_op jit(solution)/shard_map/all_to_all | solution.py:396
  78.1 1.0 copy-start.6
  79.1 1.2 %copy-start.7 = (f32[512,512]{1,0:T(8,128)S(1)}, f32[512,512]{1,0:T(8,128)}, u32[]{:S(2)}) copy-start(f32[512,512]{1,0:T(8,128)} %copy-done.6) | copy-start | bytes 3145732
